TPU v7x, 32 devices: a whole 2x2x4 slice. The times are simulated.
32 devices in a mesh: parts: 2 (over x), row: 8 (over z, y), col: 2 (over core).
Axes of the slice: x: 2, y: 2, z: 4, core: 2. Of those that a mesh axis runs over, the one named last changes fastest.
Arguments:
- spectra: bfloat16 [4, 32, 2, 32, 1024], P('parts', None, None, ('row', 'col')), parts along dimension 0, may hold values from -6 to 6
- window_flags: int32 [64, 32], P('parts', ('row', 'col')), parts along dimension 0, may hold values 0 or 1
Outputs:
- cross: float32 [4, 2, 2, 16, 32, 1024], P('parts', None, 'col', None, 'row'), parts along dimension 0
There are 2 independent parts, one for each index of `parts`. A program takes and returns all parts, laid end to end along the dimension named above; each array names one. Nothing has to cross between parts.
All inputs are finite; a program needn't handle non-finite values. No bound on the sum of `window_flags` on one device may be relied on, other than what follows from the above.
Results may differ from a plain program's by a relative error of at most 0.0034.
Values may be sent and summed in bfloat16 or wider, within the bound.
No kernel may reach another device: no remote copies, remote signals or barrier semaphores. Data moves between devices by JAX's collectives and lax.ppermute only.
A program may use at most 256 MiB of HBM per device.

v0:
```python
import jax
import jax.numpy as jnp
from jax import lax
from jax.sharding import PartitionSpec as P

HALFWIN = 64


epsilon = 1e-06


def window_mean(magnitude):
    bins = magnitude.shape[-1]
    lead = [(0, 0)] * (magnitude.ndim - 1)
    padded = jnp.pad(magnitude, lead + [(HALFWIN + 1, HALFWIN)])
    running = jnp.cumsum(padded, axis=-1)
    total = running[..., 2 * HALFWIN + 1 :] - running[..., :bins]
    positions = jnp.arange(bins, dtype=jnp.int32)
    counted = (
        jnp.minimum(positions + HALFWIN, bins - 1) - jnp.maximum(positions - HALFWIN, 0) + 1
    ).astype(jnp.float32)
    return total / counted


def whiten(values):
    magnitude = jnp.sqrt(values[:, :, 0] * values[:, :, 0] + values[:, :, 1] * values[:, :, 1])
    smooth = window_mean(magnitude)
    return (values / (smooth[:, :, None] + epsilon)).astype(jnp.bfloat16)


def combine_parts(prods, keep):
    real_part = prods[..., 0, 0, :, :, :] + prods[..., 1, 1, :, :, :]
    imag_part = prods[..., 1, 0, :, :, :] - prods[..., 0, 1, :, :, :]
    return jnp.stack([real_part * keep, imag_part * keep], axis=-4)


def on_device(spectra, window_flags):
    per_device = spectra.shape[3]
    flag_values = window_flags.astype(jnp.float32)[None, :, None, :, None]
    payload = whiten(spectra.astype(jnp.float32) * flag_values)
    row_index = lax.axis_index("row")
    col_index = lax.axis_index("col")
    col_count = lax.axis_size("col")
    row_count = lax.axis_size("row")
    half_size = row_count * per_device
    cols_here = col_count * per_device
    slot = jnp.arange(half_size, dtype=jnp.int32)
    first = (slot // per_device * col_count + col_index) * per_device + slot % per_device
    second = row_index * cols_here + jnp.arange(cols_here, dtype=jnp.int32)
    keep = (first[:, None] <= second[None, :]).astype(jnp.float32)[:, :, None]
    pieces = []
    for band_index in range(spectra.shape[0]):
        first_rows = lax.all_gather(payload[band_index : band_index + 1], "row", axis=3, tiled=True)
        second_rows = lax.all_gather(
            payload[band_index : band_index + 1], "col", axis=3, tiled=True
        )
        prods = jnp.einsum(
            "wpif,wqjf->pqijf", first_rows[0], second_rows[0], preferred_element_type=jnp.float32
        )
        pieces.append(combine_parts(prods, keep))
    result = jnp.stack(pieces, axis=0)
    return result[:, :, None]


def solution(mesh):
    in_specs = (P("parts", None, None, ("row", "col"), None), P("parts", ("row", "col")))
    out_specs = P("parts", None, "col", None, "row", None)
    return jax.shard_map(
        on_device, mesh=mesh, in_specs=in_specs, out_specs=out_specs, check_vma=False
    )
```

profile of v0, /device:TPU:0, one launch (start us, length us, event | category | flops | bytes accessed | tf_op | source)
XLA Modules:
  0.0 214.4 jit_solution(13793272223604262475)
XLA Ops:
  6.5 0.0 all-gather.5.cloned.1.call-start
  6.5 0.7 convert_element_type.26
  7.2 1.3 convert_multiply_fusion
  8.5 0.2 fusion.23
  8.7 0.2 pad.15
  8.9 0.1 reshape.174
  9.0 0.1 copy.41
  9.2 36.3 %reduce-window.6 = f32[2,32,2,10,128]{4,3,2,1,0:T(8,128)S(1)} reduce-window(f32[2,32,2,10,128]{4,3,2,1,0:T(8,128)S(1)} %copy.41, f32[]{:T(128)} %constant.44.clone.1), window={size=1x1x1x1x128 pad=0_0x0_0x0_0x0_0x127_0}, to_apply=%region_0.1 | reduce-window | flops 20807680 | bytes 1310724 | tf_op jit(solution)/shard_map/reduce-window
  45.4 0.3 slice.73
  45.8 0.5 copy.42
  46.3 0.1 copy.43
  46.4 0.3 broadcast_add_fusion
  46.7 0.0 copy-start.1
  46.7 0.4 reshape.175
  47.1 0.6 fusion.37
  47.7 0.1 copy-done.1
  47.8 0.6 divide_convert_fusion
  48.3 0.8 fusion.38
  49.2 0.0 copy-start
  49.2 0.0 all-gather.5.cloned.1.call-update
  49.2 0.0 all-gather.3.cloned.1.call-start
  49.2 0.7 all-gather.3.cloned.1.call-update
  49.9 2.5 %all_gather.14 = bf16[1,32,2,4,1024]{4,1,2,0,3:T(8,128)(2,1)S(1)} all-gather(bf16[1,32,2,2,1024]{4,1,2,0,3:T(8,128)(2,1)} %get-tuple-element.12), channel_id=1, replica_groups=mesh['parts'=2,'row'=8,'col'=2] {'col'}, dimensions={3}, use_global_device_ids=true | all-gather | bytes 786432 | tf_op jit(solution)/shard_map/all_gather | solution.py:54
  52.4 2.6 %copy.52 = bf16[1,32,2,4,1024]{1,3,2,4,0:T(4,128)(2,1)} copy(bf16[1,32,2,4,1024]{4,1,2,0,3:T(8,128)(2,1)S(1)} %all_gather.14) | data formatting | bytes 1048576 | tf_op jit(solution)/shard_map/all_gather | solution.py:54
  55.0 0.0 copy-done
  55.0 2.4 %all_gather.12 = bf16[1,32,2,4,1024]{4,1,2,0,3:T(8,128)(2,1)S(1)} all-gather(bf16[1,32,2,2,1024]{4,1,2,0,3:T(8,128)(2,1)S(1)} %copy-done), channel_id=1, replica_groups=mesh['parts'=2,'row'=8,'col'=2] {'col'}, dimensions={3}, use_global_device_ids=true | all-gather | bytes 786432 | tf_op jit(solution)/shard_map/all_gather | solution.py:54
  57.3 1.4 copy.46
  58.8 0.1 compare_convert_fusion
  58.8 42.5 %all-gather.5.cloned.1.call-done = bf16[1,32,2,16,1024]{4,1,2,0,3:T(8,128)(2,1)} async-done(((bf16[1,32,2,2,1024]{4,1,2,0,3:T(8,128)(2,1)}), bf16[1,32,2,16,1024]{4,1,2,0,3:T(8,128)(2,1)}) %all-gather.5.cloned.1.call-update) | async-done | bytes 2097168 | tf_op jit(solution)/shard_map/all_gather | solution.py:53
  101.3 12.5 %copy.53 = bf16[1,32,2,16,1024]{1,3,2,4,0:T(8,128)(2,1)} copy(bf16[1,32,2,16,1024]{4,1,2,0,3:T(8,128)(2,1)} %all-gather.5.cloned.1.call-done) | data formatting | bytes 4194304 | tf_op jit(solution)/shard_map/all_gather | solution.py:53
  113.8 26.9 %fusion.7 = f32[2,2,16,4,1024]{2,3,4,1,0:T(4,128)} fusion(bf16[1,32,2,16,1024]{1,3,2,4,0:T(8,128)(2,1)} %copy.53, bf16[1,32,2,4,1024]{1,3,2,4,0:T(4,128)(2,1)} %copy.52), kind=kOutput, calls=%fused_computation.5 | convolution fusion | flops 16777216 | bytes 3670016 | tf_op jit(solution)/shard_map/wpif,wqjf->pqijf/dot_general | solution.py:57
  140.7 10.5 %all-gather.3.cloned.1.call-done = bf16[1,32,2,16,1024]{4,1,2,0,3:T(8,128)(2,1)} async-done(((bf16[1,32,2,2,1024]{4,1,2,0,3:T(8,128)(2,1)}), bf16[1,32,2,16,1024]{4,1,2,0,3:T(8,128)(2,1)}) %all-gather.3.cloned.1.call-update) | async-done | bytes 2097168 | tf_op jit(solution)/shard_map/all_gather | solution.py:53
  151.3 12.5 %copy.47 = bf16[1,32,2,16,1024]{1,3,2,4,0:T(8,128)(2,1)} copy(bf16[1,32,2,16,1024]{4,1,2,0,3:T(8,128)(2,1)} %all-gather.3.cloned.1.call-done) | data formatting | bytes 4194304 | tf_op jit(solution)/shard_map/all_gather | solution.py:53
  163.8 26.2 %fusion.4 = f32[2,2,16,4,1024]{2,3,0,1,4:T(4,128)} fusion(bf16[1,32,2,16,1024]{1,3,2,4,0:T(8,128)(2,1)} %copy.47, bf16[1,32,2,4,1024]{1,3,2,4,0:T(4,128)(2,1)S(1)} %copy.46), kind=kOutput, calls=%fused_computation.4 | convolution fusion | flops 16777216 | bytes 3670016 | tf_op jit(solution)/shard_map/wpif,wqjf->pqijf/dot_general | solution.py:57
  190.0 9.5 %fusion.18 = (f32[1,16,4,1024]{1,2,3,0:T(4,128)}, f32[1,16,4,1024]{1,2,3,0:T(4,128)}, f32[1,16,4,1024]{1,2,3,0:T(4,128)S(1)}, f32[1,16,4,1024]{1,2,3,0:T(4,128)}) fusion(f32[2,2,16,4,1024]{2,3,0,1,4:T(4,128)} %fusion.4, f32[16,4]{0,1:T(4,128)S(1)} %compare_convert_fusion, f32[2,2,16,4,1024]{2,3,4,1,0:T(4,128)} %fusion.7), kind=kLoop, calls=%fused_computation.18 | loop fusion | flops 524288 | bytes 3145984 | tf_op jit(solution)/shard_map/mul | solution.py:34
  199.5 1.8 copy.50
  201.3 1.8 copy.51
  203.2 1.8 copy.55
  205.0 0.8 copy.56
  205.8 0.1 maximum_bitcast_fusion.1
  205.9 0.1 maximum_bitcast_fusion
  205.9 1.6 copy.57
  (5 shorter events, 0.0 us)
Async XLA Ops:
  6.5 94.8 %all-gather.5.cloned.1.call-start = ((), (), s32[]{:S(2)}) async-start(), calls=%async_computation.1 | async-start | bytes 2359296 | tf_op jit(solution)/shard_map/all_gather | solution.py:53
  46.7 1.0 copy-start.1
  49.2 5.8 %copy-start = (bf16[1,32,2,2,1024]{4,1,2,0,3:T(8,128)(2,1)S(1)}, bf16[1,32,2,2,1024]{4,1,2,0,3:T(8,128)(2,1)}, u32[]{:S(2)}) copy-start(bf16[1,32,2,2,1024]{4,1,2,0,3:T(8,128)(2,1)} %get-tuple-element.11) | copy-start | bytes 786436
  49.2 102.1 %all-gather.3.cloned.1.call-start = ((), (), s32[]{:S(2)}) async-start(), calls=%async_computation | async-start | bytes 2359296 | tf_op jit(solution)/shard_map/all_gather | solution.py:53
Sparse Core Ops, SparseCore 0:
  49.3 51.9 all-gather.4
  103.5 47.7 all-gather.2
where the time goes:
time: 215 us; the launch traced here: 214 us
  waiting for transfers between devices  53.7 us (25%)
  matrix products  53.1 us (25%)
  other arithmetic  49 us (23%)
  local copies, waits for them, and re-layouts  40.1 us (19%)
  between operations  13.5 us (6%)
  blocking collectives  4.82 us (2%)
    dot_general x2, matrix products, on_device(): jnp.einsum('wpif,wqjf->pqijf', first_rows[0], second_rows[0], preferred_e...  53.1 us
    all_gather x2, waiting for transfers between devices, on_device(): lax.all_gather(payload[band_index:band_index + 1], 'row', axis=3, tiled=T...  53 us
    another operation x3, other arithmetic  36.6 us
    all_gather x2, local copies, waits for them, and re-layouts, on_device(): lax.all_gather(payload[band_index:band_index + 1], 'row', axis=3, tiled=T...  25 us
    mul x1, other arithmetic, combine_parts(): return jnp.stack([real_part * keep, imag_part * keep], axis=-4)  9.47 us
    mul x4, local copies, waits for them, and re-layouts, combine_parts(): return jnp.stack([real_part * keep, imag_part * keep], axis=-4)  6.3 us
    all_gather x2, blocking collectives, on_device(): lax.all_gather(payload[band_index:band_index + 1], 'col', axis=3, tiled=T...  4.82 us
  transfers between devices with their start and end apart: 2, of which 2 were waited for; matrix products, arithmetic and copies ran while one was open for 20% of the time, Pallas kernels for 0%

commit v1 on v0

v1 whole, which is shorter than its diff:
```python
import functools

import jax
import jax.numpy as jnp
from jax import lax
from jax.experimental import pallas as pl
from jax.experimental.pallas import tpu as pltpu
from jax.sharding import PartitionSpec as P

HALFWIN = 64
LANES = 128
SUB = 8

epsilon = 1e-06


def window_mean(magnitude):
    bins = magnitude.shape[-1]
    lead = [(0, 0)] * (magnitude.ndim - 1)
    padded = jnp.pad(magnitude, lead + [(HALFWIN + 1, HALFWIN)])
    running = jnp.cumsum(padded, axis=-1)
    total = running[..., 2 * HALFWIN + 1 :] - running[..., :bins]
    positions = jnp.arange(bins, dtype=jnp.int32)
    counted = (
        jnp.minimum(positions + HALFWIN, bins - 1) - jnp.maximum(positions - HALFWIN, 0) + 1
    ).astype(jnp.float32)
    return total / counted


def whiten_plain(spectra, window_flags, devices):
    bands, windows, parts, chans, bins = spectra.shape
    flags = window_flags.astype(jnp.float32)[None, :, None, :, None]
    values = spectra.astype(jnp.float32) * flags
    magnitude = jnp.sqrt(values[:, :, 0] * values[:, :, 0] + values[:, :, 1] * values[:, :, 1])
    smooth = window_mean(magnitude)
    white = (values / (smooth[:, :, None] + epsilon)).astype(jnp.bfloat16)
    own = bands * bins // devices
    white = white.reshape(bands, windows, parts, chans, bins // own, own)
    white = white.transpose(0, 4, 3, 2, 1, 5)
    return white.reshape(devices, chans * parts * windows, own)


def cross_plain(got, rows, cols, chans, windows):
    own = got.shape[-1]
    data = got.reshape(rows * cols * chans, 2, windows, own)
    prods = jnp.einsum("apwf,jqwf->pqajf", data, data, preferred_element_type=jnp.float32)
    both = jnp.stack([prods[0, 0] + prods[1, 1], prods[1, 0] - prods[0, 1]])
    both = both.reshape(2, rows, cols, chans, rows, cols * chans, own)
    both = both.transpose(4, 2, 0, 1, 3, 5, 6).astype(jnp.bfloat16)
    return both.reshape(rows * cols, 2 * rows * chans * cols * chans, own)


def finish_plain(got, bands, bins, rows, cols, chans):
    own = got.shape[-1]
    row, col = lax.axis_index("row"), lax.axis_index("col")
    data = got.reshape(bands, bins // own, 2, rows * chans, cols * chans, own)
    data = data.transpose(0, 2, 3, 4, 1, 5).reshape(
        bands, 2, rows * chans, cols * chans, bins
    )
    slot = jnp.arange(rows * chans, dtype=jnp.int32)
    first = (slot // chans * cols + col) * chans + slot % chans
    second = row * cols * chans + jnp.arange(cols * chans, dtype=jnp.int32)
    keep = (first[:, None] <= second[None, :])[:, :, None]
    return jnp.where(keep, data.astype(jnp.float32), 0.0)[:, :, None]


def whiten_kernel(flags_ref, x_ref, out_ref, white_ref, *, chans):
    bands, windows, _, group, _ = x_ref.shape
    chunks = group // chans
    step = 8
    rows = step * group
    row_id = lax.broadcasted_iota(jnp.int32, (rows, LANES), 0) % group
    lane_id = lax.broadcasted_iota(jnp.int32, (rows, LANES), 1)
    spot = row_id // chans * LANES + lane_id
    last = chunks * LANES - 1
    counted = jnp.minimum(spot + HALFWIN, last) - jnp.maximum(spot - HALFWIN, 0) + 1
    inv_count = 1.0 / counted.astype(jnp.float32)
    has_prev = row_id >= chans
    has_next = row_id < group - chans
    k_id = lax.broadcasted_iota(jnp.int32, (group, LANES), 0) % chans
    src = lax.broadcasted_iota(jnp.int32, (LANES, 3 * LANES), 0)
    dst = lax.broadcasted_iota(jnp.int32, (LANES, 3 * LANES), 1) - LANES
    band_mat = jnp.where(jnp.abs(src - dst) <= HALFWIN, 1.0, 0.0).astype(jnp.bfloat16)

    def body(n, carry):
        b = n // (windows // step)
        w0 = n % (windows // step) * step
        x = x_ref[b, pl.ds(w0, step)].astype(jnp.float32)
        keeps = []
        for s in range(step):
            keep = jnp.full((group, LANES), flags_ref[0, w0 + s], jnp.int32)
            for k in range(1, chans):
                keep = jnp.where(k_id == k, flags_ref[k, w0 + s], keep)
            keeps.append(keep)
        keep = jnp.stack(keeps).astype(jnp.float32)
        re = (x[:, 0] * keep).reshape(rows, LANES)
        im = (x[:, 1] * keep).reshape(rows, LANES)
        mag = jnp.sqrt(re * re + im * im)
        high = mag.astype(jnp.bfloat16)
        low = (mag - high.astype(jnp.float32)).astype(jnp.bfloat16)
        sums = jnp.dot(high, band_mat, preferred_element_type=jnp.float32) + jnp.dot(
            low, band_mat, preferred_element_type=jnp.float32
        )
        total = sums[:, LANES : 2 * LANES]
        total += jnp.where(has_prev, pltpu.roll(sums[:, 2 * LANES :], chans, 0), 0.0)
        total += jnp.where(has_next, pltpu.roll(sums[:, :LANES], rows - chans, 0), 0.0)
        inv = 1.0 / (total * inv_count + epsilon)
        for p, part in enumerate((re, im)):
            start = pl.multiple_of(((b * 2 + p) * windows + w0) * group, rows)
            white_ref[pl.ds(start, rows), :] = part * inv
        return carry

    lax.fori_loop(0, bands * windows // step, body, 0)
    for b in range(bands):
        for c in range(chunks):
            for k in range(chans):
                for p in range(2):
                    start = (b * 2 + p) * windows * group + c * chans + k
                    slab = white_ref[pl.ds(start, windows, stride=group), :]
                    at = (k * 2 + p) * windows
                    out_ref[b * chunks + c, at : at + windows, :] = slab.astype(jnp.bfloat16)


def whiten_packed(spectra, window_flags):
    bands, windows, parts, chans, bins = spectra.shape
    chunks = bins // LANES
    view = spectra.reshape(bands, windows, parts, chans, chunks, LANES)
    view = view.transpose(0, 1, 2, 4, 3, 5).reshape(bands, windows, parts, chunks * chans, LANES)
    flags = window_flags.T
    rows = chans * parts * windows
    return pl.pallas_call(
        functools.partial(whiten_kernel, chans=chans),
        out_shape=jax.ShapeDtypeStruct((bands * chunks, rows, LANES), jnp.bfloat16),
        in_specs=[
            pl.BlockSpec(memory_space=pltpu.SMEM),
            pl.BlockSpec(memory_space=pltpu.VMEM),
        ],
        out_specs=pl.BlockSpec(memory_space=pltpu.VMEM),
        scratch_shapes=[
            pltpu.VMEM((bands * parts * windows * chunks * chans, LANES), jnp.float32)
        ],
        compiler_params=pltpu.CompilerParams(vmem_limit_bytes=32 * 2**20),
        name="whiten",
    )(flags, view)


def cross_kernel(x_ref, out_ref, flat_ref, data_ref, *, rows, cols, chans, windows):
    channels = rows * cols * chans
    own_rows = 2 * windows
    per_row = cols * chans
    for s in range(rows * cols):
        flat_ref[s * chans * own_rows : (s + 1) * chans * own_rows, :] = x_ref[s].astype(
            jnp.float32
        )

    def spread(w, carry):
        for jb in range(channels // SUB):
            at = pl.ds(jb * SUB, SUB)
            re = flat_ref[pl.ds(jb * SUB * own_rows + w, SUB, stride=own_rows), :]
            im = flat_ref[pl.ds(jb * SUB * own_rows + windows + w, SUB, stride=own_rows), :]
            data_ref[0, w, at, :] = re
            data_ref[1, w, at, :] = im
            data_ref[2, w, at, :] = re + im
            data_ref[3, w, at, :] = im - re
        return carry

    lax.fori_loop(0, windows, spread, 0)

    low = lax.broadcasted_iota(jnp.int32, (SUB, LANES), 0) < per_row
    for r_first in range(rows):
        blocks = list(range(r_first * per_row // SUB, channels // SUB))
        groups = [blocks[max(0, i - 2) : i] for i in range(len(blocks), 0, -2)]
        for group in groups:

            def body(w, sums, group=group, r_first=r_first):
                out = []
                js = [
                    [data_ref[t, w, pl.ds(jb * SUB, SUB), :] for t in (0, 3, 2)] for jb in group
                ]
                for a in range(per_row):
                    at = pl.ds(r_first * per_row + a, 1)
                    total, imag, real = (data_ref[t, w, at, :] for t in (2, 1, 0))
                    for n in range(len(group)):
                        s1, s2, s3 = sums[a * len(group) + n]
                        out.append(
                            (
                                s1 + js[n][0] * total,
                                s2 + js[n][1] * imag,
                                s3 + js[n][2] * real,
                            )
                        )
                return tuple(out)

            zero = jnp.zeros((SUB, LANES), jnp.float32)
            sums = lax.fori_loop(
                0, windows, body, ((zero, zero, zero),) * (per_row * len(group)), unroll=4
            )
            for n, jb in enumerate(group):
                for h in range(cols):
                    one = sums[(h * chans) * len(group) + n]
                    two = sums[(h * chans + 1) * len(group) + n]
                    for q in range(2):
                        va = one[0] - one[2] if q else one[0] + one[1]
                        vb = two[0] - two[2] if q else two[0] + two[1]
                        even = jnp.where(low, va, pltpu.roll(vb, per_row, 0))
                        odd = jnp.where(low, pltpu.roll(va, per_row, 0), vb)
                        at = (q * rows + r_first) * SUB
                        r = jb * SUB // per_row
                        out_ref[r * cols + h, at : at + SUB, :] = even.astype(jnp.bfloat16)
                        out_ref[(r + 1) * cols + h, at : at + SUB, :] = odd.astype(jnp.bfloat16)


def cross_packed(got, rows, cols, chans, windows):
    devices = rows * cols
    channels = devices * chans
    return pl.pallas_call(
        functools.partial(cross_kernel, rows=rows, cols=cols, chans=chans, windows=windows),
        out_shape=jax.ShapeDtypeStruct((devices, 2 * rows * SUB, LANES), jnp.bfloat16),
        in_specs=[pl.BlockSpec(memory_space=pltpu.VMEM)],
        out_specs=pl.BlockSpec(memory_space=pltpu.VMEM),
        scratch_shapes=[
            pltpu.VMEM((channels * 2 * windows, LANES), jnp.float32),
            pltpu.VMEM((4, windows, channels, LANES), jnp.float32),
        ],
        compiler_params=pltpu.CompilerParams(vmem_limit_bytes=32 * 2**20),
        name="cross",
    )(got)


def finish_kernel(x_ref, out_ref, *, rows, cols, chans):
    bands, _, _, _, pairs, _, _ = out_ref.shape
    row, col = lax.axis_index("row"), lax.axis_index("col")
    per_row = cols * chans
    sub = lax.broadcasted_iota(jnp.int32, (2, rows, SUB, LANES), 2)
    r_first = lax.broadcasted_iota(jnp.int32, (2, rows, SUB, LANES), 1)
    low = sub < per_row
    second = row * per_row + sub % per_row
    keep = [r_first * per_row + col * chans + k <= second for k in range(chans)]
    for b in range(bands):
        for c in range(pairs):
            s = (b * pairs + c) * 2
            one = x_ref[s].astype(jnp.float32).reshape(2, rows, SUB, LANES)
            two = x_ref[s + 1].astype(jnp.float32).reshape(2, rows, SUB, LANES)
            even = jnp.where(low, one, pltpu.roll(two, per_row, 2))
            odd = jnp.where(low, pltpu.roll(one, per_row, 2), two)
            out_ref[b, :, :, 0, c] = jnp.where(keep[0], even, 0.0)
            out_ref[b, :, :, 1, c] = jnp.where(keep[1], odd, 0.0)


def finish_packed(got, bands, bins, rows, cols, chans):
    chunks = bins // LANES
    out = pl.pallas_call(
        functools.partial(finish_kernel, rows=rows, cols=cols, chans=chans),
        out_shape=jax.ShapeDtypeStruct(
            (bands, 2, rows, chans, chunks // 2, SUB, LANES), jnp.float32
        ),
        in_specs=[pl.BlockSpec(memory_space=pltpu.VMEM)],
        out_specs=pl.BlockSpec(memory_space=pltpu.VMEM),
        compiler_params=pltpu.CompilerParams(vmem_limit_bytes=32 * 2**20),
        name="finish",
    )(got)
    out = out.reshape(bands, 2, rows * chans, chunks, cols * chans, LANES)
    out = out.transpose(0, 1, 2, 4, 3, 5)
    return out.reshape(bands, 2, 1, rows * chans, cols * chans, bins)


def on_device(spectra, window_flags):
    bands, windows, _, chans, bins = spectra.shape
    rows, cols = lax.axis_size("row"), lax.axis_size("col")
    devices = rows * cols
    packed = (
        bands * bins == devices * LANES
        and bins % (2 * LANES) == 0
        and chans == 2
        and cols * chans * 2 == SUB
        and windows % 16 == 0
    )
    if packed:
        payload = whiten_packed(spectra, window_flags)
    else:
        payload = whiten_plain(spectra, window_flags, devices)
    got = lax.all_to_all(payload, ("row", "col"), 0, 0, tiled=True)
    if packed:
        result = cross_packed(got, rows, cols, chans, windows)
    else:
        result = cross_plain(got, rows, cols, chans, windows)
    back = lax.all_to_all(result, ("row", "col"), 0, 0, tiled=True)
    if packed:
        return finish_packed(back, bands, bins, rows, cols, chans)
    return finish_plain(back, bands, bins, rows, cols, chans)


def solution(mesh):
    in_specs = (P("parts", None, None, ("row", "col"), None), P("parts", ("row", "col")))
    out_specs = P("parts", None, "col", None, "row", None)
    return jax.shard_map(
        on_device, mesh=mesh, in_specs=in_specs, out_specs=out_specs, check_vma=False
    )
```

time: 215 us -> 50.3 us (0.23)
  waiting for transfers between devices: 53.7 us -> 0 us
  matrix products: 53.1 us -> 0 us
  other arithmetic: 49 us -> 0 us
  local copies, waits for them, and re-layouts: 40.1 us -> 1.72 us
  blocking collectives: 4.82 us -> 40 us
  between operations: 13.5 us -> 0.02 us
  Pallas kernels: 0 us -> 8.27 us
    dot_general x2 -> x0, matrix products: 53.1 us -> none  [on_device(): jnp.einsum('wpif,wqjf->pqijf', first_rows[0], second_rows[0], preferred_e...]
    all_gather x2 -> x0, waiting for transfers between devices: 53 us -> none  [on_device(): lax.all_gather(payload[band_index:band_index + 1], 'row', axis=3, tiled=T...]
    all_to_all x0 -> x2, blocking collectives: none -> 40 us  [the longest x1 21.7 us: on_device(): got = lax.all_to_all(payload, ('row', 'col'), 0, 0, tiled=True)]
    another operation x4 -> x0, other arithmetic: 36.7 us -> none
    all_gather x4 -> x0, local copies, waits for them, and re-layouts: 29 us -> none  [the longest x2 25 us: on_device(): lax.all_gather(payload[band_index:band_index + 1], 'row', axis=3, tiled=T...]
    mul x2 -> x0, other arithmetic: 10.7 us -> none  [the longest x1 9.47 us: combine_parts(): return jnp.stack([real_part * keep, imag_part * keep], axis=-4)]
    pallas_call x0 -> x3, Pallas kernels: none -> 8.27 us  [the longest x1 4.23 us: cross_packed(): pl.pallas_call(functools.partial(cross_kernel, rows=rows, cols=cols, chan...]
    mul x4 -> x0, local copies, waits for them, and re-layouts: 6.3 us -> none  [combine_parts(): return jnp.stack([real_part * keep, imag_part * keep], axis=-4)]
  transfers between devices with their start and end apart: 2 -> 0, of which waited for: 2 -> 0; matrix products, arithmetic and copies ran while one was open for 20% -> 0% of each run, Pallas kernels for 0% -> 0%
where the time goes in v1:
time: 50.3 us; the launch traced here: 50 us
  blocking collectives  40 us (80%)
  Pallas kernels  8.27 us (16%)
  local copies, waits for them, and re-layouts  1.72 us (3%)
    all_to_all x1, blocking collectives, on_device(): got = lax.all_to_all(payload, ('row', 'col'), 0, 0, tiled=True)  21.7 us
    all_to_all x1, blocking collectives, on_device(): back = lax.all_to_all(result, ('row', 'col'), 0, 0, tiled=True)  18.4 us
    pallas_call x1, Pallas kernels, cross_packed(): pl.pallas_call(functools.partial(cross_kernel, rows=rows, cols=cols, chan...  4.23 us
    pallas_call x1, Pallas kernels, whiten_packed(): pl.pallas_call(functools.partial(whiten_kernel, chans=chans), out_shape=j...  2.89 us
    unnamed x4, local copies, waits for them, and re-layouts  1.72 us
    pallas_call x1, Pallas kernels, finish_packed(): pl.pallas_call(functools.partial(finish_kernel, rows=rows, cols=cols, cha...  1.15 us

profile of v1, /device:TPU:0, one launch (start us, length us, event | category | flops | bytes accessed | tf_op | source)
XLA Modules:
  0.0 50.0 jit_solution(7189105999672197574)
XLA Ops:
  0.0 0.0 copy-start.1
  0.0 0.7 %copy-done.1 = s32[32,2]{0,1:T(2,128)S(1)} copy-done((s32[32,2]{0,1:T(2,128)S(1)}, s32[32,2]{0,1:T(2,128)}, u32[]{:S(2)}) %copy-start.1) | copy-done | bytes 280
  0.7 0.0 copy-start
  0.7 1.0 %copy-done = bf16[2,32,2,2,1024]{4,3,2,1,0:T(2,128)(2,1)S(1)} copy-done((bf16[2,32,2,2,1024]{4,3,2,1,0:T(2,128)(2,1)S(1)}, bf16[2,32,2,2,1024]{4,3,2,1,0:T(2,128)(2,1)}, u32[]{:S(2)}) %copy-start) | copy-done | bytes 524312
  1.7 2.9 %whiten.1 = bf16[16,128,128]{2,1,0:T(8,128)(2,1)S(1)} custom-call(s32[2,32]{1,0:T(2,128)S(1)} %bitcast.12, bf16[2,32,2,16,128]{4,3,2,1,0:T(8,128)(2,1)S(1)} %bitcast.11), custom_call_target="tpu_custom_call" | custom-call | tf_op jit(solution)/shard_map/whiten/pallas_call | solution.py:131
  4.6 21.7 %all_to_all.10.x_ref = bf16[16,128,128]{2,1,0:T(8,128)(2,1)S(1)} all-to-all(bf16[16,128,128]{2,1,0:T(8,128)(2,1)S(1)} %whiten.1), channel_id=1, replica_groups=mesh['parts'=2,'row'=8,'col'=2] {'row','col'}, dimensions={0} | all-to-all | bytes 1048576 | tf_op jit(solution)/shard_map/all_to_all | solution.py:282
  26.3 4.2 %cross.1 = bf16[16,128,128]{2,1,0:T(8,128)(2,1)S(1)} custom-call(bf16[16,128,128]{2,1,0:T(8,128)(2,1)S(1)} %all_to_all.10.x_ref), custom_call_target="tpu_custom_call" | custom-call | tf_op jit(solution)/shard_map/cross/pallas_call | solution.py:216
  30.5 18.4 %all_to_all.11.x_ref = bf16[16,128,128]{2,1,0:T(8,128)(2,1)S(1)} all-to-all(bf16[16,128,128]{2,1,0:T(8,128)(2,1)S(1)} %cross.1), channel_id=1, replica_groups=mesh['parts'=2,'row'=8,'col'=2] {'row','col'}, dimensions={0} | all-to-all | bytes 1048576 | tf_op jit(solution)/shard_map/all_to_all | solution.py:287
  48.9 1.2 %finish.1 = f32[2,2,8,2,4,8,128]{6,5,4,3,2,1,0:T(8,128)} custom-call(bf16[16,128,128]{2,1,0:T(8,128)(2,1)S(1)} %all_to_all.11.x_ref), custom_call_target="tpu_custom_call" | custom-call | tf_op jit(solution)/shard_map/finish/pallas_call | solution.py:252
Async XLA Ops:
  0.0 0.7 %copy-start.1 = (s32[32,2]{0,1:T(2,128)S(1)}, s32[32,2]{0,1:T(2,128)}, u32[]{:S(2)}) copy-start(s32[32,2]{0,1:T(2,128)} %param.3) | copy-start | bytes 772
  0.7 1.0 %copy-start = (bf16[2,32,2,2,1024]{4,3,2,1,0:T(2,128)(2,1)S(1)}, bf16[2,32,2,2,1024]{4,3,2,1,0:T(2,128)(2,1)}, u32[]{:S(2)}) copy-start(bf16[2,32,2,2,1024]{4,3,2,1,0:T(2,128)(2,1)} %param.2) | copy-start | bytes 1572868

commit v2 on v1

v2 whole, which is shorter than its diff:
```python
import functools

import jax
import jax.numpy as jnp
from jax import lax
from jax.experimental import pallas as pl
from jax.experimental.pallas import tpu as pltpu
from jax.sharding import PartitionSpec as P

HALFWIN = 64
LANES = 128
SUB = 8

epsilon = 1e-06


def window_mean(magnitude):
    bins = magnitude.shape[-1]
    lead = [(0, 0)] * (magnitude.ndim - 1)
    padded = jnp.pad(magnitude, lead + [(HALFWIN + 1, HALFWIN)])
    running = jnp.cumsum(padded, axis=-1)
    total = running[..., 2 * HALFWIN + 1 :] - running[..., :bins]
    positions = jnp.arange(bins, dtype=jnp.int32)
    counted = (
        jnp.minimum(positions + HALFWIN, bins - 1) - jnp.maximum(positions - HALFWIN, 0) + 1
    ).astype(jnp.float32)
    return total / counted


def whiten_plain(spectra, window_flags, devices):
    bands, windows, parts, chans, bins = spectra.shape
    flags = window_flags.astype(jnp.float32)[None, :, None, :, None]
    values = spectra.astype(jnp.float32) * flags
    magnitude = jnp.sqrt(values[:, :, 0] * values[:, :, 0] + values[:, :, 1] * values[:, :, 1])
    smooth = window_mean(magnitude)
    white = (values / (smooth[:, :, None] + epsilon)).astype(jnp.bfloat16)
    own = bands * bins // devices
    white = white.reshape(bands, windows, parts, chans, bins // own, own)
    white = white.transpose(0, 4, 3, 2, 1, 5)
    return white.reshape(devices, chans * parts * windows, own)


def cross_plain(got, rows, cols, chans, windows):
    own = got.shape[-1]
    data = got.reshape(rows * cols * chans, 2, windows, own)
    prods = jnp.einsum("apwf,jqwf->pqajf", data, data, preferred_element_type=jnp.float32)
    both = jnp.stack([prods[0, 0] + prods[1, 1], prods[1, 0] - prods[0, 1]])
    both = both.reshape(2, rows, cols, chans, rows, cols * chans, own)
    both = both.transpose(4, 2, 0, 1, 3, 5, 6).astype(jnp.bfloat16)
    return both.reshape(rows * cols, 2 * rows * chans * cols * chans, own)


def finish_plain(got, bands, bins, rows, cols, chans):
    own = got.shape[-1]
    row, col = lax.axis_index("row"), lax.axis_index("col")
    data = got.reshape(bands, bins // own, 2, rows * chans, cols * chans, own)
    data = data.transpose(0, 2, 3, 4, 1, 5).reshape(
        bands, 2, rows * chans, cols * chans, bins
    )
    slot = jnp.arange(rows * chans, dtype=jnp.int32)
    first = (slot // chans * cols + col) * chans + slot % chans
    second = row * cols * chans + jnp.arange(cols * chans, dtype=jnp.int32)
    keep = (first[:, None] <= second[None, :])[:, :, None]
    return jnp.where(keep, data.astype(jnp.float32), 0.0)[:, :, None]


def whiten_kernel(flags_ref, x_ref, *refs, chans, tiles):
    out_refs, white_ref = refs[:-1], refs[-1]
    bands, windows, _, group, _ = x_ref.shape
    chunks = group // chans
    step = 8
    rows = step * group
    row_id = lax.broadcasted_iota(jnp.int32, (rows, LANES), 0) % group
    lane_id = lax.broadcasted_iota(jnp.int32, (rows, LANES), 1)
    spot = row_id // chans * LANES + lane_id
    last = chunks * LANES - 1
    counted = jnp.minimum(spot + HALFWIN, last) - jnp.maximum(spot - HALFWIN, 0) + 1
    inv_count = 1.0 / counted.astype(jnp.float32)
    has_prev = row_id >= chans
    has_next = row_id < group - chans
    k_id = lax.broadcasted_iota(jnp.int32, (group, LANES), 0) % chans
    src = lax.broadcasted_iota(jnp.int32, (LANES, 3 * LANES), 0)
    dst = lax.broadcasted_iota(jnp.int32, (LANES, 3 * LANES), 1) - LANES
    band_mat = jnp.where(jnp.abs(src - dst) <= HALFWIN, 1.0, 0.0).astype(jnp.bfloat16)

    def body(n, carry):
        b = n // (windows // step)
        w0 = n % (windows // step) * step
        x = x_ref[b, pl.ds(w0, step)].astype(jnp.float32)
        keeps = []
        for s in range(step):
            keep = jnp.full((group, LANES), flags_ref[0, w0 + s], jnp.int32)
            for k in range(1, chans):
                keep = jnp.where(k_id == k, flags_ref[k, w0 + s], keep)
            keeps.append(keep)
        keep = jnp.stack(keeps).astype(jnp.float32)
        re = (x[:, 0] * keep).reshape(rows, LANES)
        im = (x[:, 1] * keep).reshape(rows, LANES)
        mag = jnp.sqrt(re * re + im * im)
        high = mag.astype(jnp.bfloat16)
        low = (mag - high.astype(jnp.float32)).astype(jnp.bfloat16)
        sums = jnp.dot(high, band_mat, preferred_element_type=jnp.float32) + jnp.dot(
            low, band_mat, preferred_element_type=jnp.float32
        )
        total = sums[:, LANES : 2 * LANES]
        total += jnp.where(has_prev, pltpu.roll(sums[:, 2 * LANES :], chans, 0), 0.0)
        total += jnp.where(has_next, pltpu.roll(sums[:, :LANES], rows - chans, 0), 0.0)
        inv = 1.0 / (total * inv_count + epsilon)
        for p, part in enumerate((re, im)):
            start = pl.multiple_of(((b * 2 + p) * windows + w0) * group, rows)
            white_ref[pl.ds(start, rows), :] = part * inv
        return carry

    lax.fori_loop(0, bands * windows // step, body, 0)
    row = lax.axis_index("row")
    for n, out_ref in enumerate(out_refs):
        for t in range(tiles):
            place = (row ^ n) * tiles + t
            b, c = place // chunks, place % chunks
            for k in range(chans):
                for p in range(2):
                    start = (b * 2 + p) * windows * group + c * chans + k
                    slab = white_ref[pl.ds(start, windows, stride=group), :]
                    at = (k * 2 + p) * windows
                    out_ref[t, at : at + windows, :] = slab.astype(jnp.bfloat16)


def whiten_packed(spectra, window_flags, rows):
    bands, windows, parts, chans, bins = spectra.shape
    chunks = bins // LANES
    tiles = bands * chunks // rows
    view = spectra.reshape(bands, windows, parts, chans, chunks, LANES)
    view = view.transpose(0, 1, 2, 4, 3, 5).reshape(bands, windows, parts, chunks * chans, LANES)
    piece = jax.ShapeDtypeStruct((tiles, chans * parts * windows, LANES), jnp.bfloat16)
    return pl.pallas_call(
        functools.partial(whiten_kernel, chans=chans, tiles=tiles),
        out_shape=[piece] * rows,
        in_specs=[
            pl.BlockSpec(memory_space=pltpu.SMEM),
            pl.BlockSpec(memory_space=pltpu.VMEM),
        ],
        out_specs=[pl.BlockSpec(memory_space=pltpu.VMEM)] * rows,
        scratch_shapes=[
            pltpu.VMEM((bands * parts * windows * chunks * chans, LANES), jnp.float32)
        ],
        compiler_params=pltpu.CompilerParams(vmem_limit_bytes=32 * 2**20),
        cost_estimate=pl.CostEstimate(flops=10**9, bytes_accessed=2**20, transcendentals=0),
        name="whiten",
    )(window_flags.T, view)


def cross_kernel(*refs, rows, chans, tiles, windows):
    got, other, out_refs = refs[:rows], refs[rows : 2 * rows], refs[2 * rows : 3 * rows]
    first_ref, second_ref = refs[3 * rows :]
    firsts = rows * chans
    row = lax.axis_index("row")

    for n in range(rows):
        for s, ref in enumerate((got[n], other[n])):
            for t in range(tiles):
                for k in range(chans):
                    at = k * 2 * windows
                    re = ref[t, at : at + windows, :].astype(jnp.float32)
                    im = ref[t, at + windows : at + 2 * windows, :].astype(jnp.float32)
                    both = re + im
                    second_ref[s, n, t, k, 0] = re
                    second_ref[s, n, t, k, 1] = im - re
                    second_ref[s, n, t, k, 2] = both
                    if s == 0:
                        slot = pl.ds((row ^ n) * chans + k, windows, stride=firsts)
                        first_ref[0, t, slot, :] = both
                        first_ref[1, t, slot, :] = im
                        first_ref[2, t, slot, :] = re

    half = rows // 2
    blocks = firsts // SUB
    zero = jnp.zeros((SUB, LANES), jnp.float32)
    top = row // half
    for m in range(half):
        for s in range(2):
            for t in range(tiles):
                n_up = m + (1 - top) * half
                n_low = m + top * half
                work = [(n_up, k, blocks) for k in range(chans)]
                work += [(n_low, k, blocks // 2) for k in range(chans)]

                def body(w, sums, work=work, s=s, t=t):
                    base = pl.multiple_of(w * firsts, firsts)
                    fs = [
                        [first_ref[q, t, pl.ds(base + i * SUB, SUB), :] for q in range(3)]
                        for i in range(blocks)
                    ]
                    out = []
                    at = 0
                    for n, k, count in work:
                        g = [second_ref[s, n, t, k, q, pl.ds(w, 1), :] for q in range(3)]
                        for i in range(count):
                            s1, s2, s3 = sums[at]
                            at += 1
                            out.append(
                                (s1 + g[0] * fs[i][0], s2 + g[1] * fs[i][1], s3 + g[2] * fs[i][2])
                            )
                    return tuple(out)

                total = sum(count for _, _, count in work)
                sums = lax.fori_loop(0, windows, body, ((zero, zero, zero),) * total, unroll=4)
                parts = []
                at = 0
                for _, k, count in work:
                    mine = sums[at : at + count]
                    at += count
                    for q in range(2):
                        vals = [x[0] - x[2] if q else x[0] + x[1] for x in mine]
                        vals += [zero] * (blocks - count)
                        parts.append(jnp.concatenate(vals).astype(jnp.bfloat16))

                def put(up_ref, low_ref, parts=parts, s=s, t=t):
                    for e, ref in enumerate((up_ref, low_ref)):
                        for k in range(chans):
                            for q in range(2):
                                spot = ((q * 2 + s) * chans + k) * firsts
                                ref[t, spot : spot + firsts, :] = parts[(e * chans + k) * 2 + q]

                pl.when(top == 0)(lambda m=m, put=put: put(out_refs[m + half], out_refs[m]))
                pl.when(top == 1)(lambda m=m, put=put: put(out_refs[m], out_refs[m + half]))


def cross_packed(got, other, rows, cols, chans, windows):
    tiles = got[0].shape[0]
    size = 2 * cols * chans * rows * chans
    piece = jax.ShapeDtypeStruct((tiles, size, LANES), jnp.bfloat16)
    return pl.pallas_call(
        functools.partial(cross_kernel, rows=rows, chans=chans, tiles=tiles, windows=windows),
        out_shape=[piece] * rows,
        in_specs=[pl.BlockSpec(memory_space=pltpu.VMEM)] * (2 * rows),
        out_specs=[pl.BlockSpec(memory_space=pltpu.VMEM)] * rows,
        scratch_shapes=[
            pltpu.VMEM((3, tiles, windows * rows * chans, LANES), jnp.float32),
            pltpu.VMEM((2, rows, tiles, chans, 3, windows, LANES), jnp.float32),
        ],
        compiler_params=pltpu.CompilerParams(vmem_limit_bytes=32 * 2**20),
        cost_estimate=pl.CostEstimate(flops=10**9, bytes_accessed=2**20, transcendentals=0),
        name="cross",
    )(*got, *other)


def finish_kernel(*refs, rows, chans):
    got, out_ref, wide_ref = refs[:rows], refs[rows], refs[rows + 1]
    bands, _, firsts, quads, _, _ = out_ref.shape
    row, col = lax.axis_index("row"), lax.axis_index("col")
    per_row = 2 * chans
    second = row * per_row + lax.broadcasted_iota(jnp.int32, (SUB, LANES), 0) % per_row
    for n in range(rows):
        place = row ^ n
        b, c = place // quads, place % quads
        for t in range(2):
            for q in range(2):
                for s in range(2):
                    half = col if s == 0 else 1 - col
                    for k in range(chans):
                        spot = ((q * 2 + s) * chans + k) * firsts
                        to = pl.multiple_of(
                            (q * SUB + t * per_row + half * chans + k) * firsts, firsts
                        )
                        wide_ref[n, pl.ds(to, firsts), :] = got[n][
                            t, spot : spot + firsts, :
                        ].astype(jnp.float32)
        for q in range(2):
            for i in range(firsts):
                first = i // chans * per_row + col * chans + i % chans
                vals = wide_ref[n, pl.ds(q * SUB * firsts + i, SUB, stride=firsts), :]
                out_ref[b, q, i, c] = jnp.where(first <= second, vals, 0.0)


def finish_packed(got, bands, bins, rows, cols, chans):
    chunks = bins // LANES
    firsts = rows * chans
    out = pl.pallas_call(
        functools.partial(finish_kernel, rows=rows, chans=chans),
        out_shape=jax.ShapeDtypeStruct((bands, 2, firsts, chunks // 2, SUB, LANES), jnp.float32),
        in_specs=[pl.BlockSpec(memory_space=pltpu.VMEM)] * rows,
        out_specs=pl.BlockSpec(memory_space=pltpu.VMEM),
        scratch_shapes=[pltpu.VMEM((rows, 2 * SUB * firsts, LANES), jnp.float32)],
        compiler_params=pltpu.CompilerParams(vmem_limit_bytes=32 * 2**20),
        cost_estimate=pl.CostEstimate(flops=10**9, bytes_accessed=2**20, transcendentals=0),
        name="finish",
    )(*got)
    out = out.reshape(bands, 2, firsts, chunks, cols * chans, LANES)
    out = out.transpose(0, 1, 2, 4, 3, 5)
    return out.reshape(bands, 2, 1, firsts, cols * chans, bins)


def to_row(value, n, rows):
    return lax.ppermute(value, "row", [(r, r ^ n) for r in range(rows)])


def on_device_packed(spectra, window_flags):
    bands, windows, _, chans, bins = spectra.shape
    rows, cols = lax.axis_size("row"), lax.axis_size("col")
    order = sorted(range(1, rows), reverse=True)
    pieces = whiten_packed(spectra, window_flags, rows)
    got = [pieces[0]] * rows
    for n in order:
        got[n] = to_row(pieces[n], n, rows)
    other = [lax.ppermute(g, "col", [(0, 1), (1, 0)]) for g in got]
    result = cross_packed(got, other, rows, cols, chans, windows)
    back = [result[0]] * rows
    for n in order:
        back[n] = to_row(result[n], n, rows)
    return finish_packed(back, bands, bins, rows, cols, chans)


def on_device(spectra, window_flags):
    bands, windows, _, chans, bins = spectra.shape
    rows, cols = lax.axis_size("row"), lax.axis_size("col")
    if (
        bands * bins == rows * 2 * LANES
        and bins % (2 * LANES) == 0
        and rows in (2, 4, 8)
        and cols == 2
        and chans == 2
        and rows * chans == 2 * SUB
        and windows % 16 == 0
    ):
        return on_device_packed(spectra, window_flags)
    payload = whiten_plain(spectra, window_flags, rows * cols)
    got = lax.all_to_all(payload, ("row", "col"), 0, 0, tiled=True)
    result = cross_plain(got, rows, cols, chans, windows)
    back = lax.all_to_all(result, ("row", "col"), 0, 0, tiled=True)
    return finish_plain(back, bands, bins, rows, cols, chans)


def solution(mesh):
    in_specs = (P("parts", None, None, ("row", "col"), None), P("parts", ("row", "col")))
    out_specs = P("parts", None, "col", None, "row", None)
    return jax.shard_map(
        on_device, mesh=mesh, in_specs=in_specs, out_specs=out_specs, check_vma=False
    )
```

time: 50.3 us -> 48.9 us (0.972)
  blocking collectives: 40 us -> 0 us
  starting transfers between devices: 0 us -> 25.8 us
  waiting for transfers between devices: 0 us -> 12 us
  Pallas kernels: 8.27 us -> 8.9 us
    all_to_all x2 -> x0, blocking collectives: 40 us -> none  [the longest x1 21.7 us: on_device(): got = lax.all_to_all(payload, ('row', 'col'), 0, 0, tiled=True)]
    ppermute x0 -> x22, starting transfers between devices: none -> 25.8 us  [the longest x14 23.7 us: to_row(): return lax.ppermute(value, 'row', [(r, r ^ n) for r in range(rows)])]
    ppermute x0 -> x22, waiting for transfers between devices: none -> 12 us  [the longest x14 11.1 us: to_row(): return lax.ppermute(value, 'row', [(r, r ^ n) for r in range(rows)])]
    pallas_call x3, Pallas kernels: 8.27 us -> 8.9 us  [the longest x1 4.41 us: cross_packed(): pl.pallas_call(functools.partial(cross_kernel, rows=rows, chans=chans, ti...]
  transfers between devices with their start and end apart: 0 -> 22, of which waited for: 0 -> 8; matrix products, arithmetic and copies ran while one was open for 0% -> 0% of each run, Pallas kernels for 0% -> 0%
where the time goes in v2:
time: 48.9 us; the launch traced here: 48.4 us
  starting transfers between devices  25.8 us (53%)
  waiting for transfers between devices  12 us (25%)
  Pallas kernels  8.9 us (18%)
  local copies, waits for them, and re-layouts  1.72 us (4%)
    ppermute x14, starting transfers between devices, to_row(): return lax.ppermute(value, 'row', [(r, r ^ n) for r in range(rows)])  23.7 us
    ppermute x14, waiting for transfers between devices, to_row(): return lax.ppermute(value, 'row', [(r, r ^ n) for r in range(rows)])  11.1 us
    pallas_call x1, Pallas kernels, cross_packed(): pl.pallas_call(functools.partial(cross_kernel, rows=rows, chans=chans, ti...  4.41 us
    pallas_call x1, Pallas kernels, whiten_packed(): pl.pallas_call(functools.partial(whiten_kernel, chans=chans, tiles=tiles)...  2.95 us
    ppermute x8, starting transfers between devices, on_device_packed(): other = [lax.ppermute(g, 'col', [(0, 1), (1, 0)]) for g in got]  2.09 us
    unnamed x4, local copies, waits for them, and re-layouts  1.72 us
    pallas_call x1, Pallas kernels, finish_packed(): pl.pallas_call(functools.partial(finish_kernel, rows=rows, chans=chans),...  1.54 us
  transfers between devices with their start and end apart: 22, of which 8 were waited for; matrix products, arithmetic and copies ran while one was open for 0% of the time, Pallas kernels for 0%

profile of v2, /device:TPU:0, one launch (start us, length us, event | category | flops | bytes accessed | tf_op | source)
XLA Modules:
  0.0 48.4 jit_solution(378547193520415885)
XLA Ops:
  0.0 0.0 copy-start.1
  0.0 0.7 %copy-done.1 = s32[32,2]{0,1:T(2,128)S(1)} copy-done((s32[32,2]{0,1:T(2,128)S(1)}, s32[32,2]{0,1:T(2,128)}, u32[]{:S(2)}) %copy-start.1) | copy-done | bytes 280
  0.7 0.0 copy-start
  0.7 1.0 %copy-done = bf16[2,32,2,2,1024]{4,3,2,1,0:T(2,128)(2,1)S(1)} copy-done((bf16[2,32,2,2,1024]{4,3,2,1,0:T(2,128)(2,1)S(1)}, bf16[2,32,2,2,1024]{4,3,2,1,0:T(2,128)(2,1)}, u32[]{:S(2)}) %copy-start) | copy-done | bytes 524312
  1.7 2.9 %whiten.1 = (bf16[2,128,128]{2,1,0:T(8,128)(2,1)S(1)}, bf16[2,128,128]{2,1,0:T(8,128)(2,1)S(1)}, bf16[2,128,128]{2,1,0:T(8,128)(2,1)S(1)}, bf16[2,128,128]{2,1,0...) custom-call(s32[2,32]{1,0:T(2,128)S(1)} %bitcast.12, ...), custom_call_target="tpu_custom_call" | custom-call | flops 1000000000 | bytes 1048576 | tf_op jit(solution)/shard_map/whiten/pallas_call | solution.py:135
  4.7 3.0 %collective-permute-start = (bf16[2,128,128]{2,1,0:T(8,128)(2,1)S(1)}, bf16[2,128,128]{2,1,0:T(8,128)(2,1)S(1)}, u32[]{:S(2)}, u32[]{:S(2)}) collective-permute-start(bf16[2,128,128]{2,1,0:T(8,128)(2,1)S(1)} %get-tuple-element.22), channel_id=1, source_target_pairs={{0,2},{2,0},{4,6},{6,4},{8,10},{10,8},{12,14},{14,12},{1,3},{3,1},... | collective-permute-start | bytes 196616 | tf_op jit(solution)/shard_map/ppermute | solution.py:294
  7.7 1.6 %collective-permute-start.1 = (bf16[2,128,128]{2,1,0:T(8,128)(2,1)S(1)}, bf16[2,128,128]{2,1,0:T(8,128)(2,1)S(1)}, u32[]{:S(2)}, u32[]{:S(2)}) collective-permute-start(bf16[2,128,128]{2,1,0:T(8,128)(2,1)S(1)} %get-tuple-element.23), channel_id=1, source_target_pairs={{0,4},{2,6},{4,0},{6,2},{8,12},{10,14},{12,8},{14,10},{1,5},{3,7},... | collective-permute-start | bytes 196616 | tf_op jit(solution)/shard_map/ppermute | solution.py:294
  9.3 0.0 collective-permute-start.2
  9.3 3.0 %collective-permute-start.3 = (bf16[2,128,128]{2,1,0:T(8,128)(2,1)S(1)}, bf16[2,128,128]{2,1,0:T(8,128)(2,1)S(1)}, u32[]{:S(2)}, u32[]{:S(2)}) collective-permute-start(bf16[2,128,128]{2,1,0:T(8,128)(2,1)S(1)} %get-tuple-element.25), channel_id=1, source_target_pairs={{0,8},{2,10},{4,12},{6,14},{8,0},{10,2},{12,4},{14,6},{1,9},{3,11}... | collective-permute-start | bytes 196616 | tf_op jit(solution)/shard_map/ppermute | solution.py:294
  12.3 1.3 %collective-permute-start.4 = (bf16[2,128,128]{2,1,0:T(8,128)(2,1)S(1)}, bf16[2,128,128]{2,1,0:T(8,128)(2,1)S(1)}, u32[]{:S(2)}, u32[]{:S(2)}) collective-permute-start(bf16[2,128,128]{2,1,0:T(8,128)(2,1)S(1)} %get-tuple-element.26), channel_id=1, source_target_pairs={{0,10},{2,8},{4,14},{6,12},{8,2},{10,0},{12,6},{14,4},{1,11},{3,9}... | collective-permute-start | bytes 196616 | tf_op jit(solution)/shard_map/ppermute | solution.py:294
  13.6 0.0 collective-permute-done.refs_1_
  13.6 3.6 %collective-permute-start.5 = (bf16[2,128,128]{2,1,0:T(8,128)(2,1)S(1)}, bf16[2,128,128]{2,1,0:T(8,128)(2,1)S(1)}, u32[]{:S(2)}, u32[]{:S(2)}) collective-permute-start(bf16[2,128,128]{2,1,0:T(8,128)(2,1)S(1)} %get-tuple-element.27), channel_id=1, source_target_pairs={{0,12},{2,14},{4,8},{6,10},{8,4},{10,6},{12,0},{14,2},{1,13},{3,15... | collective-permute-start | bytes 196616 | tf_op jit(solution)/shard_map/ppermute | solution.py:294
  17.2 0.0 collective-permute-done.1.refs_2_
  17.2 0.0 collective-permute-start.6
  17.2 0.0 collective-permute-done.2.refs_3_
  17.2 0.1 collective-permute-start.7
  17.3 0.0 collective-permute-done.3.refs_4_
  17.3 0.5 %collective-permute-start.8 = (bf16[2,128,128]{2,1,0:T(8,128)(2,1)S(1)}, bf16[2,128,128]{2,1,0:T(8,128)(2,1)S(1)}, u32[]{:S(2)}, u32[]{:S(2)}) collective-permute-start(bf16[2,128,128]{2,1,0:T(8,128)(2,1)S(1)} %collective-permute-done.refs_1_), channel_id=1, source_target_pairs={{0,1},{1,0},{2,3},{3,2},{4,5},{5,4},{6,7},{7,6},{8,9},{9,8},{10,11... | collective-permute-start | bytes 196616 | tf_op jit(solution)/shard_map/ppermute | solution.py:305
  17.8 4.7 %collective-permute-done.4.refs_5_ = bf16[2,128,128]{2,1,0:T(8,128)(2,1)S(1)} collective-permute-done((bf16[2,128,128]{2,1,0:T(8,128)(2,1)S(1)}, bf16[2,128,128]{2,1,0:T(8,128)(2,1)S(1)}, u32[]{:S(2)}, u32[]{:S(2)}) %collective-permute-start.4) | collective-permute-done | bytes 65568 | tf_op jit(solution)/shard_map/ppermute | solution.py:294
  22.5 0.0 collective-permute-start.9
  22.5 0.0 collective-permute-done.5.refs_6_
  22.5 0.5 %collective-permute-start.10 = (bf16[2,128,128]{2,1,0:T(8,128)(2,1)S(1)}, bf16[2,128,128]{2,1,0:T(8,128)(2,1)S(1)}, u32[]{:S(2)}, u32[]{:S(2)}) collective-permute-start(bf16[2,128,128]{2,1,0:T(8,128)(2,1)S(1)} %collective-permute-done.2.refs_3_), channel_id=1, source_target_pairs={{0,1},{1,0},{2,3},{3,2},{4,5},{5,4},{6,7},{7,6},{8,9},{9,8},{10,11... | collective-permute-start | bytes 196616 | tf_op jit(solution)/shard_map/ppermute | solution.py:305
  23.0 1.2 %collective-permute-done.6.refs_7_ = bf16[2,128,128]{2,1,0:T(8,128)(2,1)S(1)} collective-permute-done((bf16[2,128,128]{2,1,0:T(8,128)(2,1)S(1)}, bf16[2,128,128]{2,1,0:T(8,128)(2,1)S(1)}, u32[]{:S(2)}, u32[]{:S(2)}) %collective-permute-start.6) | collective-permute-done | bytes 65568 | tf_op jit(solution)/shard_map/ppermute | solution.py:294
  24.2 0.0 collective-permute-start.11
  24.2 0.0 collective-permute-done.7.refs_8_
  24.2 0.5 %collective-permute-start.12 = (bf16[2,128,128]{2,1,0:T(8,128)(2,1)S(1)}, bf16[2,128,128]{2,1,0:T(8,128)(2,1)S(1)}, u32[]{:S(2)}, u32[]{:S(2)}) collective-permute-start(bf16[2,128,128]{2,1,0:T(8,128)(2,1)S(1)} %collective-permute-done.4.refs_5_), channel_id=1, source_target_pairs={{0,1},{1,0},{2,3},{3,2},{4,5},{5,4},{6,7},{7,6},{8,9},{9,8},{10,11... | collective-permute-start | bytes 196616 | tf_op jit(solution)/shard_map/ppermute | solution.py:305
  24.7 0.0 collective-permute-done.8.refs_9_
  24.8 0.1 collective-permute-start.13
  24.8 0.0 collective-permute-done.9.refs_10_
  24.8 0.4 collective-permute-start.14
  25.3 0.0 collective-permute-done.10.refs_11_
  25.3 0.2 collective-permute-done.11.refs_12_
  25.5 0.2 collective-permute-done.12.refs_13_
  25.7 0.4 collective-permute-done.13.refs_14_
  26.0 0.2 collective-permute-done.14.refs_15_
  26.2 4.4 %cross.1 = (bf16[2,128,128]{2,1,0:T(8,128)(2,1)S(1)}, bf16[2,128,128]{2,1,0:T(8,128)(2,1)S(1)}, bf16[2,128,128]{2,1,0:T(8,128)(2,1)S(1)}, bf16[2,128,128]{2,1,0:...) custom-call(bf16[2,128,128]{2,1,0:T(8,128)(2,1)S(1)} %get-tuple-elem, ...), custom_call_target="tpu_custom_call" | custom-call | flops 1000000000 | bytes 1048576 | tf_op jit(solution)/shard_map/cross/pallas_call | solution.py:232
  30.6 0.6 %collective-permute-start.15 = (bf16[2,128,128]{2,1,0:T(8,128)(2,1)S(1)}, bf16[2,128,128]{2,1,0:T(8,128)(2,1)S(1)}, u32[]{:S(2)}, u32[]{:S(2)}) collective-permute-start(bf16[2,128,128]{2,1,0:T(8,128)(2,1)S(1)} %get-tuple-element.30), channel_id=1, source_target_pairs={{0,2},{2,0},{4,6},{6,4},{8,10},{10,8},{12,14},{14,12},{1,3},{3,1},... | collective-permute-start | bytes 196616 | tf_op jit(solution)/shard_map/ppermute | solution.py:294
  31.2 1.9 %collective-permute-start.16 = (bf16[2,128,128]{2,1,0:T(8,128)(2,1)S(1)}, bf16[2,128,128]{2,1,0:T(8,128)(2,1)S(1)}, u32[]{:S(2)}, u32[]{:S(2)}) collective-permute-start(bf16[2,128,128]{2,1,0:T(8,128)(2,1)S(1)} %get-tuple-element.31), channel_id=1, source_target_pairs={{0,4},{2,6},{4,0},{6,2},{8,12},{10,14},{12,8},{14,10},{1,5},{3,7},... | collective-permute-start | bytes 196616 | tf_op jit(solution)/shard_map/ppermute | solution.py:294
  33.1 1.1 %collective-permute-start.17 = (bf16[2,128,128]{2,1,0:T(8,128)(2,1)S(1)}, bf16[2,128,128]{2,1,0:T(8,128)(2,1)S(1)}, u32[]{:S(2)}, u32[]{:S(2)}) collective-permute-start(bf16[2,128,128]{2,1,0:T(8,128)(2,1)S(1)} %get-tuple-element.32), channel_id=1, source_target_pairs={{0,6},{2,4},{4,2},{6,0},{8,14},{10,12},{12,10},{14,8},{1,7},{3,5},... | collective-permute-start | bytes 196616 | tf_op jit(solution)/shard_map/ppermute | solution.py:294
  34.1 2.7 %collective-permute-start.18 = (bf16[2,128,128]{2,1,0:T(8,128)(2,1)S(1)}, bf16[2,128,128]{2,1,0:T(8,128)(2,1)S(1)}, u32[]{:S(2)}, u32[]{:S(2)}) collective-permute-start(bf16[2,128,128]{2,1,0:T(8,128)(2,1)S(1)} %get-tuple-element.33), channel_id=1, source_target_pairs={{0,8},{2,10},{4,12},{6,14},{8,0},{10,2},{12,4},{14,6},{1,9},{3,11}... | collective-permute-start | bytes 196616 | tf_op jit(solution)/shard_map/ppermute | solution.py:294
  36.9 0.1 collective-permute-start.19
  37.0 0.0 collective-permute-done.15.refs_1_
  37.0 2.2 %collective-permute-start.20 = (bf16[2,128,128]{2,1,0:T(8,128)(2,1)S(1)}, bf16[2,128,128]{2,1,0:T(8,128)(2,1)S(1)}, u32[]{:S(2)}, u32[]{:S(2)}) collective-permute-start(bf16[2,128,128]{2,1,0:T(8,128)(2,1)S(1)} %get-tuple-element.35), channel_id=1, source_target_pairs={{0,12},{2,14},{4,8},{6,10},{8,4},{10,6},{12,0},{14,2},{1,13},{3,15... | collective-permute-start | bytes 196616 | tf_op jit(solution)/shard_map/ppermute | solution.py:294
  39.3 0.0 collective-permute-done.16.refs_2_
  39.3 2.5 %collective-permute-start.21 = (bf16[2,128,128]{2,1,0:T(8,128)(2,1)S(1)}, bf16[2,128,128]{2,1,0:T(8,128)(2,1)S(1)}, u32[]{:S(2)}, u32[]{:S(2)}) collective-permute-start(bf16[2,128,128]{2,1,0:T(8,128)(2,1)S(1)} %get-tuple-element.36), channel_id=1, source_target_pairs={{0,14},{2,12},{4,10},{6,8},{8,6},{10,4},{12,2},{14,0},{1,15},{3,13... | collective-permute-start | bytes 196616 | tf_op jit(solution)/shard_map/ppermute | solution.py:294
  41.8 0.0 collective-permute-done.17.refs_3_
  41.8 2.5 %collective-permute-done.18.refs_4_ = bf16[2,128,128]{2,1,0:T(8,128)(2,1)S(1)} collective-permute-done((bf16[2,128,128]{2,1,0:T(8,128)(2,1)S(1)}, bf16[2,128,128]{2,1,0:T(8,128)(2,1)S(1)}, u32[]{:S(2)}, u32[]{:S(2)}) %collective-permute-start.18) | collective-permute-done | bytes 65568 | tf_op jit(solution)/shard_map/ppermute | solution.py:294
  44.3 2.6 %collective-permute-done.19.refs_5_ = bf16[2,128,128]{2,1,0:T(8,128)(2,1)S(1)} collective-permute-done((bf16[2,128,128]{2,1,0:T(8,128)(2,1)S(1)}, bf16[2,128,128]{2,1,0:T(8,128)(2,1)S(1)}, u32[]{:S(2)}, u32[]{:S(2)}) %collective-permute-start.19) | collective-permute-done | bytes 65568 | tf_op jit(solution)/shard_map/ppermute | solution.py:294
  46.9 0.0 collective-permute-done.20.refs_6_
  46.9 0.0 collective-permute-done.21.refs_7_
  46.9 1.5 %finish.1 = f32[2,2,16,4,8,128]{5,4,3,2,1,0:T(8,128)} custom-call(bf16[2,128,128]{2,1,0:T(8,128)(2,1)S(1)} %get-tuple-element.29.refs_0_, bf16[2,128,128]{2,1,0:T(8,128)(2,1)S(1)} %collective-permute-done.15.refs_1_, bf16[2,128,128]{2,1,0:T(8,128)(2,1)S(1)} %collective-permute-done.16.refs_2_, bf16[2,128,128]{2,1,0:T(8,128)(2,1)S(1)} %collective-permute-done.17.refs_3_, ...), custom_call_target="tpu_custom_call" | custom-call | flops 1000000000 | bytes 1048576 | tf_op jit(solution)/shard_map/finish/pallas_call | solution.py:278
Async XLA Ops:
  0.0 0.7 %copy-start.1 = (s32[32,2]{0,1:T(2,128)S(1)}, s32[32,2]{0,1:T(2,128)}, u32[]{:S(2)}) copy-start(s32[32,2]{0,1:T(2,128)} %param.3) | copy-start | bytes 772
  0.7 1.0 %copy-start = (bf16[2,32,2,2,1024]{4,3,2,1,0:T(2,128)(2,1)S(1)}, bf16[2,32,2,2,1024]{4,3,2,1,0:T(2,128)(2,1)}, u32[]{:S(2)}) copy-start(bf16[2,32,2,2,1024]{4,3,2,1,0:T(2,128)(2,1)} %param.2) | copy-start | bytes 1572868
  4.7 8.9 %collective-permute-start = (bf16[2,128,128]{2,1,0:T(8,128)(2,1)S(1)}, bf16[2,128,128]{2,1,0:T(8,128)(2,1)S(1)}, u32[]{:S(2)}, u32[]{:S(2)}) collective-permute-start(bf16[2,128,128]{2,1,0:T(8,128)(2,1)S(1)} %get-tuple-element.22), channel_id=1, source_target_pairs={{0,2},{2,0},{4,6},{6,4},{8,10},{10,8},{12,14},{14,12},{1,3},{3,1},... | collective-permute-start | bytes 196616 | tf_op jit(solution)/shard_map/ppermute | solution.py:294
  7.7 9.5 %collective-permute-start.1 = (bf16[2,128,128]{2,1,0:T(8,128)(2,1)S(1)}, bf16[2,128,128]{2,1,0:T(8,128)(2,1)S(1)}, u32[]{:S(2)}, u32[]{:S(2)}) collective-permute-start(bf16[2,128,128]{2,1,0:T(8,128)(2,1)S(1)} %get-tuple-element.23), channel_id=1, source_target_pairs={{0,4},{2,6},{4,0},{6,2},{8,12},{10,14},{12,8},{14,10},{1,5},{3,7},... | collective-permute-start | bytes 196616 | tf_op jit(solution)/shard_map/ppermute | solution.py:294
  9.3 7.9 %collective-permute-start.2 = (bf16[2,128,128]{2,1,0:T(8,128)(2,1)S(1)}, bf16[2,128,128]{2,1,0:T(8,128)(2,1)S(1)}, u32[]{:S(2)}, u32[]{:S(2)}) collective-permute-start(bf16[2,128,128]{2,1,0:T(8,128)(2,1)S(1)} %get-tuple-element.24), channel_id=1, source_target_pairs={{0,6},{2,4},{4,2},{6,0},{8,14},{10,12},{12,10},{14,8},{1,7},{3,5},... | collective-permute-start | bytes 196616 | tf_op jit(solution)/shard_map/ppermute | solution.py:294
  9.3 8.0 %collective-permute-start.3 = (bf16[2,128,128]{2,1,0:T(8,128)(2,1)S(1)}, bf16[2,128,128]{2,1,0:T(8,128)(2,1)S(1)}, u32[]{:S(2)}, u32[]{:S(2)}) collective-permute-start(bf16[2,128,128]{2,1,0:T(8,128)(2,1)S(1)} %get-tuple-element.25), channel_id=1, source_target_pairs={{0,8},{2,10},{4,12},{6,14},{8,0},{10,2},{12,4},{14,6},{1,9},{3,11}... | collective-permute-start | bytes 196616 | tf_op jit(solution)/shard_map/ppermute | solution.py:294
  12.3 10.2 %collective-permute-start.4 = (bf16[2,128,128]{2,1,0:T(8,128)(2,1)S(1)}, bf16[2,128,128]{2,1,0:T(8,128)(2,1)S(1)}, u32[]{:S(2)}, u32[]{:S(2)}) collective-permute-start(bf16[2,128,128]{2,1,0:T(8,128)(2,1)S(1)} %get-tuple-element.26), channel_id=1, source_target_pairs={{0,10},{2,8},{4,14},{6,12},{8,2},{10,0},{12,6},{14,4},{1,11},{3,9}... | collective-permute-start | bytes 196616 | tf_op jit(solution)/shard_map/ppermute | solution.py:294
  13.6 8.9 %collective-permute-start.5 = (bf16[2,128,128]{2,1,0:T(8,128)(2,1)S(1)}, bf16[2,128,128]{2,1,0:T(8,128)(2,1)S(1)}, u32[]{:S(2)}, u32[]{:S(2)}) collective-permute-start(bf16[2,128,128]{2,1,0:T(8,128)(2,1)S(1)} %get-tuple-element.27), channel_id=1, source_target_pairs={{0,12},{2,14},{4,8},{6,10},{8,4},{10,6},{12,0},{14,2},{1,13},{3,15... | collective-permute-start | bytes 196616 | tf_op jit(solution)/shard_map/ppermute | solution.py:294
  17.2 7.1 %collective-permute-start.6 = (bf16[2,128,128]{2,1,0:T(8,128)(2,1)S(1)}, bf16[2,128,128]{2,1,0:T(8,128)(2,1)S(1)}, u32[]{:S(2)}, u32[]{:S(2)}) collective-permute-start(bf16[2,128,128]{2,1,0:T(8,128)(2,1)S(1)} %get-tuple-element.28), channel_id=1, source_target_pairs={{0,14},{2,12},{4,10},{6,8},{8,6},{10,4},{12,2},{14,0},{1,15},{3,13... | collective-permute-start | bytes 196616 | tf_op jit(solution)/shard_map/ppermute | solution.py:294
  17.2 7.1 %collective-permute-start.7 = (bf16[2,128,128]{2,1,0:T(8,128)(2,1)S(1)}, bf16[2,128,128]{2,1,0:T(8,128)(2,1)S(1)}, u32[]{:S(2)}, u32[]{:S(2)}) collective-permute-start(bf16[2,128,128]{2,1,0:T(8,128)(2,1)S(1)} %get-tuple-element.21.refs_0_), channel_id=1, source_target_pairs={{0,1},{1,0},{2,3},{3,2},{4,5},{5,4},{6,7},{7,6},{8,9},{9,8},{10,11... | collective-permute-start | bytes 196616 | tf_op jit(solution)/shard_map/ppermute | solution.py:305
  17.3 7.5 %collective-permute-start.8 = (bf16[2,128,128]{2,1,0:T(8,128)(2,1)S(1)}, bf16[2,128,128]{2,1,0:T(8,128)(2,1)S(1)}, u32[]{:S(2)}, u32[]{:S(2)}) collective-permute-start(bf16[2,128,128]{2,1,0:T(8,128)(2,1)S(1)} %collective-permute-done.refs_1_), channel_id=1, source_target_pairs={{0,1},{1,0},{2,3},{3,2},{4,5},{5,4},{6,7},{7,6},{8,9},{9,8},{10,11... | collective-permute-start | bytes 196616 | tf_op jit(solution)/shard_map/ppermute | solution.py:305
  22.5 2.3 %collective-permute-start.9 = (bf16[2,128,128]{2,1,0:T(8,128)(2,1)S(1)}, bf16[2,128,128]{2,1,0:T(8,128)(2,1)S(1)}, u32[]{:S(2)}, u32[]{:S(2)}) collective-permute-start(bf16[2,128,128]{2,1,0:T(8,128)(2,1)S(1)} %collective-permute-done.1.refs_2_), channel_id=1, source_target_pairs={{0,1},{1,0},{2,3},{3,2},{4,5},{5,4},{6,7},{7,6},{8,9},{9,8},{10,11... | collective-permute-start | bytes 196616 | tf_op jit(solution)/shard_map/ppermute | solution.py:305
  22.5 2.8 %collective-permute-start.10 = (bf16[2,128,128]{2,1,0:T(8,128)(2,1)S(1)}, bf16[2,128,128]{2,1,0:T(8,128)(2,1)S(1)}, u32[]{:S(2)}, u32[]{:S(2)}) collective-permute-start(bf16[2,128,128]{2,1,0:T(8,128)(2,1)S(1)} %collective-permute-done.2.refs_3_), channel_id=1, source_target_pairs={{0,1},{1,0},{2,3},{3,2},{4,5},{5,4},{6,7},{7,6},{8,9},{9,8},{10,11... | collective-permute-start | bytes 196616 | tf_op jit(solution)/shard_map/ppermute | solution.py:305
  24.2 1.3 %collective-permute-start.11 = (bf16[2,128,128]{2,1,0:T(8,128)(2,1)S(1)}, bf16[2,128,128]{2,1,0:T(8,128)(2,1)S(1)}, u32[]{:S(2)}, u32[]{:S(2)}) collective-permute-start(bf16[2,128,128]{2,1,0:T(8,128)(2,1)S(1)} %collective-permute-done.3.refs_4_), channel_id=1, source_target_pairs={{0,1},{1,0},{2,3},{3,2},{4,5},{5,4},{6,7},{7,6},{8,9},{9,8},{10,11... | collective-permute-start | bytes 196616 | tf_op jit(solution)/shard_map/ppermute | solution.py:305
  24.2 1.4 %collective-permute-start.12 = (bf16[2,128,128]{2,1,0:T(8,128)(2,1)S(1)}, bf16[2,128,128]{2,1,0:T(8,128)(2,1)S(1)}, u32[]{:S(2)}, u32[]{:S(2)}) collective-permute-start(bf16[2,128,128]{2,1,0:T(8,128)(2,1)S(1)} %collective-permute-done.4.refs_5_), channel_id=1, source_target_pairs={{0,1},{1,0},{2,3},{3,2},{4,5},{5,4},{6,7},{7,6},{8,9},{9,8},{10,11... | collective-permute-start | bytes 196616 | tf_op jit(solution)/shard_map/ppermute | solution.py:305
  24.8 1.3 %collective-permute-start.13 = (bf16[2,128,128]{2,1,0:T(8,128)(2,1)S(1)}, bf16[2,128,128]{2,1,0:T(8,128)(2,1)S(1)}, u32[]{:S(2)}, u32[]{:S(2)}) collective-permute-start(bf16[2,128,128]{2,1,0:T(8,128)(2,1)S(1)} %collective-permute-done.5.refs_6_), channel_id=1, source_target_pairs={{0,1},{1,0},{2,3},{3,2},{4,5},{5,4},{6,7},{7,6},{8,9},{9,8},{10,11... | collective-permute-start | bytes 196616 | tf_op jit(solution)/shard_map/ppermute | solution.py:305
  24.8 1.3 %collective-permute-start.14 = (bf16[2,128,128]{2,1,0:T(8,128)(2,1)S(1)}, bf16[2,128,128]{2,1,0:T(8,128)(2,1)S(1)}, u32[]{:S(2)}, u32[]{:S(2)}) collective-permute-start(bf16[2,128,128]{2,1,0:T(8,128)(2,1)S(1)} %collective-permute-done.6.refs_7_), channel_id=1, source_target_pairs={{0,1},{1,0},{2,3},{3,2},{4,5},{5,4},{6,7},{7,6},{8,9},{9,8},{10,11... | collective-permute-start | bytes 196616 | tf_op jit(solution)/shard_map/ppermute | solution.py:305
  30.6 6.4 %collective-permute-start.15 = (bf16[2,128,128]{2,1,0:T(8,128)(2,1)S(1)}, bf16[2,128,128]{2,1,0:T(8,128)(2,1)S(1)}, u32[]{:S(2)}, u32[]{:S(2)}) collective-permute-start(bf16[2,128,128]{2,1,0:T(8,128)(2,1)S(1)} %get-tuple-element.30), channel_id=1, source_target_pairs={{0,2},{2,0},{4,6},{6,4},{8,10},{10,8},{12,14},{14,12},{1,3},{3,1},... | collective-permute-start | bytes 196616 | tf_op jit(solution)/shard_map/ppermute | solution.py:294
  31.2 8.1 %collective-permute-start.16 = (bf16[2,128,128]{2,1,0:T(8,128)(2,1)S(1)}, bf16[2,128,128]{2,1,0:T(8,128)(2,1)S(1)}, u32[]{:S(2)}, u32[]{:S(2)}) collective-permute-start(bf16[2,128,128]{2,1,0:T(8,128)(2,1)S(1)} %get-tuple-element.31), channel_id=1, source_target_pairs={{0,4},{2,6},{4,0},{6,2},{8,12},{10,14},{12,8},{14,10},{1,5},{3,7},... | collective-permute-start | bytes 196616 | tf_op jit(solution)/shard_map/ppermute | solution.py:294
  33.1 8.7 %collective-permute-start.17 = (bf16[2,128,128]{2,1,0:T(8,128)(2,1)S(1)}, bf16[2,128,128]{2,1,0:T(8,128)(2,1)S(1)}, u32[]{:S(2)}, u32[]{:S(2)}) collective-permute-start(bf16[2,128,128]{2,1,0:T(8,128)(2,1)S(1)} %get-tuple-element.32), channel_id=1, source_target_pairs={{0,6},{2,4},{4,2},{6,0},{8,14},{10,12},{12,10},{14,8},{1,7},{3,5},... | collective-permute-start | bytes 196616 | tf_op jit(solution)/shard_map/ppermute | solution.py:294
  34.1 10.2 %collective-permute-start.18 = (bf16[2,128,128]{2,1,0:T(8,128)(2,1)S(1)}, bf16[2,128,128]{2,1,0:T(8,128)(2,1)S(1)}, u32[]{:S(2)}, u32[]{:S(2)}) collective-permute-start(bf16[2,128,128]{2,1,0:T(8,128)(2,1)S(1)} %get-tuple-element.33), channel_id=1, source_target_pairs={{0,8},{2,10},{4,12},{6,14},{8,0},{10,2},{12,4},{14,6},{1,9},{3,11}... | collective-permute-start | bytes 196616 | tf_op jit(solution)/shard_map/ppermute | solution.py:294
  36.9 10.0 %collective-permute-start.19 = (bf16[2,128,128]{2,1,0:T(8,128)(2,1)S(1)}, bf16[2,128,128]{2,1,0:T(8,128)(2,1)S(1)}, u32[]{:S(2)}, u32[]{:S(2)}) collective-permute-start(bf16[2,128,128]{2,1,0:T(8,128)(2,1)S(1)} %get-tuple-element.34), channel_id=1, source_target_pairs={{0,10},{2,8},{4,14},{6,12},{8,2},{10,0},{12,6},{14,4},{1,11},{3,9}... | collective-permute-start | bytes 196616 | tf_op jit(solution)/shard_map/ppermute | solution.py:294
  37.0 9.9 %collective-permute-start.20 = (bf16[2,128,128]{2,1,0:T(8,128)(2,1)S(1)}, bf16[2,128,128]{2,1,0:T(8,128)(2,1)S(1)}, u32[]{:S(2)}, u32[]{:S(2)}) collective-permute-start(bf16[2,128,128]{2,1,0:T(8,128)(2,1)S(1)} %get-tuple-element.35), channel_id=1, source_target_pairs={{0,12},{2,14},{4,8},{6,10},{8,4},{10,6},{12,0},{14,2},{1,13},{3,15... | collective-permute-start | bytes 196616 | tf_op jit(solution)/shard_map/ppermute | solution.py:294
  39.3 7.6 %collective-permute-start.21 = (bf16[2,128,128]{2,1,0:T(8,128)(2,1)S(1)}, bf16[2,128,128]{2,1,0:T(8,128)(2,1)S(1)}, u32[]{:S(2)}, u32[]{:S(2)}) collective-permute-start(bf16[2,128,128]{2,1,0:T(8,128)(2,1)S(1)} %get-tuple-element.36), channel_id=1, source_target_pairs={{0,14},{2,12},{4,10},{6,8},{8,6},{10,4},{12,2},{14,0},{1,15},{3,13... | collective-permute-start | bytes 196616 | tf_op jit(solution)/shard_map/ppermute | solution.py:294

commit v3 on v0

v3 whole, which is shorter than its diff:
```python
import functools

import jax
import jax.numpy as jnp
from jax import lax
from jax.experimental import pallas as pl
from jax.experimental.pallas import tpu as pltpu
from jax.sharding import PartitionSpec as P

HALFWIN = 64
LANES = 128
SUB = 8

epsilon = 1e-06


def window_mean(magnitude):
    bins = magnitude.shape[-1]
    lead = [(0, 0)] * (magnitude.ndim - 1)
    padded = jnp.pad(magnitude, lead + [(HALFWIN + 1, HALFWIN)])
    running = jnp.cumsum(padded, axis=-1)
    total = running[..., 2 * HALFWIN + 1 :] - running[..., :bins]
    positions = jnp.arange(bins, dtype=jnp.int32)
    counted = (
        jnp.minimum(positions + HALFWIN, bins - 1) - jnp.maximum(positions - HALFWIN, 0) + 1
    ).astype(jnp.float32)
    return total / counted


def whiten_plain(spectra, window_flags, devices):
    bands, windows, parts, chans, bins = spectra.shape
    flags = window_flags.astype(jnp.float32)[None, :, None, :, None]
    values = spectra.astype(jnp.float32) * flags
    magnitude = jnp.sqrt(values[:, :, 0] * values[:, :, 0] + values[:, :, 1] * values[:, :, 1])
    smooth = window_mean(magnitude)
    white = (values / (smooth[:, :, None] + epsilon)).astype(jnp.bfloat16)
    own = bands * bins // devices
    white = white.reshape(bands, windows, parts, chans, bins // own, own)
    white = white.transpose(0, 4, 3, 2, 1, 5)
    return white.reshape(devices, chans * parts * windows, own)


def cross_plain(got, rows, cols, chans, windows):
    own = got.shape[-1]
    data = got.reshape(rows * cols * chans, 2, windows, own)
    prods = jnp.einsum("apwf,jqwf->pqajf", data, data, preferred_element_type=jnp.float32)
    both = jnp.stack([prods[0, 0] + prods[1, 1], prods[1, 0] - prods[0, 1]])
    both = both.reshape(2, rows, cols, chans, rows, cols * chans, own)
    both = both.transpose(4, 2, 0, 1, 3, 5, 6).astype(jnp.bfloat16)
    return both.reshape(rows * cols, 2 * rows * chans * cols * chans, own)


def finish_plain(got, bands, bins, rows, cols, chans):
    own = got.shape[-1]
    row, col = lax.axis_index("row"), lax.axis_index("col")
    data = got.reshape(bands, bins // own, 2, rows * chans, cols * chans, own)
    data = data.transpose(0, 2, 3, 4, 1, 5).reshape(
        bands, 2, rows * chans, cols * chans, bins
    )
    slot = jnp.arange(rows * chans, dtype=jnp.int32)
    first = (slot // chans * cols + col) * chans + slot % chans
    second = row * cols * chans + jnp.arange(cols * chans, dtype=jnp.int32)
    keep = (first[:, None] <= second[None, :])[:, :, None]
    return jnp.where(keep, data.astype(jnp.float32), 0.0)[:, :, None]


TILES = 2
VMEM_FIRST = 65454080


def whiten_kernel(flags_hbm, x_hbm, out_ref, flags_ref, x_ref, white_ref, sems, *, chans):
    bands, windows, _, group, _ = x_ref.shape
    chunks = group // chans
    step = 16
    steps = windows // step
    rows = step * group

    copies = [pltpu.make_async_copy(flags_hbm, flags_ref, sems.at[bands * steps])]
    for n in range(bands * steps):
        part = (n // steps, pl.ds(n % steps * step, step))
        copies.append(pltpu.make_async_copy(x_hbm.at[part], x_ref.at[part], sems.at[n]))
    for copy in copies:
        copy.start()

    row_id = lax.broadcasted_iota(jnp.int32, (rows, LANES), 0) % group
    lane_id = lax.broadcasted_iota(jnp.int32, (rows, LANES), 1)
    spot = row_id // chans * LANES + lane_id
    last = chunks * LANES - 1
    counted = jnp.minimum(spot + HALFWIN, last) - jnp.maximum(spot - HALFWIN, 0) + 1
    inv_count = 1.0 / counted.astype(jnp.float32)
    has_prev = row_id >= chans
    has_next = row_id < group - chans
    k_id = lax.broadcasted_iota(jnp.int32, (group, LANES), 0) % chans
    src = lax.broadcasted_iota(jnp.int32, (LANES, 3 * LANES), 0)
    dst = lax.broadcasted_iota(jnp.int32, (LANES, 3 * LANES), 1) - LANES
    band_mat = jnp.where(jnp.abs(src - dst) <= HALFWIN, 1.0, 0.0).astype(jnp.bfloat16)

    copies[0].wait()
    for b in range(bands):
        for n in range(steps):
            w0 = n * step
            copies[1 + b * steps + n].wait()
            x = x_ref[b, w0 : w0 + step].astype(jnp.float32)
            keeps = []
            for s in range(step):
                keep = jnp.full((group, LANES), flags_ref[0, w0 + s], jnp.int32)
                for k in range(1, chans):
                    keep = jnp.where(k_id == k, flags_ref[k, w0 + s], keep)
                keeps.append(keep)
            keep = jnp.stack(keeps).astype(jnp.float32)
            re = (x[:, 0] * keep).reshape(rows, LANES)
            im = (x[:, 1] * keep).reshape(rows, LANES)
            mag = jnp.sqrt(re * re + im * im)
            high = mag.astype(jnp.bfloat16)
            rest = (mag - high.astype(jnp.float32)).astype(jnp.bfloat16)
            sums = jnp.dot(high, band_mat, preferred_element_type=jnp.float32) + jnp.dot(
                rest, band_mat, preferred_element_type=jnp.float32
            )
            total = sums[:, LANES : 2 * LANES]
            total += jnp.where(has_prev, pltpu.roll(sums[:, 2 * LANES :], chans, 0), 0.0)
            total += jnp.where(has_next, pltpu.roll(sums[:, :LANES], rows - chans, 0), 0.0)
            inv = 1.0 / (total * inv_count + epsilon)
            for p, part in enumerate((re, im)):
                start = ((b * 2 + p) * windows + w0) * group
                white_ref[start : start + rows, :] = part * inv
        for c in range(chunks):
            for k in range(chans):
                for p in range(2):
                    start = (b * 2 + p) * windows * group + c * chans + k
                    slab = white_ref[pl.ds(start, windows, stride=group), :]
                    at = (k * 2 + p) * windows
                    out_ref[b * chunks + c, at : at + windows, :] = slab.astype(jnp.bfloat16)


def whiten_packed(view, flags):
    bands, windows, parts, group, _ = view.shape
    chans = flags.shape[0]
    tiles = bands * group // chans
    hbm = pl.BlockSpec(memory_space=pltpu.HBM)
    return pl.pallas_call(
        functools.partial(whiten_kernel, chans=chans),
        out_shape=jax.ShapeDtypeStruct((tiles, chans * parts * windows, LANES), jnp.bfloat16),
        in_specs=[hbm, hbm],
        out_specs=pl.BlockSpec(memory_space=pltpu.VMEM),
        scratch_shapes=[
            pltpu.SMEM(flags.shape, jnp.int32),
            pltpu.VMEM(view.shape, jnp.bfloat16),
            pltpu.VMEM((bands * parts * windows * group, LANES), jnp.float32),
            pltpu.SemaphoreType.DMA((bands * windows // 16 + 1,)),
        ],
        compiler_params=pltpu.CompilerParams(vmem_limit_bytes=VMEM_FIRST),
        cost_estimate=pl.CostEstimate(flops=10**9, bytes_accessed=2**20, transcendentals=0),
        name="whiten",
    )(flags, view)


def spread_second(second_ref, values, windows, chans):
    for k in range(chans):
        row = k * 2 * windows
        re = values[row : row + windows].astype(jnp.float32)
        im = values[row + windows : row + 2 * windows].astype(jnp.float32)
        second_ref[k, 0] = re
        second_ref[k, 1] = im - re
        second_ref[k, 2] = re + im


def spread_first(first_ref, row_at, values, windows, chans):
    for k in range(chans):
        row = k * 2 * windows
        re = values[row : row + windows].astype(jnp.float32)
        im = values[row + windows : row + 2 * windows].astype(jnp.float32)
        slot = pl.ds(row_at * chans + k, windows, stride=SUB)
        first_ref[0, slot, :] = re + im
        first_ref[1, slot, :] = im
        first_ref[2, slot, :] = re


def pair_sums(work, windows):
    zero = jnp.zeros((SUB, LANES), jnp.float32)

    def body(w, sums):
        base = pl.multiple_of(w * SUB, SUB)
        loaded = {}

        def load(ref, at):
            if id(ref) not in loaded:
                loaded[id(ref)] = [ref[q, at, :] for q in range(3)]
            return loaded[id(ref)]

        out = []
        for (first_ref, second_ref), (s1, s2, s3) in zip(work, sums):
            f = load(first_ref, pl.ds(base, SUB))
            g = load(second_ref, pl.ds(w, 1))
            out.append((s1 + g[0] * f[0], s2 + g[1] * f[1], s3 + g[2] * f[2]))
        return tuple(out)

    sums = lax.fori_loop(0, windows, body, ((zero, zero, zero),) * len(work), unroll=8)
    return [(s1 + s2, s1 - s3) for s1, s2, s3 in sums]


def far_sums(first_ref, values_ref, second_ref, put, rows, chans, windows):
    low = lax.broadcasted_iota(jnp.int32, (SUB, LANES), 0) < SUB // 2
    for t in range(TILES):
        firsts = [first_ref.at[block, t] for block in range(2)]
        seconds = {}
        for r in range(2, rows):
            spread_second(second_ref.at[t, r], values_ref[r * TILES + t], windows, chans)
            seconds[r] = [second_ref.at[t, r, k] for k in range(chans)]
        mid = range(2, rows - 2)
        sums = pair_sums([(firsts[0], g) for r in mid for g in seconds[r]], windows)
        for n, r in enumerate(mid):
            for q in range(2):
                vals = jnp.concatenate([sums[n * chans + k][q] for k in range(chans)])
                put(r, t, q * chans * SUB, vals)
        last = range(rows - 2, rows)
        sums = pair_sums([(f, g) for r in last for g in seconds[r] for f in firsts], windows)
        for n, r in enumerate(last):
            mine = sums[n * 2 * chans : (n + 1) * 2 * chans]
            rest = []
            for q in range(2):
                vals = jnp.concatenate([mine[k * 2][q] for k in range(chans)])
                put(r, t, q * chans * SUB, vals)
                rest.append(jnp.where(low, mine[1][q], pltpu.roll(mine[3][q], SUB // 2, 0)))
            put(r, t, 2 * chans * SUB, jnp.concatenate(rest))


def far_own_kernel(got_ref, first_ref, out_ref, second_ref, *, rows, chans, windows):
    for t in range(TILES):
        for r in range(rows - 2):
            spread_first(
                first_ref.at[r * chans // SUB, t],
                r % (SUB // chans),
                got_ref[r * TILES + t],
                windows,
                chans,
            )

    def put(r, t, at, vals):
        out_ref[r * TILES + t, at : at + 2 * SUB, :] = vals.astype(jnp.bfloat16)

    far_sums(first_ref, got_ref, second_ref, put, rows, chans, windows)


def far_other_kernel(other_ref, first_ref, own_ref, out_ref, second_ref, *, rows, chans, windows):
    size = own_ref.shape[1]
    out_ref[: 2 * TILES] = jnp.zeros((2 * TILES, *out_ref.shape[1:]), out_ref.dtype)
    mid = pl.ds(2 * TILES, (rows - 4) * TILES)
    rest = jnp.zeros(((rows - 4) * TILES, 2 * SUB, LANES), out_ref.dtype)
    out_ref[2 * TILES :, :size, :] = own_ref[2 * TILES :]
    for s in range(2):
        out_ref[mid, s * size + 4 * SUB : s * size + 6 * SUB, :] = rest

    def put(r, t, at, vals):
        at += size
        out_ref[r * TILES + t, at : at + 2 * SUB, :] = vals.astype(jnp.bfloat16)

    far_sums(first_ref, other_ref, second_ref, put, rows, chans, windows)


def far_packed(got, swap, rows, chans, windows):
    vmem = pl.BlockSpec(memory_space=pltpu.VMEM)
    params = dict(
        scratch_shapes=[pltpu.VMEM((TILES, rows, chans, 3, windows, LANES), jnp.float32)],
        compiler_params=pltpu.CompilerParams(vmem_limit_bytes=32 * 2**20),
        cost_estimate=pl.CostEstimate(flops=10**9, bytes_accessed=2**20, transcendentals=0),
    )
    size = 3 * chans * SUB
    sizes = dict(rows=rows, chans=chans, windows=windows)
    first, own = pl.pallas_call(
        functools.partial(far_own_kernel, **sizes),
        out_shape=[
            jax.ShapeDtypeStruct((2, TILES, 3, windows * SUB, LANES), jnp.float32),
            jax.ShapeDtypeStruct((rows * TILES, size, LANES), jnp.bfloat16),
        ],
        in_specs=[vmem],
        out_specs=[vmem] * 2,
        name="far_own",
        **params,
    )(got)
    return pl.pallas_call(
        functools.partial(far_other_kernel, **sizes),
        out_shape=jax.ShapeDtypeStruct((rows * TILES, 2 * size, LANES), jnp.bfloat16),
        in_specs=[vmem] * 3,
        out_specs=vmem,
        name="far_other",
        **params,
    )(swap(got), first, own)


def halves_kernel(own_ref, keep_ref, give_ref):
    odd = lax.axis_index("row") % 2
    tiles = keep_ref.shape[0]
    keep_ref[...] = own_ref[pl.ds(odd * tiles, tiles)]
    give_ref[...] = own_ref[pl.ds((1 - odd) * tiles, tiles)]


def halves_packed(own):
    vmem = pl.BlockSpec(memory_space=pltpu.VMEM)
    band = jax.ShapeDtypeStruct((own.shape[0] // 2, *own.shape[1:]), own.dtype)
    return pl.pallas_call(
        halves_kernel,
        out_shape=[band] * 2,
        in_specs=[vmem],
        out_specs=[vmem] * 2,
        compiler_params=pltpu.CompilerParams(vmem_limit_bytes=32 * 2**20),
        cost_estimate=pl.CostEstimate(flops=10**9, bytes_accessed=2**20, transcendentals=0),
        name="halves",
    )(own)


def near_kernel(*refs, windows):
    sources, outs, (first_ref, second_ref) = refs[:4], refs[4:6], refs[6:]
    chans = 2
    odd = lax.axis_index("row") % 2
    low = lax.broadcasted_iota(jnp.int32, (SUB, LANES), 0) < SUB // 2
    tiles = outs[0].shape[0]

    def body(m, carry):
        for t in range(TILES):
            tile = m * TILES + t
            first = first_ref.at[t]
            work = []
            for n in range(2):
                own_ref, other_ref = sources[2 * n : 2 * n + 2]
                spread_first(first, odd if n == 0 else 1 - odd, own_ref[tile], windows, chans)
                for s, ref in enumerate((own_ref, other_ref)):
                    spread_second(second_ref.at[t, n, s], ref[tile], windows, chans)
                    work += [(first, second_ref.at[t, n, s, k]) for k in range(chans)]
            sums = pair_sums(work, windows)
            for n, out_ref in enumerate(outs):
                for s in range(2):
                    one, two = sums[(n * 2 + s) * chans : (n * 2 + s + 1) * chans]
                    vals = [
                        jnp.where(low, one[q], pltpu.roll(two[q], SUB // 2, 0)) for q in range(2)
                    ]
                    vals = jnp.concatenate(vals).astype(jnp.bfloat16)
                    out_ref[tile, s * 2 * SUB : (s + 1) * 2 * SUB, :] = vals
        return carry

    lax.fori_loop(0, tiles // TILES, body, 0)


def near_packed(keep, keep_other, took, took_other, windows):
    vmem = pl.BlockSpec(memory_space=pltpu.VMEM)
    piece = jax.ShapeDtypeStruct((keep.shape[0], 4 * SUB, LANES), jnp.bfloat16)
    return pl.pallas_call(
        functools.partial(near_kernel, windows=windows),
        out_shape=[piece] * 2,
        in_specs=[vmem] * 4,
        out_specs=[vmem] * 2,
        scratch_shapes=[
            pltpu.VMEM((TILES, 3, windows * SUB, LANES), jnp.float32),
            pltpu.VMEM((TILES, 2, 2, 2, 3, windows, LANES), jnp.float32),
        ],
        compiler_params=pltpu.CompilerParams(vmem_limit_bytes=32 * 2**20),
        cost_estimate=pl.CostEstimate(flops=10**9, bytes_accessed=2**20, transcendentals=0),
        name="near",
    )(keep, keep_other, took, took_other)


def finish_kernel(far_ref, kept_ref, taken_ref, out_ref, wide_ref, near_ref, *, rows, chans):
    level, odd = lax.axis_index("row") // 2, lax.axis_index("row") % 2
    col = lax.axis_index("col")
    per_row = 2 * chans
    firsts = rows * chans
    half = rows // 2
    size = 3 * chans * SUB
    for r in range(rows):
        for t in range(TILES):
            for s in range(2):
                side = col if s == 0 else 1 - col
                rest = far_ref[r * TILES + t, s * size + 4 * SUB : (s + 1) * size, :]
                rest = rest.astype(jnp.float32)
                for q in range(2):
                    spot = s * size + q * chans * SUB
                    vals = far_ref[r * TILES + t, spot : spot + chans * SUB, :]
                    vals = vals.astype(jnp.float32)
                    more = rest[q * SUB : (q + 1) * SUB]
                    for k in range(chans):
                        to = (q * SUB + t * per_row + side * chans + k) * firsts
                        to = pl.multiple_of(to, firsts)
                        wide_ref[r, pl.ds(to, SUB), :] = vals[k * SUB : (k + 1) * SUB]
                        tail = more if k == 0 else pltpu.roll(more, SUB // 2, 0)
                        wide_ref[r, pl.ds(to + SUB, SUB), :] = tail
    for r in range(rows):
        for q in range(2):
            for i in range(firsts):
                if i < firsts - per_row:
                    vals = wide_ref[r, pl.ds(q * SUB * firsts + i, SUB, stride=firsts), :]
                    keep = jnp.full((SUB, LANES), level, jnp.int32) > i // per_row
                    vals = jnp.where(keep, vals, 0.0)
                else:
                    vals = jnp.zeros((SUB, LANES), jnp.float32)
                out_ref[r // half, q, i, r % half] = vals
    second = odd * per_row + lax.broadcasted_iota(jnp.int32, (SUB, LANES), 0) % per_row
    for n, ref in enumerate((kept_ref, taken_ref)):
        for m in range(half):
            for t in range(TILES):
                for s in range(2):
                    side = col if s == 0 else 1 - col
                    vals = ref[m * TILES + t, s * 2 * SUB : (s + 1) * 2 * SUB, :]
                    vals = vals.astype(jnp.float32)
                    for q in range(2):
                        for k in range(chans):
                            to = (q * SUB + t * per_row + side * chans + k) * SUB
                            part = vals[q * SUB : (q + 1) * SUB]
                            part = part if k == 0 else pltpu.roll(part, SUB // 2, 0)
                            near_ref[n, m, pl.ds(pl.multiple_of(to, SUB), SUB), :] = part
    for n in range(2):
        band = odd if n == 0 else 1 - odd
        for m in range(half):
            for q in range(2):
                for i in range(per_row):
                    first = i // chans * per_row + col * chans + i % chans
                    vals = near_ref[n, m, pl.ds(q * SUB * SUB + i, SUB, stride=SUB), :]
                    out_ref[band, q, level * per_row + i, m] = jnp.where(first <= second, vals, 0.0)


def finish_packed(far, kept, taken, rows, chans):
    vmem = pl.BlockSpec(memory_space=pltpu.VMEM)
    firsts = rows * chans
    return pl.pallas_call(
        functools.partial(finish_kernel, rows=rows, chans=chans),
        out_shape=jax.ShapeDtypeStruct((2, 2, firsts, rows // 2, SUB, LANES), jnp.float32),
        in_specs=[vmem] * 3,
        out_specs=vmem,
        scratch_shapes=[
            pltpu.VMEM((rows, 2 * SUB * firsts, LANES), jnp.float32),
            pltpu.VMEM((2, rows // 2, 2 * SUB * SUB, LANES), jnp.float32),
        ],
        compiler_params=pltpu.CompilerParams(vmem_limit_bytes=32 * 2**20),
        cost_estimate=pl.CostEstimate(flops=10**9, bytes_accessed=2**20, transcendentals=0),
        name="finish",
    )(far, kept, taken)


def on_device_packed(spectra, window_flags):
    bands, windows, parts, chans, bins = spectra.shape
    rows, cols = lax.axis_size("row"), lax.axis_size("col")
    chunks = bins // LANES
    view = spectra.reshape(bands, windows, parts, chans, chunks, LANES)
    view = view.transpose(0, 1, 2, 4, 3, 5).reshape(bands, windows, parts, chunks * chans, LANES)

    def swap(value):
        return lax.ppermute(value, "col", [(0, 1), (1, 0)])

    own = whiten_packed(view, window_flags.T)
    got = lax.all_to_all(own, "row", 0, 0, tiled=True)

    def level_swap(value):
        return lax.ppermute(value, "row", [(r, r ^ 1) for r in range(rows)])

    keep, give = halves_packed(own)
    took = level_swap(give)
    got, took = lax.optimization_barrier((got, took))
    far = far_packed(got, swap, rows, chans, windows)
    far = lax.all_to_all(far, "row", 0, 0, tiled=True)
    kept, give = near_packed(keep, swap(keep), took, swap(took), windows)
    out = finish_packed(far, kept, level_swap(give), rows, chans)
    out = out.reshape(bands, 2, rows * chans, chunks, cols * chans, LANES)
    out = out.transpose(0, 1, 2, 4, 3, 5)
    return out.reshape(bands, 2, 1, rows * chans, cols * chans, bins)


def on_device(spectra, window_flags):
    bands, windows, _, chans, bins = spectra.shape
    rows, cols = lax.axis_size("row"), lax.axis_size("col")
    if (
        bands == 2
        and rows == 8
        and bands * bins == rows * TILES * LANES
        and cols == 2
        and chans == 2
        and windows % 16 == 0
        and bins == rows * LANES
    ):
        return on_device_packed(spectra, window_flags)
    payload = whiten_plain(spectra, window_flags, rows * cols)
    got = lax.all_to_all(payload, ("row", "col"), 0, 0, tiled=True)
    result = cross_plain(got, rows, cols, chans, windows)
    back = lax.all_to_all(result, ("row", "col"), 0, 0, tiled=True)
    return finish_plain(back, bands, bins, rows, cols, chans)


def solution(mesh):
    in_specs = (P("parts", None, None, ("row", "col"), None), P("parts", ("row", "col")))
    out_specs = P("parts", None, "col", None, "row", None)
    return jax.shard_map(
        on_device, mesh=mesh, in_specs=in_specs, out_specs=out_specs, check_vma=False
    )
```

time: 215 us -> 46.7 us (0.22)
  matrix products: 53.1 us -> 0 us
  other arithmetic: 49 us -> 0 us
  local copies, waits for them, and re-layouts: 40.1 us -> 1.07 us
  waiting for transfers between devices: 53.7 us -> 18.5 us
  starting transfers between devices: 0.04 us -> 16 us
  between operations: 13.5 us -> 0.04 us
  Pallas kernels: 0 us -> 10.8 us
  blocking collectives: 4.82 us -> 0 us
    dot_general x2 -> x0, matrix products: 53.1 us -> none  [on_device(): jnp.einsum('wpif,wqjf->pqijf', first_rows[0], second_rows[0], preferred_e...]
    all_gather x2 -> x0, waiting for transfers between devices: 53 us -> none  [on_device(): lax.all_gather(payload[band_index:band_index + 1], 'row', axis=3, tiled=T...]
    another operation x4 -> x0, other arithmetic: 36.7 us -> none
    all_gather x4 -> x0, local copies, waits for them, and re-layouts: 29 us -> none  [the longest x2 25 us: on_device(): lax.all_gather(payload[band_index:band_index + 1], 'row', axis=3, tiled=T...]
    ppermute x0 -> x5, waiting for transfers between devices: none -> 15.7 us  [the longest x2 13.8 us: level_swap(): return lax.ppermute(value, 'row', [(r, r ^ 1) for r in range(rows)])]
    all_to_all x0 -> x2, starting transfers between devices: none -> 11.3 us  [the longest x1 7.3 us: on_device_packed(): got = lax.all_to_all(own, 'row', 0, 0, tiled=True)]
    pallas_call x0 -> x6, Pallas kernels: none -> 10.8 us  [the longest x1 3.31 us: whiten_packed(): pl.pallas_call(functools.partial(whiten_kernel, chans=chans), out_shape=j...]
    mul x2 -> x0, other arithmetic: 10.7 us -> none  [the longest x1 9.47 us: combine_parts(): return jnp.stack([real_part * keep, imag_part * keep], axis=-4)]
  transfers between devices with their start and end apart: 2 -> 7, of which waited for: 2 -> 7; matrix products, arithmetic and copies ran while one was open for 20% -> 0% of each run, Pallas kernels for 0% -> 9%
where the time goes in v3:
time: 46.7 us; the launch traced here: 46.4 us
  waiting for transfers between devices  18.5 us (40%)
  starting transfers between devices  16 us (34%)
  Pallas kernels  10.8 us (23%)
  local copies, waits for them, and re-layouts  1.07 us (2%)
    ppermute x2, waiting for transfers between devices, level_swap(): return lax.ppermute(value, 'row', [(r, r ^ 1) for r in range(rows)])  13.8 us
    all_to_all x1, starting transfers between devices, on_device_packed(): got = lax.all_to_all(own, 'row', 0, 0, tiled=True)  7.3 us
    ppermute x2, starting transfers between devices, level_swap(): return lax.ppermute(value, 'row', [(r, r ^ 1) for r in range(rows)])  4.17 us
    all_to_all x1, starting transfers between devices, on_device_packed(): far = lax.all_to_all(far, 'row', 0, 0, tiled=True)  4 us
    pallas_call x1, Pallas kernels, whiten_packed(): pl.pallas_call(functools.partial(whiten_kernel, chans=chans), out_shape=j...  3.31 us
    pallas_call x1, Pallas kernels, near_packed(): pl.pallas_call(functools.partial(near_kernel, windows=windows), out_shape...  2.66 us
    all_to_all x1, waiting for transfers between devices, on_device_packed(): far = lax.all_to_all(far, 'row', 0, 0, tiled=True)  2.17 us
    pallas_call x1, Pallas kernels, far_packed(): pl.pallas_call(functools.partial(far_other_kernel, **sizes), out_shape=ja...  1.94 us
  transfers between devices with their start and end apart: 7, of which 7 were waited for; matrix products, arithmetic and copies ran while one was open for 0% of the time, Pallas kernels for 9%

profile of v3, /device:TPU:0, one launch (start us, length us, event | category | flops | bytes accessed | tf_op | source)
XLA Modules:
  0.0 46.4 jit_solution(9934567463938589049)
XLA Ops:
  0.0 3.3 %whiten.1.own_ref = bf16[16,128,128]{2,1,0:T(8,128)(2,1)} custom-call(s32[2,32]{1,0:T(2,128)} %bitcast.12, bf16[2,32,2,16,128]{4,3,2,1,0:T(8,128)(2,1)} %bitcast.11), custom_call_target="tpu_custom_call" | custom-call | flops 1000000000 | bytes 1048576 | tf_op jit(solution)/shard_map/whiten/pallas_call | solution.py:140
  3.3 7.3 %all-to-all-start = ((bf16[16,128,128]{2,1,0:T(8,128)(2,1)}), bf16[16,128,128]{2,1,0:T(8,128)(2,1)S(1)}, u32[]{:S(2)}, u32[]{:S(2)}) async-start(bf16[16,128,128]{2,1,0:T(8,128)(2,1)} %whiten.1.own_ref), calls=%async_computation | async-start | bytes 1048576 | tf_op jit(solution)/shard_map/all_to_all | solution.py:448
  10.6 0.0 copy-start
  10.6 1.1 %copy-done = bf16[16,128,128]{2,1,0:T(8,128)(2,1)S(1)} copy-done((bf16[16,128,128]{2,1,0:T(8,128)(2,1)S(1)}, bf16[16,128,128]{2,1,0:T(8,128)(2,1)}, u32[]{:S(2)}) %copy-start) | copy-done | bytes 524312
  11.7 2.1 %collective-permute-start = (bf16[8,128,128]{2,1,0:T(8,128)(2,1)S(1)}, bf16[8,128,128]{2,1,0:T(8,128)(2,1)S(1)}, u32[]{:S(2)}, u32[]{:S(2)}) collective-permute-start(bf16[8,128,128]{2,1,0:T(8,128)(2,1)S(1)} %get-tuple-element.13), channel_id=1, source_target_pairs={{0,2},{2,0},{4,6},{6,4},{8,10},{10,8},{12,14},{14,12},{1,3},{3,1},... | collective-permute-start | bytes 786440 | tf_op jit(solution)/shard_map/ppermute | solution.py:451
  13.8 10.7 %collective-permute-done.refs_2_ = bf16[8,128,128]{2,1,0:T(8,128)(2,1)S(1)} collective-permute-done((bf16[8,128,128]{2,1,0:T(8,128)(2,1)S(1)}, bf16[8,128,128]{2,1,0:T(8,128)(2,1)S(1)}, u32[]{:S(2)}, u32[]{:S(2)}) %collective-permute-start) | collective-permute-done | bytes 262176 | tf_op jit(solution)/shard_map/ppermute | solution.py:451
  24.5 0.6 %all-to-all-done.got_ref = bf16[16,128,128]{2,1,0:T(8,128)(2,1)S(1)} async-done(((bf16[16,128,128]{2,1,0:T(8,128)(2,1)}), bf16[16,128,128]{2,1,0:T(8,128)(2,1)S(1)}, u32[]{:S(2)}, u32[]{:S(2)}) %all-to-all-start) | async-done | bytes 524320 | tf_op jit(solution)/shard_map/all_to_all | solution.py:448
  25.1 0.0 collective-permute-start.1
  25.1 1.4 %far_own.1 = (f32[2,2,3,256,128]{4,3,2,1,0:T(8,128)S(1)}, bf16[16,48,128]{2,1,0:T(8,128)(2,1)S(1)}) custom-call(bf16[16,128,128]{2,1,0:T(8,128)(2,1)S(1)} %all-to-all-done.got_ref), custom_call_target="tpu_custom_call" | custom-call | flops 1000000000 | bytes 1048576 | tf_op jit(solution)/shard_map/far_own/pallas_call | solution.py:269
  26.5 0.5 %collective-permute-done.1.other_ref = bf16[16,128,128]{2,1,0:T(8,128)(2,1)S(1)} collective-permute-done((bf16[16,128,128]{2,1,0:T(8,128)(2,1)S(1)}, bf16[16,128,128]{2,1,0:T(8,128)(2,1)S(1)}, u32[]{:S(2)}, u32[]{:S(2)}) %collective-permute-start.1) | collective-permute-done | bytes 524320 | tf_op jit(solution)/shard_map/ppermute | solution.py:445
  27.0 1.9 %far_other.1 = bf16[16,96,128]{2,1,0:T(8,128)(2,1)} custom-call(bf16[16,128,128]{2,1,0:T(8,128)(2,1)S(1)} %collective-permute-done.1.other_ref, f32[2,2,3,256,128]{4,3,2,1,0:T(8,128)S(1)} %get-tuple-element.15.first_ref, bf16[16,48,128]{2,1,0:T(8,128)(2,1)S(1)} %get-tuple-element.16.own_ref), custom_call_target="tpu_custom_call" | custom-call | flops 1000000000 | bytes 1048576 | tf_op jit(solution)/shard_map/far_other/pallas_call | solution.py:280
  29.0 4.0 %all-to-all-start.1 = ((bf16[16,96,128]{2,1,0:T(8,128)(2,1)}), bf16[16,96,128]{2,1,0:T(8,128)(2,1)S(1)}, u32[]{:S(2)}, u32[]{:S(2)}) async-start(bf16[16,96,128]{2,1,0:T(8,128)(2,1)} %far_other.1), calls=%async_computation.1 | async-start | bytes 786432 | tf_op jit(solution)/shard_map/all_to_all | solution.py:457
  33.0 0.0 collective-permute-start.2
  33.0 0.5 %collective-permute-start.3 = (bf16[8,128,128]{2,1,0:T(8,128)(2,1)S(1)}, bf16[8,128,128]{2,1,0:T(8,128)(2,1)S(1)}, u32[]{:S(2)}, u32[]{:S(2)}) collective-permute-start(bf16[8,128,128]{2,1,0:T(8,128)(2,1)S(1)} %collective-permute-done.refs_2_), channel_id=1, source_target_pairs={{0,1},{1,0},{2,3},{3,2},{4,5},{5,4},{6,7},{7,6},{8,9},{9,8},{10,11... | collective-permute-start | bytes 786440 | tf_op jit(solution)/shard_map/ppermute | solution.py:445
  33.5 1.0 %collective-permute-done.2.refs_1_ = bf16[8,128,128]{2,1,0:T(8,128)(2,1)S(1)} collective-permute-done((bf16[8,128,128]{2,1,0:T(8,128)(2,1)S(1)}, bf16[8,128,128]{2,1,0:T(8,128)(2,1)S(1)}, u32[]{:S(2)}, u32[]{:S(2)}) %collective-permute-start.2) | collective-permute-done | bytes 262176 | tf_op jit(solution)/shard_map/ppermute | solution.py:445
  34.5 0.4 collective-permute-done.3.refs_3_
  34.9 2.7 %near.1 = (bf16[8,32,128]{2,1,0:T(8,128)(2,1)S(1)}, bf16[8,32,128]{2,1,0:T(8,128)(2,1)S(1)}) custom-call(bf16[8,128,128]{2,1,0:T(8,128)(2,1)S(1)} %get-tuple-element.17.refs_0_, bf16[8,128,128]{2,1,0:T(8,128)(2,1)S(1)} %collective-permute-done.2.refs_1_, bf16[8,128,128]{2,1,0:T(8,128)(2,1)S(1)} %collective-permute-done.refs_2_, ...), custom_call_target="tpu_custom_call" | custom-call | flops 1000000000 | bytes 1048576 | tf_op jit(solution)/shard_map/near/pallas_call | solution.py:346
  37.5 2.1 %collective-permute-start.4 = (bf16[8,32,128]{2,1,0:T(8,128)(2,1)S(1)}, bf16[8,32,128]{2,1,0:T(8,128)(2,1)S(1)}, u32[]{:S(2)}, u32[]{:S(2)}) collective-permute-start(bf16[8,32,128]{2,1,0:T(8,128)(2,1)S(1)} %get-tuple-element.20), channel_id=1, source_target_pairs={{0,2},{2,0},{4,6},{6,4},{8,10},{10,8},{12,14},{14,12},{1,3},{3,1},... | collective-permute-start | bytes 196616 | tf_op jit(solution)/shard_map/ppermute | solution.py:451
  39.6 3.1 %collective-permute-done.4.taken_ref = bf16[8,32,128]{2,1,0:T(8,128)(2,1)S(1)} collective-permute-done((bf16[8,32,128]{2,1,0:T(8,128)(2,1)S(1)}, bf16[8,32,128]{2,1,0:T(8,128)(2,1)S(1)}, u32[]{:S(2)}, u32[]{:S(2)}) %collective-permute-start.4) | collective-permute-done | bytes 65568 | tf_op jit(solution)/shard_map/ppermute | solution.py:451
  42.8 2.2 %all-to-all-done.1.far_ref = bf16[16,96,128]{2,1,0:T(8,128)(2,1)S(1)} async-done(((bf16[16,96,128]{2,1,0:T(8,128)(2,1)}), bf16[16,96,128]{2,1,0:T(8,128)(2,1)S(1)}, u32[]{:S(2)}, u32[]{:S(2)}) %all-to-all-start.1) | async-done | bytes 393248 | tf_op jit(solution)/shard_map/all_to_all | solution.py:457
  44.9 1.4 %finish.1 = f32[2,2,16,4,8,128]{5,4,3,2,1,0:T(8,128)} custom-call(bf16[16,96,128]{2,1,0:T(8,128)(2,1)S(1)} %all-to-all-done.1.far_ref, bf16[8,32,128]{2,1,0:T(8,128)(2,1)S(1)} %get-tuple-element.19.kept_ref, bf16[8,32,128]{2,1,0:T(8,128)(2,1)S(1)} %collective-permute-done.4.taken_ref), custom_call_target="tpu_custom_call" | custom-call | flops 1000000000 | bytes 1048576 | tf_op jit(solution)/shard_map/finish/pallas_call | solution.py:422
  (1 shorter events, 0.0 us)
Async XLA Ops:
  3.3 21.8 %all-to-all-start = ((bf16[16,128,128]{2,1,0:T(8,128)(2,1)}), bf16[16,128,128]{2,1,0:T(8,128)(2,1)S(1)}, u32[]{:S(2)}, u32[]{:S(2)}) async-start(bf16[16,128,128]{2,1,0:T(8,128)(2,1)} %whiten.1.own_ref), calls=%async_computation | async-start | bytes 1048576 | tf_op jit(solution)/shard_map/all_to_all | solution.py:448
  10.6 1.1 %copy-start = (bf16[16,128,128]{2,1,0:T(8,128)(2,1)S(1)}, bf16[16,128,128]{2,1,0:T(8,128)(2,1)}, u32[]{:S(2)}) copy-start(bf16[16,128,128]{2,1,0:T(8,128)(2,1)} %whiten.1.own_ref) | copy-start | bytes 1572868
  11.7 12.7 %collective-permute-start = (bf16[8,128,128]{2,1,0:T(8,128)(2,1)S(1)}, bf16[8,128,128]{2,1,0:T(8,128)(2,1)S(1)}, u32[]{:S(2)}, u32[]{:S(2)}) collective-permute-start(bf16[8,128,128]{2,1,0:T(8,128)(2,1)S(1)} %get-tuple-element.13), channel_id=1, source_target_pairs={{0,2},{2,0},{4,6},{6,4},{8,10},{10,8},{12,14},{14,12},{1,3},{3,1},... | collective-permute-start | bytes 786440 | tf_op jit(solution)/shard_map/ppermute | solution.py:451
  25.1 1.9 %collective-permute-start.1 = (bf16[16,128,128]{2,1,0:T(8,128)(2,1)S(1)}, bf16[16,128,128]{2,1,0:T(8,128)(2,1)S(1)}, u32[]{:S(2)}, u32[]{:S(2)}) collective-permute-start(bf16[16,128,128]{2,1,0:T(8,128)(2,1)S(1)} %all-to-all-done.got_ref), channel_id=1, source_target_pairs={{0,1},{1,0},{2,3},{3,2},{4,5},{5,4},{6,7},{7,6},{8,9},{9,8},{10,11... | collective-permute-start | bytes 1572872 | tf_op jit(solution)/shard_map/ppermute | solution.py:445
  29.0 16.0 %all-to-all-start.1 = ((bf16[16,96,128]{2,1,0:T(8,128)(2,1)}), bf16[16,96,128]{2,1,0:T(8,128)(2,1)S(1)}, u32[]{:S(2)}, u32[]{:S(2)}) async-start(bf16[16,96,128]{2,1,0:T(8,128)(2,1)} %far_other.1), calls=%async_computation.1 | async-start | bytes 786432 | tf_op jit(solution)/shard_map/all_to_all | solution.py:457
  33.0 1.5 %collective-permute-start.2 = (bf16[8,128,128]{2,1,0:T(8,128)(2,1)S(1)}, bf16[8,128,128]{2,1,0:T(8,128)(2,1)S(1)}, u32[]{:S(2)}, u32[]{:S(2)}) collective-permute-start(bf16[8,128,128]{2,1,0:T(8,128)(2,1)S(1)} %get-tuple-element.17.refs_0_), channel_id=1, source_target_pairs={{0,1},{1,0},{2,3},{3,2},{4,5},{5,4},{6,7},{7,6},{8,9},{9,8},{10,11... | collective-permute-start | bytes 786440 | tf_op jit(solution)/shard_map/ppermute | solution.py:445
  33.0 1.9 %collective-permute-start.3 = (bf16[8,128,128]{2,1,0:T(8,128)(2,1)S(1)}, bf16[8,128,128]{2,1,0:T(8,128)(2,1)S(1)}, u32[]{:S(2)}, u32[]{:S(2)}) collective-permute-start(bf16[8,128,128]{2,1,0:T(8,128)(2,1)S(1)} %collective-permute-done.refs_2_), channel_id=1, source_target_pairs={{0,1},{1,0},{2,3},{3,2},{4,5},{5,4},{6,7},{7,6},{8,9},{9,8},{10,11... | collective-permute-start | bytes 786440 | tf_op jit(solution)/shard_map/ppermute | solution.py:445
  37.5 5.2 %collective-permute-start.4 = (bf16[8,32,128]{2,1,0:T(8,128)(2,1)S(1)}, bf16[8,32,128]{2,1,0:T(8,128)(2,1)S(1)}, u32[]{:S(2)}, u32[]{:S(2)}) collective-permute-start(bf16[8,32,128]{2,1,0:T(8,128)(2,1)S(1)} %get-tuple-element.20), channel_id=1, source_target_pairs={{0,2},{2,0},{4,6},{6,4},{8,10},{10,8},{12,14},{14,12},{1,3},{3,1},... | collective-permute-start | bytes 196616 | tf_op jit(solution)/shard_map/ppermute | solution.py:451

commit v4 on v3

--- a/solution.py
+++ b/solution.py
@@ -68,7 +68,9 @@
 VMEM_FIRST = 65454080
 
 
-def whiten_kernel(flags_hbm, x_hbm, out_ref, flags_ref, x_ref, white_ref, sems, *, chans):
+def whiten_kernel(
+    flags_hbm, x_hbm, out_hbm, flags_ref, x_ref, white_ref, out_ref, sems, out_sems, *, chans
+):
     bands, windows, _, group, _ = x_ref.shape
     chunks = group // chans
     step = 16
@@ -130,6 +132,14 @@
                     slab = white_ref[pl.ds(start, windows, stride=group), :]
                     at = (k * 2 + p) * windows
                     out_ref[b * chunks + c, at : at + windows, :] = slab.astype(jnp.bfloat16)
+            if c % TILES == TILES - 1:
+                n = (b * chunks + c) // TILES
+                part = pl.ds(n * TILES, TILES)
+                copy = pltpu.make_async_copy(out_ref.at[part], out_hbm.at[part], out_sems.at[n])
+                copy.start()
+                copies.append(copy)
+    for copy in copies[1 + bands * steps :]:
+        copy.wait()
 
 
 def whiten_packed(view, flags):
@@ -137,16 +147,19 @@
     chans = flags.shape[0]
     tiles = bands * group // chans
     hbm = pl.BlockSpec(memory_space=pltpu.HBM)
+    shape = (tiles, chans * parts * windows, LANES)
     return pl.pallas_call(
         functools.partial(whiten_kernel, chans=chans),
-        out_shape=jax.ShapeDtypeStruct((tiles, chans * parts * windows, LANES), jnp.bfloat16),
+        out_shape=jax.ShapeDtypeStruct(shape, jnp.bfloat16),
         in_specs=[hbm, hbm],
-        out_specs=pl.BlockSpec(memory_space=pltpu.VMEM),
+        out_specs=hbm,
         scratch_shapes=[
             pltpu.SMEM(flags.shape, jnp.int32),
             pltpu.VMEM(view.shape, jnp.bfloat16),
             pltpu.VMEM((bands * parts * windows * group, LANES), jnp.float32),
+            pltpu.VMEM(shape, jnp.bfloat16),
             pltpu.SemaphoreType.DMA((bands * windows // 16 + 1,)),
+            pltpu.SemaphoreType.DMA((tiles // TILES,)),
         ],
         compiler_params=pltpu.CompilerParams(vmem_limit_bytes=VMEM_FIRST),
         cost_estimate=pl.CostEstimate(flops=10**9, bytes_accessed=2**20, transcendentals=0),
@@ -198,7 +211,7 @@
     return [(s1 + s2, s1 - s3) for s1, s2, s3 in sums]
 
 
-def far_sums(first_ref, values_ref, second_ref, put, rows, chans, windows):
+def far_sums(first_ref, values_ref, second_ref, put, rows, chans, windows, done=None):
     low = lax.broadcasted_iota(jnp.int32, (SUB, LANES), 0) < SUB // 2
     for t in range(TILES):
         firsts = [first_ref.at[block, t] for block in range(2)]
@@ -222,6 +235,8 @@
                 put(r, t, q * chans * SUB, vals)
                 rest.append(jnp.where(low, mine[1][q], pltpu.roll(mine[3][q], SUB // 2, 0)))
             put(r, t, 2 * chans * SUB, jnp.concatenate(rest))
+        if done is not None:
+            done(t)
 
 
 def far_own_kernel(got_ref, first_ref, out_ref, second_ref, *, rows, chans, windows):
@@ -241,9 +256,20 @@
     far_sums(first_ref, got_ref, second_ref, put, rows, chans, windows)
 
 
-def far_other_kernel(other_ref, first_ref, own_ref, out_ref, second_ref, *, rows, chans, windows):
+def far_other_kernel(
+    other_ref, first_ref, own_ref, out_hbm, second_ref, out_ref, sems, *, rows, chans, windows
+):
     size = own_ref.shape[1]
+    copies = []
+
+    def send(first, count):
+        part = pl.ds(first, count)
+        sem = sems.at[len(copies)]
+        copies.append(pltpu.make_async_copy(out_ref.at[part], out_hbm.at[part], sem))
+        copies[-1].start()
+
     out_ref[: 2 * TILES] = jnp.zeros((2 * TILES, *out_ref.shape[1:]), out_ref.dtype)
+    send(0, 2 * TILES)
     mid = pl.ds(2 * TILES, (rows - 4) * TILES)
     rest = jnp.zeros(((rows - 4) * TILES, 2 * SUB, LANES), out_ref.dtype)
     out_ref[2 * TILES :, :size, :] = own_ref[2 * TILES :]
@@ -254,13 +280,19 @@
         at += size
         out_ref[r * TILES + t, at : at + 2 * SUB, :] = vals.astype(jnp.bfloat16)
 
-    far_sums(first_ref, other_ref, second_ref, put, rows, chans, windows)
+    def done(t):
+        for r in range(2, rows):
+            send(r * TILES + t, 1)
+
+    far_sums(first_ref, other_ref, second_ref, put, rows, chans, windows, done)
+    for copy in copies:
+        copy.wait()
 
 
 def far_packed(got, swap, rows, chans, windows):
     vmem = pl.BlockSpec(memory_space=pltpu.VMEM)
+    scratch = [pltpu.VMEM((TILES, rows, chans, 3, windows, LANES), jnp.float32)]
     params = dict(
-        scratch_shapes=[pltpu.VMEM((TILES, rows, chans, 3, windows, LANES), jnp.float32)],
         compiler_params=pltpu.CompilerParams(vmem_limit_bytes=32 * 2**20),
         cost_estimate=pl.CostEstimate(flops=10**9, bytes_accessed=2**20, transcendentals=0),
     )
@@ -274,6 +306,7 @@
         ],
         in_specs=[vmem],
         out_specs=[vmem] * 2,
+        scratch_shapes=scratch,
         name="far_own",
         **params,
     )(got)
@@ -281,7 +314,12 @@
         functools.partial(far_other_kernel, **sizes),
         out_shape=jax.ShapeDtypeStruct((rows * TILES, 2 * size, LANES), jnp.bfloat16),
         in_specs=[vmem] * 3,
-        out_specs=vmem,
+        out_specs=pl.BlockSpec(memory_space=pltpu.HBM),
+        scratch_shapes=scratch
+        + [
+            pltpu.VMEM((rows * TILES, 2 * size, LANES), jnp.bfloat16),
+            pltpu.SemaphoreType.DMA((1 + (rows - 2) * TILES,)),
+        ],
         name="far_other",
         **params,
     )(swap(got), first, own)
@@ -358,80 +396,144 @@
     )(keep, keep_other, took, took_other)
 
 
-def finish_kernel(far_ref, kept_ref, taken_ref, out_ref, wide_ref, near_ref, *, rows, chans):
+def near_out_kernel(kept_ref, taken_ref, out_hbm, wide_ref, out_ref, sems, *, chans):
     level, odd = lax.axis_index("row") // 2, lax.axis_index("row") % 2
     col = lax.axis_index("col")
     per_row = 2 * chans
-    firsts = rows * chans
-    half = rows // 2
-    size = 3 * chans * SUB
-    for r in range(rows):
-        for t in range(TILES):
-            for s in range(2):
-                side = col if s == 0 else 1 - col
-                rest = far_ref[r * TILES + t, s * size + 4 * SUB : (s + 1) * size, :]
-                rest = rest.astype(jnp.float32)
-                for q in range(2):
-                    spot = s * size + q * chans * SUB
-                    vals = far_ref[r * TILES + t, spot : spot + chans * SUB, :]
-                    vals = vals.astype(jnp.float32)
-                    more = rest[q * SUB : (q + 1) * SUB]
-                    for k in range(chans):
-                        to = (q * SUB + t * per_row + side * chans + k) * firsts
-                        to = pl.multiple_of(to, firsts)
-                        wide_ref[r, pl.ds(to, SUB), :] = vals[k * SUB : (k + 1) * SUB]
-                        tail = more if k == 0 else pltpu.roll(more, SUB // 2, 0)
-                        wide_ref[r, pl.ds(to + SUB, SUB), :] = tail
-    for r in range(rows):
-        for q in range(2):
-            for i in range(firsts):
-                if i < firsts - per_row:
-                    vals = wide_ref[r, pl.ds(q * SUB * firsts + i, SUB, stride=firsts), :]
-                    keep = jnp.full((SUB, LANES), level, jnp.int32) > i // per_row
-                    vals = jnp.where(keep, vals, 0.0)
-                else:
-                    vals = jnp.zeros((SUB, LANES), jnp.float32)
-                out_ref[r // half, q, i, r % half] = vals
+    bands, parts, _, quads, _, _ = out_ref.shape
     second = odd * per_row + lax.broadcasted_iota(jnp.int32, (SUB, LANES), 0) % per_row
     for n, ref in enumerate((kept_ref, taken_ref)):
-        for m in range(half):
+        for m in range(quads):
             for t in range(TILES):
                 for s in range(2):
                     side = col if s == 0 else 1 - col
                     vals = ref[m * TILES + t, s * 2 * SUB : (s + 1) * 2 * SUB, :]
                     vals = vals.astype(jnp.float32)
-                    for q in range(2):
+                    for q in range(parts):
                         for k in range(chans):
                             to = (q * SUB + t * per_row + side * chans + k) * SUB
                             part = vals[q * SUB : (q + 1) * SUB]
                             part = part if k == 0 else pltpu.roll(part, SUB // 2, 0)
-                            near_ref[n, m, pl.ds(pl.multiple_of(to, SUB), SUB), :] = part
-    for n in range(2):
-        band = odd if n == 0 else 1 - odd
-        for m in range(half):
-            for q in range(2):
+                            wide_ref[n, m, pl.ds(pl.multiple_of(to, SUB), SUB), :] = part
+    copies = []
+    for b in range(bands):
+        for q in range(parts):
+            out_ref[b, q] = jnp.zeros(out_ref.shape[2:], out_ref.dtype)
+            for m in range(quads):
                 for i in range(per_row):
                     first = i // chans * per_row + col * chans + i % chans
-                    vals = near_ref[n, m, pl.ds(q * SUB * SUB + i, SUB, stride=SUB), :]
-                    out_ref[band, q, level * per_row + i, m] = jnp.where(first <= second, vals, 0.0)
-
-
-def finish_packed(far, kept, taken, rows, chans):
+                    spot = pl.ds(q * SUB * SUB + i, SUB, stride=SUB)
+                    vals = wide_ref[b ^ odd, m, spot, :]
+                    out_ref[b, q, level * per_row + i, m] = jnp.where(first <= second, vals, 0.0)
+            sem = sems.at[b * parts + q]
+            copies.append(pltpu.make_async_copy(out_ref.at[b, q], out_hbm.at[b, q], sem))
+            copies[-1].start()
+    for copy in copies:
+        copy.wait()
+
+
+def near_out_packed(kept, taken, rows, chans):
     vmem = pl.BlockSpec(memory_space=pltpu.VMEM)
-    firsts = rows * chans
+    shape = (2, 2, rows * chans, rows // 2, SUB, LANES)
     return pl.pallas_call(
-        functools.partial(finish_kernel, rows=rows, chans=chans),
-        out_shape=jax.ShapeDtypeStruct((2, 2, firsts, rows // 2, SUB, LANES), jnp.float32),
-        in_specs=[vmem] * 3,
-        out_specs=vmem,
+        functools.partial(near_out_kernel, chans=chans),
+        out_shape=jax.ShapeDtypeStruct(shape, jnp.float32),
+        in_specs=[vmem] * 2,
+        out_specs=pl.BlockSpec(memory_space=pltpu.HBM),
         scratch_shapes=[
-            pltpu.VMEM((rows, 2 * SUB * firsts, LANES), jnp.float32),
             pltpu.VMEM((2, rows // 2, 2 * SUB * SUB, LANES), jnp.float32),
+            pltpu.VMEM(shape, jnp.float32),
+            pltpu.SemaphoreType.DMA((4,)),
         ],
         compiler_params=pltpu.CompilerParams(vmem_limit_bytes=32 * 2**20),
         cost_estimate=pl.CostEstimate(flops=10**9, bytes_accessed=2**20, transcendentals=0),
+        name="near_out",
+    )(kept, taken)
+
+
+def finish_kernel(far_ref, _, out_hbm, wide_ref, block_ref, sems, *, rows, chans):
+    level = lax.axis_index("row") // 2
+    col = lax.axis_index("col")
+    per_row = 2 * chans
+    half = rows // 2
+    size = 3 * chans * SUB
+    levels, bands, parts = block_ref.shape[:3]
+
+    def widen(piece, of_half, count):
+        for r in range(rows):
+            for t in range(TILES):
+                for s in range(2):
+                    side = col if s == 0 else 1 - col
+                    vals = far_ref[r * TILES + t, s * size + of_half : s * size + of_half + count, :]
+                    vals = vals.astype(jnp.float32)
+                    each = count // parts
+                    for q in range(parts):
+                        for k in range(chans):
+                            to = (q * SUB + t * per_row + side * chans + k) * SUB
+                            if each == SUB:
+                                part = vals[q * SUB : (q + 1) * SUB]
+                                part = part if k == 0 else pltpu.roll(part, SUB // 2, 0)
+                            else:
+                                part = vals[q * each + k * SUB : q * each + (k + 1) * SUB]
+                            wide_ref[piece, r, pl.ds(pl.multiple_of(to, SUB), SUB), :] = part
+
+    def copies(z):
+        firsts = pl.ds(z * per_row, per_row)
+        return [
+            pltpu.make_async_copy(
+                block_ref.at[z, b, q], out_hbm.at[b, q, firsts], sems.at[z, b * parts + q]
+            )
+            for b in range(bands)
+            for q in range(parts)
+        ]
+
+    def send(z):
+        piece, at = (z * per_row) // SUB, (z * per_row) % SUB
+        for r in range(rows):
+            for q in range(parts):
+                for i in range(per_row):
+                    spot = pl.ds(q * SUB * SUB + at + i, SUB, stride=SUB)
+                    block_ref[z, r // half, q, i, r % half] = wide_ref[piece, r, spot, :]
+        for copy in copies(z):
+            copy.start()
+
+    def wait(z):
+        for copy in copies(z):
+            copy.wait()
+
+    def first_level():
+        widen(0, 0, 2 * chans * SUB)
+        send(0)
+
+    def third_level():
+        widen(1, 2 * chans * SUB, chans * SUB)
+        send(2)
+
+    pl.when(level > 0)(first_level)
+    pl.when(level > 1)(lambda: send(1))
+    pl.when(level > 2)(third_level)
+    for z in range(levels):
+        pl.when(level > z)(functools.partial(wait, z))
+
+
+def finish_packed(far, out, rows, chans):
+    hbm = pl.BlockSpec(memory_space=pltpu.HBM)
+    levels, quads = rows // 2 - 1, out.shape[3]
+    return pl.pallas_call(
+        functools.partial(finish_kernel, rows=rows, chans=chans),
+        out_shape=jax.ShapeDtypeStruct(out.shape, out.dtype),
+        in_specs=[pl.BlockSpec(memory_space=pltpu.VMEM), hbm],
+        out_specs=hbm,
+        scratch_shapes=[
+            pltpu.VMEM((2, rows, 2 * SUB * SUB, LANES), jnp.float32),
+            pltpu.VMEM((levels, 2, 2, 2 * chans, quads, SUB, LANES), jnp.float32),
+            pltpu.SemaphoreType.DMA((levels, 4)),
+        ],
+        input_output_aliases={1: 0},
+        compiler_params=pltpu.CompilerParams(vmem_limit_bytes=32 * 2**20),
+        cost_estimate=pl.CostEstimate(flops=10**9, bytes_accessed=2**20, transcendentals=0),
         name="finish",
-    )(far, kept, taken)
+    )(far, out)
 
 
 def on_device_packed(spectra, window_flags):
@@ -452,11 +554,13 @@
 
     keep, give = halves_packed(own)
     took = level_swap(give)
-    got, took = lax.optimization_barrier((got, took))
+    keep_other = swap(keep)
+    got, took, keep_other = lax.optimization_barrier((got, took, keep_other))
     far = far_packed(got, swap, rows, chans, windows)
     far = lax.all_to_all(far, "row", 0, 0, tiled=True)
-    kept, give = near_packed(keep, swap(keep), took, swap(took), windows)
-    out = finish_packed(far, kept, level_swap(give), rows, chans)
+    kept, give = near_packed(keep, keep_other, took, swap(took), windows)
+    out = near_out_packed(kept, level_swap(give), rows, chans)
+    out = finish_packed(far, out, rows, chans)
     out = out.reshape(bands, 2, rows * chans, chunks, cols * chans, LANES)
     out = out.transpose(0, 1, 2, 4, 3, 5)
     return out.reshape(bands, 2, 1, rows * chans, cols * chans, bins)

time: 46.7 us -> 45.3 us (0.970)
  waiting for transfers between devices: 18.5 us -> 17.9 us
  starting transfers between devices: 16 us -> 15.5 us
    pallas_call x1, Pallas kernels: 1.42 us -> 0.11 us  [finish_packed(): pl.pallas_call(functools.partial(finish_kernel, rows=rows, chans=chans),...]
    pallas_call x0 -> x1, Pallas kernels: none -> 1.07 us  [near_out_packed(): pl.pallas_call(functools.partial(near_out_kernel, chans=chans), out_shape...]
    all_to_all x1, waiting for transfers between devices: 2.17 us -> 1.44 us  [on_device_packed(): far = lax.all_to_all(far, 'row', 0, 0, tiled=True)]
    ppermute x3, starting transfers between devices: 0.51 us -> 0.01 us  [swap(): return lax.ppermute(value, 'col', [(0, 1), (1, 0)])]
  transfers between devices with their start and end apart: 7 -> 7, of which waited for: 7 -> 6; matrix products, arithmetic and copies ran while one was open for 0% -> 0% of each run, Pallas kernels for 9% -> 12%
where the time goes in v4:
time: 45.3 us; the launch traced here: 45 us
  waiting for transfers between devices  17.9 us (40%)
  starting transfers between devices  15.5 us (34%)
  Pallas kernels  10.5 us (23%)
  local copies, waits for them, and re-layouts  1.07 us (2%)
    ppermute x2, waiting for transfers between devices, level_swap(): return lax.ppermute(value, 'row', [(r, r ^ 1) for r in range(rows)])  13.8 us
    all_to_all x1, starting transfers between devices, on_device_packed(): got = lax.all_to_all(own, 'row', 0, 0, tiled=True)  7.3 us
    ppermute x2, starting transfers between devices, level_swap(): return lax.ppermute(value, 'row', [(r, r ^ 1) for r in range(rows)])  4.17 us
    all_to_all x1, starting transfers between devices, on_device_packed(): far = lax.all_to_all(far, 'row', 0, 0, tiled=True)  4.01 us
    pallas_call x1, Pallas kernels, whiten_packed(): pl.pallas_call(functools.partial(whiten_kernel, chans=chans), out_shape=j...  3.19 us
    pallas_call x1, Pallas kernels, near_packed(): pl.pallas_call(functools.partial(near_kernel, windows=windows), out_shape...  2.66 us
    ppermute x3, waiting for transfers between devices, swap(): return lax.ppermute(value, 'col', [(0, 1), (1, 0)])  2.03 us
    pallas_call x1, Pallas kernels, far_packed(): pl.pallas_call(functools.partial(far_other_kernel, **sizes), out_shape=ja...  1.98 us
  transfers between devices with their start and end apart: 7, of which 6 were waited for; matrix products, arithmetic and copies ran while one was open for 0% of the time, Pallas kernels for 12%

profile of v4, /device:TPU:0, one launch (start us, length us, event | category | flops | bytes accessed | tf_op | source)
XLA Modules:
  0.0 45.0 jit_solution(17390907856088066214)
XLA Ops:
  0.0 3.2 %whiten.1.own_ref = bf16[16,128,128]{2,1,0:T(8,128)(2,1)} custom-call(s32[2,32]{1,0:T(2,128)} %bitcast.12, bf16[2,32,2,16,128]{4,3,2,1,0:T(8,128)(2,1)} %bitcast.11), custom_call_target="tpu_custom_call" | custom-call | flops 1000000000 | bytes 1048576 | tf_op jit(solution)/shard_map/whiten/pallas_call | solution.py:151
  3.2 7.3 %all-to-all-start = ((bf16[16,128,128]{2,1,0:T(8,128)(2,1)}), bf16[16,128,128]{2,1,0:T(8,128)(2,1)S(1)}, u32[]{:S(2)}, u32[]{:S(2)}) async-start(bf16[16,128,128]{2,1,0:T(8,128)(2,1)} %whiten.1.own_ref), calls=%async_computation | async-start | bytes 1048576 | tf_op jit(solution)/shard_map/all_to_all | solution.py:550
  10.5 0.0 copy-start
  10.5 1.1 %copy-done = bf16[16,128,128]{2,1,0:T(8,128)(2,1)S(1)} copy-done((bf16[16,128,128]{2,1,0:T(8,128)(2,1)S(1)}, bf16[16,128,128]{2,1,0:T(8,128)(2,1)}, u32[]{:S(2)}) %copy-start) | copy-done | bytes 524312
  11.6 2.1 %collective-permute-start = (bf16[8,128,128]{2,1,0:T(8,128)(2,1)S(1)}, bf16[8,128,128]{2,1,0:T(8,128)(2,1)S(1)}, u32[]{:S(2)}, u32[]{:S(2)}) collective-permute-start(bf16[8,128,128]{2,1,0:T(8,128)(2,1)S(1)} %get-tuple-element.14), channel_id=1, source_target_pairs={{0,2},{2,0},{4,6},{6,4},{8,10},{10,8},{12,14},{14,12},{1,3},{3,1},... | collective-permute-start | bytes 786440 | tf_op jit(solution)/shard_map/ppermute | solution.py:553
  13.7 0.0 collective-permute-start.1
  13.7 10.7 %collective-permute-done.refs_2_ = bf16[8,128,128]{2,1,0:T(8,128)(2,1)S(1)} collective-permute-done((bf16[8,128,128]{2,1,0:T(8,128)(2,1)S(1)}, bf16[8,128,128]{2,1,0:T(8,128)(2,1)S(1)}, u32[]{:S(2)}, u32[]{:S(2)}) %collective-permute-start) | collective-permute-done | bytes 262176 | tf_op jit(solution)/shard_map/ppermute | solution.py:553
  24.4 0.0 collective-permute-done.1.refs_1_
  24.4 0.6 %all-to-all-done.got_ref = bf16[16,128,128]{2,1,0:T(8,128)(2,1)S(1)} async-done(((bf16[16,128,128]{2,1,0:T(8,128)(2,1)}), bf16[16,128,128]{2,1,0:T(8,128)(2,1)S(1)}, u32[]{:S(2)}, u32[]{:S(2)}) %all-to-all-start) | async-done | bytes 524320 | tf_op jit(solution)/shard_map/all_to_all | solution.py:550
  25.0 0.0 collective-permute-start.2
  25.0 1.4 %far_own.1 = (f32[2,2,3,256,128]{4,3,2,1,0:T(8,128)S(1)}, bf16[16,48,128]{2,1,0:T(8,128)(2,1)S(1)}) custom-call(bf16[16,128,128]{2,1,0:T(8,128)(2,1)S(1)} %all-to-all-done.got_ref), custom_call_target="tpu_custom_call" | custom-call | flops 1000000000 | bytes 1048576 | tf_op jit(solution)/shard_map/far_own/pallas_call | solution.py:301
  26.4 0.5 %collective-permute-done.2.other_ref = bf16[16,128,128]{2,1,0:T(8,128)(2,1)S(1)} collective-permute-done((bf16[16,128,128]{2,1,0:T(8,128)(2,1)S(1)}, bf16[16,128,128]{2,1,0:T(8,128)(2,1)S(1)}, u32[]{:S(2)}, u32[]{:S(2)}) %collective-permute-start.2) | collective-permute-done | bytes 524320 | tf_op jit(solution)/shard_map/ppermute | solution.py:547
  26.9 2.0 %far_other.1 = bf16[16,96,128]{2,1,0:T(8,128)(2,1)} custom-call(bf16[16,128,128]{2,1,0:T(8,128)(2,1)S(1)} %collective-permute-done.2.other_ref, f32[2,2,3,256,128]{4,3,2,1,0:T(8,128)S(1)} %get-tuple-element.17.first_ref, bf16[16,48,128]{2,1,0:T(8,128)(2,1)S(1)} %get-tuple-element.18.own_ref), custom_call_target="tpu_custom_call" | custom-call | flops 1000000000 | bytes 1048576 | tf_op jit(solution)/shard_map/far_other/pallas_call | solution.py:313
  28.9 4.0 %all-to-all-start.1 = ((bf16[16,96,128]{2,1,0:T(8,128)(2,1)}), bf16[16,96,128]{2,1,0:T(8,128)(2,1)S(1)}, u32[]{:S(2)}, u32[]{:S(2)}) async-start(bf16[16,96,128]{2,1,0:T(8,128)(2,1)} %far_other.1), calls=%async_computation.1 | async-start | bytes 786432 | tf_op jit(solution)/shard_map/all_to_all | solution.py:560
  32.9 0.0 collective-permute-start.3
  32.9 1.5 %collective-permute-done.3.refs_3_ = bf16[8,128,128]{2,1,0:T(8,128)(2,1)S(1)} collective-permute-done((bf16[8,128,128]{2,1,0:T(8,128)(2,1)S(1)}, bf16[8,128,128]{2,1,0:T(8,128)(2,1)S(1)}, u32[]{:S(2)}, u32[]{:S(2)}) %collective-permute-start.3) | collective-permute-done | bytes 262176 | tf_op jit(solution)/shard_map/ppermute | solution.py:547
  34.4 2.7 %near.1 = (bf16[8,32,128]{2,1,0:T(8,128)(2,1)S(1)}, bf16[8,32,128]{2,1,0:T(8,128)(2,1)S(1)}) custom-call(bf16[8,128,128]{2,1,0:T(8,128)(2,1)S(1)} %get-tuple-element.15.refs_0_, bf16[8,128,128]{2,1,0:T(8,128)(2,1)S(1)} %collective-permute-done.1.refs_1_, bf16[8,128,128]{2,1,0:T(8,128)(2,1)S(1)} %collective-permute-done.refs_2_, ...), custom_call_target="tpu_custom_call" | custom-call | flops 1000000000 | bytes 1048576 | tf_op jit(solution)/shard_map/near/pallas_call | solution.py:384
  37.1 2.1 %collective-permute-start.4 = (bf16[8,32,128]{2,1,0:T(8,128)(2,1)S(1)}, bf16[8,32,128]{2,1,0:T(8,128)(2,1)S(1)}, u32[]{:S(2)}, u32[]{:S(2)}) collective-permute-start(bf16[8,32,128]{2,1,0:T(8,128)(2,1)S(1)} %get-tuple-element.22), channel_id=1, source_target_pairs={{0,2},{2,0},{4,6},{6,4},{8,10},{10,8},{12,14},{14,12},{1,3},{3,1},... | collective-permute-start | bytes 196616 | tf_op jit(solution)/shard_map/ppermute | solution.py:553
  39.2 3.2 %collective-permute-done.4.taken_ref = bf16[8,32,128]{2,1,0:T(8,128)(2,1)S(1)} collective-permute-done((bf16[8,32,128]{2,1,0:T(8,128)(2,1)S(1)}, bf16[8,32,128]{2,1,0:T(8,128)(2,1)S(1)}, u32[]{:S(2)}, u32[]{:S(2)}) %collective-permute-start.4) | collective-permute-done | bytes 65568 | tf_op jit(solution)/shard_map/ppermute | solution.py:553
  42.4 1.1 %near_out.1._ = f32[2,2,16,4,8,128]{5,4,3,2,1,0:T(8,128)} custom-call(bf16[8,32,128]{2,1,0:T(8,128)(2,1)S(1)} %get-tuple-element.21.kept_ref, bf16[8,32,128]{2,1,0:T(8,128)(2,1)S(1)} %collective-permute-done.4.taken_ref), custom_call_target="tpu_custom_call" | custom-call | flops 1000000000 | bytes 1048576 | tf_op jit(solution)/shard_map/near_out/pallas_call | solution.py:438
  43.4 1.4 %all-to-all-done.1.far_ref = bf16[16,96,128]{2,1,0:T(8,128)(2,1)S(1)} async-done(((bf16[16,96,128]{2,1,0:T(8,128)(2,1)}), bf16[16,96,128]{2,1,0:T(8,128)(2,1)S(1)}, u32[]{:S(2)}, u32[]{:S(2)}) %all-to-all-start.1) | async-done | bytes 393248 | tf_op jit(solution)/shard_map/all_to_all | solution.py:560
  44.9 0.1 finish.1
  (1 shorter events, 0.0 us)
Async XLA Ops:
  3.2 21.8 %all-to-all-start = ((bf16[16,128,128]{2,1,0:T(8,128)(2,1)}), bf16[16,128,128]{2,1,0:T(8,128)(2,1)S(1)}, u32[]{:S(2)}, u32[]{:S(2)}) async-start(bf16[16,128,128]{2,1,0:T(8,128)(2,1)} %whiten.1.own_ref), calls=%async_computation | async-start | bytes 1048576 | tf_op jit(solution)/shard_map/all_to_all | solution.py:550
  10.5 1.1 %copy-start = (bf16[16,128,128]{2,1,0:T(8,128)(2,1)S(1)}, bf16[16,128,128]{2,1,0:T(8,128)(2,1)}, u32[]{:S(2)}) copy-start(bf16[16,128,128]{2,1,0:T(8,128)(2,1)} %whiten.1.own_ref) | copy-start | bytes 1572868
  11.6 12.7 %collective-permute-start = (bf16[8,128,128]{2,1,0:T(8,128)(2,1)S(1)}, bf16[8,128,128]{2,1,0:T(8,128)(2,1)S(1)}, u32[]{:S(2)}, u32[]{:S(2)}) collective-permute-start(bf16[8,128,128]{2,1,0:T(8,128)(2,1)S(1)} %get-tuple-element.14), channel_id=1, source_target_pairs={{0,2},{2,0},{4,6},{6,4},{8,10},{10,8},{12,14},{14,12},{1,3},{3,1},... | collective-permute-start | bytes 786440 | tf_op jit(solution)/shard_map/ppermute | solution.py:553
  13.7 10.7 %collective-permute-start.1 = (bf16[8,128,128]{2,1,0:T(8,128)(2,1)S(1)}, bf16[8,128,128]{2,1,0:T(8,128)(2,1)S(1)}, u32[]{:S(2)}, u32[]{:S(2)}) collective-permute-start(bf16[8,128,128]{2,1,0:T(8,128)(2,1)S(1)} %get-tuple-element.15.refs_0_), channel_id=1, source_target_pairs={{0,1},{1,0},{2,3},{3,2},{4,5},{5,4},{6,7},{7,6},{8,9},{9,8},{10,11... | collective-permute-start | bytes 786440 | tf_op jit(solution)/shard_map/ppermute | solution.py:547
  25.0 1.9 %collective-permute-start.2 = (bf16[16,128,128]{2,1,0:T(8,128)(2,1)S(1)}, bf16[16,128,128]{2,1,0:T(8,128)(2,1)S(1)}, u32[]{:S(2)}, u32[]{:S(2)}) collective-permute-start(bf16[16,128,128]{2,1,0:T(8,128)(2,1)S(1)} %all-to-all-done.got_ref), channel_id=1, source_target_pairs={{0,1},{1,0},{2,3},{3,2},{4,5},{5,4},{6,7},{7,6},{8,9},{9,8},{10,11... | collective-permute-start | bytes 1572872 | tf_op jit(solution)/shard_map/ppermute | solution.py:547
  28.9 16.0 %all-to-all-start.1 = ((bf16[16,96,128]{2,1,0:T(8,128)(2,1)}), bf16[16,96,128]{2,1,0:T(8,128)(2,1)S(1)}, u32[]{:S(2)}, u32[]{:S(2)}) async-start(bf16[16,96,128]{2,1,0:T(8,128)(2,1)} %far_other.1), calls=%async_computation.1 | async-start | bytes 786432 | tf_op jit(solution)/shard_map/all_to_all | solution.py:560
  32.9 1.5 %collective-permute-start.3 = (bf16[8,128,128]{2,1,0:T(8,128)(2,1)S(1)}, bf16[8,128,128]{2,1,0:T(8,128)(2,1)S(1)}, u32[]{:S(2)}, u32[]{:S(2)}) collective-permute-start(bf16[8,128,128]{2,1,0:T(8,128)(2,1)S(1)} %collective-permute-done.refs_2_), channel_id=1, source_target_pairs={{0,1},{1,0},{2,3},{3,2},{4,5},{5,4},{6,7},{7,6},{8,9},{9,8},{10,11... | collective-permute-start | bytes 786440 | tf_op jit(solution)/shard_map/ppermute | solution.py:547
  37.1 5.3 %collective-permute-start.4 = (bf16[8,32,128]{2,1,0:T(8,128)(2,1)S(1)}, bf16[8,32,128]{2,1,0:T(8,128)(2,1)S(1)}, u32[]{:S(2)}, u32[]{:S(2)}) collective-permute-start(bf16[8,32,128]{2,1,0:T(8,128)(2,1)S(1)} %get-tuple-element.22), channel_id=1, source_target_pairs={{0,2},{2,0},{4,6},{6,4},{8,10},{10,8},{12,14},{14,12},{1,3},{3,1},... | collective-permute-start | bytes 196616 | tf_op jit(solution)/shard_map/ppermute | solution.py:553

commit v5 on v4

--- a/solution.py
+++ b/solution.py
@@ -73,7 +73,7 @@
 ):
     bands, windows, _, group, _ = x_ref.shape
     chunks = group // chans
-    step = 16
+    step = 32
     steps = windows // step
     rows = step * group
 
@@ -93,8 +93,8 @@
     has_prev = row_id >= chans
     has_next = row_id < group - chans
     k_id = lax.broadcasted_iota(jnp.int32, (group, LANES), 0) % chans
-    src = lax.broadcasted_iota(jnp.int32, (LANES, 3 * LANES), 0)
-    dst = lax.broadcasted_iota(jnp.int32, (LANES, 3 * LANES), 1) - LANES
+    src = lax.broadcasted_iota(jnp.int32, (2 * LANES, 3 * LANES), 0) % LANES
+    dst = lax.broadcasted_iota(jnp.int32, (2 * LANES, 3 * LANES), 1) - LANES
     band_mat = jnp.where(jnp.abs(src - dst) <= HALFWIN, 1.0, 0.0).astype(jnp.bfloat16)
 
     copies[0].wait()
@@ -115,9 +115,8 @@
             mag = jnp.sqrt(re * re + im * im)
             high = mag.astype(jnp.bfloat16)
             rest = (mag - high.astype(jnp.float32)).astype(jnp.bfloat16)
-            sums = jnp.dot(high, band_mat, preferred_element_type=jnp.float32) + jnp.dot(
-                rest, band_mat, preferred_element_type=jnp.float32
-            )
+            both = jnp.concatenate([high, rest], axis=1)
+            sums = jnp.dot(both, band_mat, preferred_element_type=jnp.float32)
             total = sums[:, LANES : 2 * LANES]
             total += jnp.where(has_prev, pltpu.roll(sums[:, 2 * LANES :], chans, 0), 0.0)
             total += jnp.where(has_next, pltpu.roll(sums[:, :LANES], rows - chans, 0), 0.0)
@@ -207,7 +206,7 @@
             out.append((s1 + g[0] * f[0], s2 + g[1] * f[1], s3 + g[2] * f[2]))
         return tuple(out)
 
-    sums = lax.fori_loop(0, windows, body, ((zero, zero, zero),) * len(work), unroll=8)
+    sums = lax.fori_loop(0, windows, body, ((zero, zero, zero),) * len(work), unroll=32)
     return [(s1 + s2, s1 - s3) for s1, s2, s3 in sums]
 
 
@@ -225,6 +224,8 @@
             for q in range(2):
                 vals = jnp.concatenate([sums[n * chans + k][q] for k in range(chans)])
                 put(r, t, q * chans * SUB, vals)
+        if done is not None:
+            done(mid, t)
         last = range(rows - 2, rows)
         sums = pair_sums([(f, g) for r in last for g in seconds[r] for f in firsts], windows)
         for n, r in enumerate(last):
@@ -236,7 +237,7 @@
                 rest.append(jnp.where(low, mine[1][q], pltpu.roll(mine[3][q], SUB // 2, 0)))
             put(r, t, 2 * chans * SUB, jnp.concatenate(rest))
         if done is not None:
-            done(t)
+            done(last, t)
 
 
 def far_own_kernel(got_ref, first_ref, out_ref, second_ref, *, rows, chans, windows):
@@ -280,8 +281,8 @@
         at += size
         out_ref[r * TILES + t, at : at + 2 * SUB, :] = vals.astype(jnp.bfloat16)
 
-    def done(t):
-        for r in range(2, rows):
+    def done(which, t):
+        for r in which:
             send(r * TILES + t, 1)
 
     far_sums(first_ref, other_ref, second_ref, put, rows, chans, windows, done)

time: 45.3 us -> 44.7 us (0.987)
  Pallas kernels: 10.5 us -> 9.15 us
  waiting for transfers between devices: 17.9 us -> 18.6 us
    all_to_all x1, waiting for transfers between devices: 1.44 us -> 2.22 us  [on_device_packed(): far = lax.all_to_all(far, 'row', 0, 0, tiled=True)]
  transfers between devices with their start and end apart: 7 -> 7, of which waited for: 6 -> 6; matrix products, arithmetic and copies ran while one was open for 0% -> 0% of each run, Pallas kernels for 12% -> 10%
where the time goes in v5:
time: 44.7 us; the launch traced here: 44.3 us
  waiting for transfers between devices  18.6 us (42%)
  starting transfers between devices  15.5 us (35%)
  Pallas kernels  9.15 us (20%)
  local copies, waits for them, and re-layouts  1.07 us (2%)
    ppermute x2, waiting for transfers between devices, level_swap(): return lax.ppermute(value, 'row', [(r, r ^ 1) for r in range(rows)])  13.4 us
    all_to_all x1, starting transfers between devices, on_device_packed(): got = lax.all_to_all(own, 'row', 0, 0, tiled=True)  7.29 us
    ppermute x2, starting transfers between devices, level_swap(): return lax.ppermute(value, 'row', [(r, r ^ 1) for r in range(rows)])  4.17 us
    all_to_all x1, starting transfers between devices, on_device_packed(): far = lax.all_to_all(far, 'row', 0, 0, tiled=True)  4.01 us
    pallas_call x1, Pallas kernels, whiten_packed(): pl.pallas_call(functools.partial(whiten_kernel, chans=chans), out_shape=j...  2.83 us
    ppermute x3, waiting for transfers between devices, swap(): return lax.ppermute(value, 'col', [(0, 1), (1, 0)])  2.28 us
    pallas_call x1, Pallas kernels, near_packed(): pl.pallas_call(functools.partial(near_kernel, windows=windows), out_shape...  2.26 us
    all_to_all x1, waiting for transfers between devices, on_device_packed(): far = lax.all_to_all(far, 'row', 0, 0, tiled=True)  2.22 us
  transfers between devices with their start and end apart: 7, of which 6 were waited for; matrix products, arithmetic and copies ran while one was open for 0% of the time, Pallas kernels for 10%

profile of v5, /device:TPU:0, one launch (start us, length us, event | category | flops | bytes accessed | tf_op | source)
XLA Modules:
  0.0 44.3 jit_solution(7919453235980643423)
XLA Ops:
  0.0 2.8 %whiten.1.own_ref = bf16[16,128,128]{2,1,0:T(8,128)(2,1)} custom-call(s32[2,32]{1,0:T(2,128)} %bitcast.12, bf16[2,32,2,16,128]{4,3,2,1,0:T(8,128)(2,1)} %bitcast.11), custom_call_target="tpu_custom_call" | custom-call | flops 1000000000 | bytes 1048576 | tf_op jit(solution)/shard_map/whiten/pallas_call | solution.py:150
  2.8 7.3 %all-to-all-start = ((bf16[16,128,128]{2,1,0:T(8,128)(2,1)}), bf16[16,128,128]{2,1,0:T(8,128)(2,1)S(1)}, u32[]{:S(2)}, u32[]{:S(2)}) async-start(bf16[16,128,128]{2,1,0:T(8,128)(2,1)} %whiten.1.own_ref), calls=%async_computation | async-start | bytes 1048576 | tf_op jit(solution)/shard_map/all_to_all | solution.py:551
  10.1 0.0 copy-start
  10.1 1.1 %copy-done = bf16[16,128,128]{2,1,0:T(8,128)(2,1)S(1)} copy-done((bf16[16,128,128]{2,1,0:T(8,128)(2,1)S(1)}, bf16[16,128,128]{2,1,0:T(8,128)(2,1)}, u32[]{:S(2)}) %copy-start) | copy-done | bytes 524312
  11.2 2.1 %collective-permute-start = (bf16[8,128,128]{2,1,0:T(8,128)(2,1)S(1)}, bf16[8,128,128]{2,1,0:T(8,128)(2,1)S(1)}, u32[]{:S(2)}, u32[]{:S(2)}) collective-permute-start(bf16[8,128,128]{2,1,0:T(8,128)(2,1)S(1)} %get-tuple-element.14), channel_id=1, source_target_pairs={{0,2},{2,0},{4,6},{6,4},{8,10},{10,8},{12,14},{14,12},{1,3},{3,1},... | collective-permute-start | bytes 786440 | tf_op jit(solution)/shard_map/ppermute | solution.py:554
  13.3 0.0 collective-permute-start.1
  13.3 10.7 %collective-permute-done.refs_2_ = bf16[8,128,128]{2,1,0:T(8,128)(2,1)S(1)} collective-permute-done((bf16[8,128,128]{2,1,0:T(8,128)(2,1)S(1)}, bf16[8,128,128]{2,1,0:T(8,128)(2,1)S(1)}, u32[]{:S(2)}, u32[]{:S(2)}) %collective-permute-start) | collective-permute-done | bytes 262176 | tf_op jit(solution)/shard_map/ppermute | solution.py:554
  24.0 0.0 collective-permute-done.1.refs_1_
  24.0 0.6 %all-to-all-done.got_ref = bf16[16,128,128]{2,1,0:T(8,128)(2,1)S(1)} async-done(((bf16[16,128,128]{2,1,0:T(8,128)(2,1)}), bf16[16,128,128]{2,1,0:T(8,128)(2,1)S(1)}, u32[]{:S(2)}, u32[]{:S(2)}) %all-to-all-start) | async-done | bytes 524320 | tf_op jit(solution)/shard_map/all_to_all | solution.py:551
  24.6 0.0 collective-permute-start.2
  24.6 1.2 %far_own.1 = (f32[2,2,3,256,128]{4,3,2,1,0:T(8,128)S(1)}, bf16[16,48,128]{2,1,0:T(8,128)(2,1)S(1)}) custom-call(bf16[16,128,128]{2,1,0:T(8,128)(2,1)S(1)} %all-to-all-done.got_ref), custom_call_target="tpu_custom_call" | custom-call | flops 1000000000 | bytes 1048576 | tf_op jit(solution)/shard_map/far_own/pallas_call | solution.py:302
  25.8 0.7 %collective-permute-done.2.other_ref = bf16[16,128,128]{2,1,0:T(8,128)(2,1)S(1)} collective-permute-done((bf16[16,128,128]{2,1,0:T(8,128)(2,1)S(1)}, bf16[16,128,128]{2,1,0:T(8,128)(2,1)S(1)}, u32[]{:S(2)}, u32[]{:S(2)}) %collective-permute-start.2) | collective-permute-done | bytes 524320 | tf_op jit(solution)/shard_map/ppermute | solution.py:548
  26.5 1.7 %far_other.1 = bf16[16,96,128]{2,1,0:T(8,128)(2,1)} custom-call(bf16[16,128,128]{2,1,0:T(8,128)(2,1)S(1)} %collective-permute-done.2.other_ref, f32[2,2,3,256,128]{4,3,2,1,0:T(8,128)S(1)} %get-tuple-element.17.first_ref, bf16[16,48,128]{2,1,0:T(8,128)(2,1)S(1)} %get-tuple-element.18.own_ref), custom_call_target="tpu_custom_call" | custom-call | flops 1000000000 | bytes 1048576 | tf_op jit(solution)/shard_map/far_other/pallas_call | solution.py:314
  28.2 4.0 %all-to-all-start.1 = ((bf16[16,96,128]{2,1,0:T(8,128)(2,1)}), bf16[16,96,128]{2,1,0:T(8,128)(2,1)S(1)}, u32[]{:S(2)}, u32[]{:S(2)}) async-start(bf16[16,96,128]{2,1,0:T(8,128)(2,1)} %far_other.1), calls=%async_computation.1 | async-start | bytes 786432 | tf_op jit(solution)/shard_map/all_to_all | solution.py:561
  32.3 0.0 collective-permute-start.3
  32.3 1.5 %collective-permute-done.3.refs_3_ = bf16[8,128,128]{2,1,0:T(8,128)(2,1)S(1)} collective-permute-done((bf16[8,128,128]{2,1,0:T(8,128)(2,1)S(1)}, bf16[8,128,128]{2,1,0:T(8,128)(2,1)S(1)}, u32[]{:S(2)}, u32[]{:S(2)}) %collective-permute-start.3) | collective-permute-done | bytes 262176 | tf_op jit(solution)/shard_map/ppermute | solution.py:548
  33.8 2.3 %near.1 = (bf16[8,32,128]{2,1,0:T(8,128)(2,1)S(1)}, bf16[8,32,128]{2,1,0:T(8,128)(2,1)S(1)}) custom-call(bf16[8,128,128]{2,1,0:T(8,128)(2,1)S(1)} %get-tuple-element.15.refs_0_, bf16[8,128,128]{2,1,0:T(8,128)(2,1)S(1)} %collective-permute-done.1.refs_1_, bf16[8,128,128]{2,1,0:T(8,128)(2,1)S(1)} %collective-permute-done.refs_2_, ...), custom_call_target="tpu_custom_call" | custom-call | flops 1000000000 | bytes 1048576 | tf_op jit(solution)/shard_map/near/pallas_call | solution.py:385
  36.1 2.1 %collective-permute-start.4 = (bf16[8,32,128]{2,1,0:T(8,128)(2,1)S(1)}, bf16[8,32,128]{2,1,0:T(8,128)(2,1)S(1)}, u32[]{:S(2)}, u32[]{:S(2)}) collective-permute-start(bf16[8,32,128]{2,1,0:T(8,128)(2,1)S(1)} %get-tuple-element.22), channel_id=1, source_target_pairs={{0,2},{2,0},{4,6},{6,4},{8,10},{10,8},{12,14},{14,12},{1,3},{3,1},... | collective-permute-start | bytes 196616 | tf_op jit(solution)/shard_map/ppermute | solution.py:554
  38.1 2.8 %collective-permute-done.4.taken_ref = bf16[8,32,128]{2,1,0:T(8,128)(2,1)S(1)} collective-permute-done((bf16[8,32,128]{2,1,0:T(8,128)(2,1)S(1)}, bf16[8,32,128]{2,1,0:T(8,128)(2,1)S(1)}, u32[]{:S(2)}, u32[]{:S(2)}) %collective-permute-start.4) | collective-permute-done | bytes 65568 | tf_op jit(solution)/shard_map/ppermute | solution.py:554
  40.9 1.1 %near_out.1._ = f32[2,2,16,4,8,128]{5,4,3,2,1,0:T(8,128)} custom-call(bf16[8,32,128]{2,1,0:T(8,128)(2,1)S(1)} %get-tuple-element.21.kept_ref, bf16[8,32,128]{2,1,0:T(8,128)(2,1)S(1)} %collective-permute-done.4.taken_ref), custom_call_target="tpu_custom_call" | custom-call | flops 1000000000 | bytes 1048576 | tf_op jit(solution)/shard_map/near_out/pallas_call | solution.py:439
  42.0 2.2 %all-to-all-done.1.far_ref = bf16[16,96,128]{2,1,0:T(8,128)(2,1)S(1)} async-done(((bf16[16,96,128]{2,1,0:T(8,128)(2,1)}), bf16[16,96,128]{2,1,0:T(8,128)(2,1)S(1)}, u32[]{:S(2)}, u32[]{:S(2)}) %all-to-all-start.1) | async-done | bytes 393248 | tf_op jit(solution)/shard_map/all_to_all | solution.py:561
  44.2 0.1 finish.1
  (1 shorter events, 0.0 us)
Async XLA Ops:
  2.8 21.8 %all-to-all-start = ((bf16[16,128,128]{2,1,0:T(8,128)(2,1)}), bf16[16,128,128]{2,1,0:T(8,128)(2,1)S(1)}, u32[]{:S(2)}, u32[]{:S(2)}) async-start(bf16[16,128,128]{2,1,0:T(8,128)(2,1)} %whiten.1.own_ref), calls=%async_computation | async-start | bytes 1048576 | tf_op jit(solution)/shard_map/all_to_all | solution.py:551
  10.1 1.1 %copy-start = (bf16[16,128,128]{2,1,0:T(8,128)(2,1)S(1)}, bf16[16,128,128]{2,1,0:T(8,128)(2,1)}, u32[]{:S(2)}) copy-start(bf16[16,128,128]{2,1,0:T(8,128)(2,1)} %whiten.1.own_ref) | copy-start | bytes 1572868
  11.2 12.7 %collective-permute-start = (bf16[8,128,128]{2,1,0:T(8,128)(2,1)S(1)}, bf16[8,128,128]{2,1,0:T(8,128)(2,1)S(1)}, u32[]{:S(2)}, u32[]{:S(2)}) collective-permute-start(bf16[8,128,128]{2,1,0:T(8,128)(2,1)S(1)} %get-tuple-element.14), channel_id=1, source_target_pairs={{0,2},{2,0},{4,6},{6,4},{8,10},{10,8},{12,14},{14,12},{1,3},{3,1},... | collective-permute-start | bytes 786440 | tf_op jit(solution)/shard_map/ppermute | solution.py:554
  13.3 10.7 %collective-permute-start.1 = (bf16[8,128,128]{2,1,0:T(8,128)(2,1)S(1)}, bf16[8,128,128]{2,1,0:T(8,128)(2,1)S(1)}, u32[]{:S(2)}, u32[]{:S(2)}) collective-permute-start(bf16[8,128,128]{2,1,0:T(8,128)(2,1)S(1)} %get-tuple-element.15.refs_0_), channel_id=1, source_target_pairs={{0,1},{1,0},{2,3},{3,2},{4,5},{5,4},{6,7},{7,6},{8,9},{9,8},{10,11... | collective-permute-start | bytes 786440 | tf_op jit(solution)/shard_map/ppermute | solution.py:548
  24.6 1.9 %collective-permute-start.2 = (bf16[16,128,128]{2,1,0:T(8,128)(2,1)S(1)}, bf16[16,128,128]{2,1,0:T(8,128)(2,1)S(1)}, u32[]{:S(2)}, u32[]{:S(2)}) collective-permute-start(bf16[16,128,128]{2,1,0:T(8,128)(2,1)S(1)} %all-to-all-done.got_ref), channel_id=1, source_target_pairs={{0,1},{1,0},{2,3},{3,2},{4,5},{5,4},{6,7},{7,6},{8,9},{9,8},{10,11... | collective-permute-start | bytes 1572872 | tf_op jit(solution)/shard_map/ppermute | solution.py:548
  28.2 16.0 %all-to-all-start.1 = ((bf16[16,96,128]{2,1,0:T(8,128)(2,1)}), bf16[16,96,128]{2,1,0:T(8,128)(2,1)S(1)}, u32[]{:S(2)}, u32[]{:S(2)}) async-start(bf16[16,96,128]{2,1,0:T(8,128)(2,1)} %far_other.1), calls=%async_computation.1 | async-start | bytes 786432 | tf_op jit(solution)/shard_map/all_to_all | solution.py:561
  32.3 1.5 %collective-permute-start.3 = (bf16[8,128,128]{2,1,0:T(8,128)(2,1)S(1)}, bf16[8,128,128]{2,1,0:T(8,128)(2,1)S(1)}, u32[]{:S(2)}, u32[]{:S(2)}) collective-permute-start(bf16[8,128,128]{2,1,0:T(8,128)(2,1)S(1)} %collective-permute-done.refs_2_), channel_id=1, source_target_pairs={{0,1},{1,0},{2,3},{3,2},{4,5},{5,4},{6,7},{7,6},{8,9},{9,8},{10,11... | collective-permute-start | bytes 786440 | tf_op jit(solution)/shard_map/ppermute | solution.py:548
  36.1 4.9 %collective-permute-start.4 = (bf16[8,32,128]{2,1,0:T(8,128)(2,1)S(1)}, bf16[8,32,128]{2,1,0:T(8,128)(2,1)S(1)}, u32[]{:S(2)}, u32[]{:S(2)}) collective-permute-start(bf16[8,32,128]{2,1,0:T(8,128)(2,1)S(1)} %get-tuple-element.22), channel_id=1, source_target_pairs={{0,2},{2,0},{4,6},{6,4},{8,10},{10,8},{12,14},{14,12},{1,3},{3,1},... | collective-permute-start | bytes 196616 | tf_op jit(solution)/shard_map/ppermute | solution.py:554

commit v6 on v5

--- a/solution.py
+++ b/solution.py
@@ -97,11 +97,11 @@
     dst = lax.broadcasted_iota(jnp.int32, (2 * LANES, 3 * LANES), 1) - LANES
     band_mat = jnp.where(jnp.abs(src - dst) <= HALFWIN, 1.0, 0.0).astype(jnp.bfloat16)
 
-    copies[0].wait()
+    for copy in copies:
+        copy.wait()
     for b in range(bands):
         for n in range(steps):
             w0 = n * step
-            copies[1 + b * steps + n].wait()
             x = x_ref[b, w0 : w0 + step].astype(jnp.float32)
             keeps = []
             for s in range(step):
@@ -157,7 +157,7 @@
             pltpu.VMEM(view.shape, jnp.bfloat16),
             pltpu.VMEM((bands * parts * windows * group, LANES), jnp.float32),
             pltpu.VMEM(shape, jnp.bfloat16),
-            pltpu.SemaphoreType.DMA((bands * windows // 16 + 1,)),
+            pltpu.SemaphoreType.DMA((bands * windows // 32 + 1,)),
             pltpu.SemaphoreType.DMA((tiles // TILES,)),
         ],
         compiler_params=pltpu.CompilerParams(vmem_limit_bytes=VMEM_FIRST),
@@ -576,7 +576,7 @@
         and bands * bins == rows * TILES * LANES
         and cols == 2
         and chans == 2
-        and windows % 16 == 0
+        and windows % 32 == 0
         and bins == rows * LANES
     ):
         return on_device_packed(spectra, window_flags)

time: 44.7 us -> 44.6 us (level)
  no operation moved by 1% of the time
where the time goes in v6:
time: 44.6 us; the launch traced here: 44.3 us
  waiting for transfers between devices  18.6 us (42%)
  starting transfers between devices  15.5 us (35%)
  Pallas kernels  9.08 us (20%)
  local copies, waits for them, and re-layouts  1.07 us (2%)
    ppermute x2, waiting for transfers between devices, level_swap(): return lax.ppermute(value, 'row', [(r, r ^ 1) for r in range(rows)])  13.4 us
    all_to_all x1, starting transfers between devices, on_device_packed(): got = lax.all_to_all(own, 'row', 0, 0, tiled=True)  7.29 us
    ppermute x2, starting transfers between devices, level_swap(): return lax.ppermute(value, 'row', [(r, r ^ 1) for r in range(rows)])  4.17 us
    all_to_all x1, starting transfers between devices, on_device_packed(): far = lax.all_to_all(far, 'row', 0, 0, tiled=True)  4.01 us
    pallas_call x1, Pallas kernels, whiten_packed(): pl.pallas_call(functools.partial(whiten_kernel, chans=chans), out_shape=j...  2.75 us
    ppermute x3, waiting for transfers between devices, swap(): return lax.ppermute(value, 'col', [(0, 1), (1, 0)])  2.28 us
    pallas_call x1, Pallas kernels, near_packed(): pl.pallas_call(functools.partial(near_kernel, windows=windows), out_shape...  2.26 us
    all_to_all x1, waiting for transfers between devices, on_device_packed(): far = lax.all_to_all(far, 'row', 0, 0, tiled=True)  2.22 us
  transfers between devices with their start and end apart: 7, of which 6 were waited for; matrix products, arithmetic and copies ran while one was open for 0% of the time, Pallas kernels for 10%

profile of v6, /device:TPU:0, one launch (start us, length us, event | category | flops | bytes accessed | tf_op | source)
XLA Modules:
  0.0 44.3 jit_solution(994627952577716090)
XLA Ops:
  0.0 2.8 %whiten.1.own_ref = bf16[16,128,128]{2,1,0:T(8,128)(2,1)} custom-call(s32[2,32]{1,0:T(2,128)} %bitcast.12, bf16[2,32,2,16,128]{4,3,2,1,0:T(8,128)(2,1)} %bitcast.11), custom_call_target="tpu_custom_call" | custom-call | flops 1000000000 | bytes 1048576 | tf_op jit(solution)/shard_map/whiten/pallas_call | solution.py:150
  2.8 7.3 %all-to-all-start = ((bf16[16,128,128]{2,1,0:T(8,128)(2,1)}), bf16[16,128,128]{2,1,0:T(8,128)(2,1)S(1)}, u32[]{:S(2)}, u32[]{:S(2)}) async-start(bf16[16,128,128]{2,1,0:T(8,128)(2,1)} %whiten.1.own_ref), calls=%async_computation | async-start | bytes 1048576 | tf_op jit(solution)/shard_map/all_to_all | solution.py:551
  10.1 0.0 copy-start
  10.1 1.1 %copy-done = bf16[16,128,128]{2,1,0:T(8,128)(2,1)S(1)} copy-done((bf16[16,128,128]{2,1,0:T(8,128)(2,1)S(1)}, bf16[16,128,128]{2,1,0:T(8,128)(2,1)}, u32[]{:S(2)}) %copy-start) | copy-done | bytes 524312
  11.2 2.1 %collective-permute-start = (bf16[8,128,128]{2,1,0:T(8,128)(2,1)S(1)}, bf16[8,128,128]{2,1,0:T(8,128)(2,1)S(1)}, u32[]{:S(2)}, u32[]{:S(2)}) collective-permute-start(bf16[8,128,128]{2,1,0:T(8,128)(2,1)S(1)} %get-tuple-element.14), channel_id=1, source_target_pairs={{0,2},{2,0},{4,6},{6,4},{8,10},{10,8},{12,14},{14,12},{1,3},{3,1},... | collective-permute-start | bytes 786440 | tf_op jit(solution)/shard_map/ppermute | solution.py:554
  13.3 0.0 collective-permute-start.1
  13.3 10.7 %collective-permute-done.refs_2_ = bf16[8,128,128]{2,1,0:T(8,128)(2,1)S(1)} collective-permute-done((bf16[8,128,128]{2,1,0:T(8,128)(2,1)S(1)}, bf16[8,128,128]{2,1,0:T(8,128)(2,1)S(1)}, u32[]{:S(2)}, u32[]{:S(2)}) %collective-permute-start) | collective-permute-done | bytes 262176 | tf_op jit(solution)/shard_map/ppermute | solution.py:554
  23.9 0.0 collective-permute-done.1.refs_1_
  23.9 0.6 %all-to-all-done.got_ref = bf16[16,128,128]{2,1,0:T(8,128)(2,1)S(1)} async-done(((bf16[16,128,128]{2,1,0:T(8,128)(2,1)}), bf16[16,128,128]{2,1,0:T(8,128)(2,1)S(1)}, u32[]{:S(2)}, u32[]{:S(2)}) %all-to-all-start) | async-done | bytes 524320 | tf_op jit(solution)/shard_map/all_to_all | solution.py:551
  24.5 0.0 collective-permute-start.2
  24.5 1.2 %far_own.1 = (f32[2,2,3,256,128]{4,3,2,1,0:T(8,128)S(1)}, bf16[16,48,128]{2,1,0:T(8,128)(2,1)S(1)}) custom-call(bf16[16,128,128]{2,1,0:T(8,128)(2,1)S(1)} %all-to-all-done.got_ref), custom_call_target="tpu_custom_call" | custom-call | flops 1000000000 | bytes 1048576 | tf_op jit(solution)/shard_map/far_own/pallas_call | solution.py:302
  25.7 0.7 %collective-permute-done.2.other_ref = bf16[16,128,128]{2,1,0:T(8,128)(2,1)S(1)} collective-permute-done((bf16[16,128,128]{2,1,0:T(8,128)(2,1)S(1)}, bf16[16,128,128]{2,1,0:T(8,128)(2,1)S(1)}, u32[]{:S(2)}, u32[]{:S(2)}) %collective-permute-start.2) | collective-permute-done | bytes 524320 | tf_op jit(solution)/shard_map/ppermute | solution.py:548
  26.4 1.7 %far_other.1 = bf16[16,96,128]{2,1,0:T(8,128)(2,1)} custom-call(bf16[16,128,128]{2,1,0:T(8,128)(2,1)S(1)} %collective-permute-done.2.other_ref, f32[2,2,3,256,128]{4,3,2,1,0:T(8,128)S(1)} %get-tuple-element.17.first_ref, bf16[16,48,128]{2,1,0:T(8,128)(2,1)S(1)} %get-tuple-element.18.own_ref), custom_call_target="tpu_custom_call" | custom-call | flops 1000000000 | bytes 1048576 | tf_op jit(solution)/shard_map/far_other/pallas_call | solution.py:314
  28.2 4.0 %all-to-all-start.1 = ((bf16[16,96,128]{2,1,0:T(8,128)(2,1)}), bf16[16,96,128]{2,1,0:T(8,128)(2,1)S(1)}, u32[]{:S(2)}, u32[]{:S(2)}) async-start(bf16[16,96,128]{2,1,0:T(8,128)(2,1)} %far_other.1), calls=%async_computation.1 | async-start | bytes 786432 | tf_op jit(solution)/shard_map/all_to_all | solution.py:561
  32.2 0.0 collective-permute-start.3
  32.2 1.5 %collective-permute-done.3.refs_3_ = bf16[8,128,128]{2,1,0:T(8,128)(2,1)S(1)} collective-permute-done((bf16[8,128,128]{2,1,0:T(8,128)(2,1)S(1)}, bf16[8,128,128]{2,1,0:T(8,128)(2,1)S(1)}, u32[]{:S(2)}, u32[]{:S(2)}) %collective-permute-start.3) | collective-permute-done | bytes 262176 | tf_op jit(solution)/shard_map/ppermute | solution.py:548
  33.7 2.3 %near.1 = (bf16[8,32,128]{2,1,0:T(8,128)(2,1)S(1)}, bf16[8,32,128]{2,1,0:T(8,128)(2,1)S(1)}) custom-call(bf16[8,128,128]{2,1,0:T(8,128)(2,1)S(1)} %get-tuple-element.15.refs_0_, bf16[8,128,128]{2,1,0:T(8,128)(2,1)S(1)} %collective-permute-done.1.refs_1_, bf16[8,128,128]{2,1,0:T(8,128)(2,1)S(1)} %collective-permute-done.refs_2_, ...), custom_call_target="tpu_custom_call" | custom-call | flops 1000000000 | bytes 1048576 | tf_op jit(solution)/shard_map/near/pallas_call | solution.py:385
  36.0 2.1 %collective-permute-start.4 = (bf16[8,32,128]{2,1,0:T(8,128)(2,1)S(1)}, bf16[8,32,128]{2,1,0:T(8,128)(2,1)S(1)}, u32[]{:S(2)}, u32[]{:S(2)}) collective-permute-start(bf16[8,32,128]{2,1,0:T(8,128)(2,1)S(1)} %get-tuple-element.22), channel_id=1, source_target_pairs={{0,2},{2,0},{4,6},{6,4},{8,10},{10,8},{12,14},{14,12},{1,3},{3,1},... | collective-permute-start | bytes 196616 | tf_op jit(solution)/shard_map/ppermute | solution.py:554
  38.1 2.8 %collective-permute-done.4.taken_ref = bf16[8,32,128]{2,1,0:T(8,128)(2,1)S(1)} collective-permute-done((bf16[8,32,128]{2,1,0:T(8,128)(2,1)S(1)}, bf16[8,32,128]{2,1,0:T(8,128)(2,1)S(1)}, u32[]{:S(2)}, u32[]{:S(2)}) %collective-permute-start.4) | collective-permute-done | bytes 65568 | tf_op jit(solution)/shard_map/ppermute | solution.py:554
  40.8 1.1 %near_out.1._ = f32[2,2,16,4,8,128]{5,4,3,2,1,0:T(8,128)} custom-call(bf16[8,32,128]{2,1,0:T(8,128)(2,1)S(1)} %get-tuple-element.21.kept_ref, bf16[8,32,128]{2,1,0:T(8,128)(2,1)S(1)} %collective-permute-done.4.taken_ref), custom_call_target="tpu_custom_call" | custom-call | flops 1000000000 | bytes 1048576 | tf_op jit(solution)/shard_map/near_out/pallas_call | solution.py:439
  41.9 2.2 %all-to-all-done.1.far_ref = bf16[16,96,128]{2,1,0:T(8,128)(2,1)S(1)} async-done(((bf16[16,96,128]{2,1,0:T(8,128)(2,1)}), bf16[16,96,128]{2,1,0:T(8,128)(2,1)S(1)}, u32[]{:S(2)}, u32[]{:S(2)}) %all-to-all-start.1) | async-done | bytes 393248 | tf_op jit(solution)/shard_map/all_to_all | solution.py:561
  44.1 0.1 finish.1
  (1 shorter events, 0.0 us)
Async XLA Ops:
  2.8 21.8 %all-to-all-start = ((bf16[16,128,128]{2,1,0:T(8,128)(2,1)}), bf16[16,128,128]{2,1,0:T(8,128)(2,1)S(1)}, u32[]{:S(2)}, u32[]{:S(2)}) async-start(bf16[16,128,128]{2,1,0:T(8,128)(2,1)} %whiten.1.own_ref), calls=%async_computation | async-start | bytes 1048576 | tf_op jit(solution)/shard_map/all_to_all | solution.py:551
  10.1 1.1 %copy-start = (bf16[16,128,128]{2,1,0:T(8,128)(2,1)S(1)}, bf16[16,128,128]{2,1,0:T(8,128)(2,1)}, u32[]{:S(2)}) copy-start(bf16[16,128,128]{2,1,0:T(8,128)(2,1)} %whiten.1.own_ref) | copy-start | bytes 1572868
  11.2 12.7 %collective-permute-start = (bf16[8,128,128]{2,1,0:T(8,128)(2,1)S(1)}, bf16[8,128,128]{2,1,0:T(8,128)(2,1)S(1)}, u32[]{:S(2)}, u32[]{:S(2)}) collective-permute-start(bf16[8,128,128]{2,1,0:T(8,128)(2,1)S(1)} %get-tuple-element.14), channel_id=1, source_target_pairs={{0,2},{2,0},{4,6},{6,4},{8,10},{10,8},{12,14},{14,12},{1,3},{3,1},... | collective-permute-start | bytes 786440 | tf_op jit(solution)/shard_map/ppermute | solution.py:554
  13.3 10.7 %collective-permute-start.1 = (bf16[8,128,128]{2,1,0:T(8,128)(2,1)S(1)}, bf16[8,128,128]{2,1,0:T(8,128)(2,1)S(1)}, u32[]{:S(2)}, u32[]{:S(2)}) collective-permute-start(bf16[8,128,128]{2,1,0:T(8,128)(2,1)S(1)} %get-tuple-element.15.refs_0_), channel_id=1, source_target_pairs={{0,1},{1,0},{2,3},{3,2},{4,5},{5,4},{6,7},{7,6},{8,9},{9,8},{10,11... | collective-permute-start | bytes 786440 | tf_op jit(solution)/shard_map/ppermute | solution.py:548
  24.5 1.9 %collective-permute-start.2 = (bf16[16,128,128]{2,1,0:T(8,128)(2,1)S(1)}, bf16[16,128,128]{2,1,0:T(8,128)(2,1)S(1)}, u32[]{:S(2)}, u32[]{:S(2)}) collective-permute-start(bf16[16,128,128]{2,1,0:T(8,128)(2,1)S(1)} %all-to-all-done.got_ref), channel_id=1, source_target_pairs={{0,1},{1,0},{2,3},{3,2},{4,5},{5,4},{6,7},{7,6},{8,9},{9,8},{10,11... | collective-permute-start | bytes 1572872 | tf_op jit(solution)/shard_map/ppermute | solution.py:548
  28.2 16.0 %all-to-all-start.1 = ((bf16[16,96,128]{2,1,0:T(8,128)(2,1)}), bf16[16,96,128]{2,1,0:T(8,128)(2,1)S(1)}, u32[]{:S(2)}, u32[]{:S(2)}) async-start(bf16[16,96,128]{2,1,0:T(8,128)(2,1)} %far_other.1), calls=%async_computation.1 | async-start | bytes 786432 | tf_op jit(solution)/shard_map/all_to_all | solution.py:561
  32.2 1.5 %collective-permute-start.3 = (bf16[8,128,128]{2,1,0:T(8,128)(2,1)S(1)}, bf16[8,128,128]{2,1,0:T(8,128)(2,1)S(1)}, u32[]{:S(2)}, u32[]{:S(2)}) collective-permute-start(bf16[8,128,128]{2,1,0:T(8,128)(2,1)S(1)} %collective-permute-done.refs_2_), channel_id=1, source_target_pairs={{0,1},{1,0},{2,3},{3,2},{4,5},{5,4},{6,7},{7,6},{8,9},{9,8},{10,11... | collective-permute-start | bytes 786440 | tf_op jit(solution)/shard_map/ppermute | solution.py:548
  36.0 4.9 %collective-permute-start.4 = (bf16[8,32,128]{2,1,0:T(8,128)(2,1)S(1)}, bf16[8,32,128]{2,1,0:T(8,128)(2,1)S(1)}, u32[]{:S(2)}, u32[]{:S(2)}) collective-permute-start(bf16[8,32,128]{2,1,0:T(8,128)(2,1)S(1)} %get-tuple-element.22), channel_id=1, source_target_pairs={{0,2},{2,0},{4,6},{6,4},{8,10},{10,8},{12,14},{14,12},{1,3},{3,1},... | collective-permute-start | bytes 196616 | tf_op jit(solution)/shard_map/ppermute | solution.py:554

commit v7 on v6

--- a/solution.py
+++ b/solution.py
@@ -189,6 +189,7 @@
 
 def pair_sums(work, windows):
     zero = jnp.zeros((SUB, LANES), jnp.float32)
+    low = lax.broadcasted_iota(jnp.int32, (SUB, LANES), 0) < SUB // 2
 
     def body(w, sums):
         base = pl.multiple_of(w * SUB, SUB)
@@ -202,7 +203,11 @@
         out = []
         for (first_ref, second_ref), (s1, s2, s3) in zip(work, sums):
             f = load(first_ref, pl.ds(base, SUB))
-            g = load(second_ref, pl.ds(w, 1))
+            if isinstance(second_ref, tuple):
+                ends = [load(ref, pl.ds(w, 1)) for ref in second_ref]
+                g = [jnp.where(low, one, two) for one, two in zip(*ends)]
+            else:
+                g = load(second_ref, pl.ds(w, 1))
             out.append((s1 + g[0] * f[0], s2 + g[1] * f[1], s3 + g[2] * f[2]))
         return tuple(out)
 
@@ -210,31 +215,37 @@
     return [(s1 + s2, s1 - s3) for s1, s2, s3 in sums]
 
 
-def far_sums(first_ref, values_ref, second_ref, put, rows, chans, windows, done=None):
-    low = lax.broadcasted_iota(jnp.int32, (SUB, LANES), 0) < SUB // 2
+def far_sums(first_ref, values_ref, second_ref, put, rows, chans, windows, done=None, skip=0):
     for t in range(TILES):
-        firsts = [first_ref.at[block, t] for block in range(2)]
+        firsts, last_firsts, level_firsts = (first_ref.at[block, t] for block in range(3))
         seconds = {}
         for r in range(2, rows):
-            spread_second(second_ref.at[t, r], values_ref[r * TILES + t], windows, chans)
-            seconds[r] = [second_ref.at[t, r, k] for k in range(chans)]
-        mid = range(2, rows - 2)
-        sums = pair_sums([(firsts[0], g) for r in mid for g in seconds[r]], windows)
+            spread_second(second_ref.at[t, r], values_ref[(r - skip) * TILES + t], windows, chans)
+            seconds[r] = tuple(second_ref.at[t, r, k] for k in range(chans))
+        mid = range(4, rows - 2)
+        work = [(level_firsts, seconds[r]) for r in (2, 3)]
+        work += [(firsts, g) for r in mid for g in seconds[r]]
+        sums = pair_sums(work, windows)
+        for n, r in enumerate((2, 3)):
+            for q in range(2):
+                vals = sums[n][q]
+                vals = jnp.concatenate([vals, pltpu.roll(vals, SUB // 2, 0)])
+                put(r, t, q * chans * SUB, vals)
         for n, r in enumerate(mid):
+            for q in range(2):
+                vals = jnp.concatenate([sums[2 + n * chans + k][q] for k in range(chans)])
+                put(r, t, q * chans * SUB, vals)
+        if done is not None:
+            done(range(2, rows - 2), t)
+        last = range(rows - 2, rows)
+        work = [(firsts, g) for r in last for g in seconds[r]]
+        work += [(last_firsts, seconds[r]) for r in last]
+        sums = pair_sums(work, windows)
+        for n, r in enumerate(last):
             for q in range(2):
                 vals = jnp.concatenate([sums[n * chans + k][q] for k in range(chans)])
                 put(r, t, q * chans * SUB, vals)
-        if done is not None:
-            done(mid, t)
-        last = range(rows - 2, rows)
-        sums = pair_sums([(f, g) for r in last for g in seconds[r] for f in firsts], windows)
-        for n, r in enumerate(last):
-            mine = sums[n * 2 * chans : (n + 1) * 2 * chans]
-            rest = []
-            for q in range(2):
-                vals = jnp.concatenate([mine[k * 2][q] for k in range(chans)])
-                put(r, t, q * chans * SUB, vals)
-                rest.append(jnp.where(low, mine[1][q], pltpu.roll(mine[3][q], SUB // 2, 0)))
+            rest = sums[len(last) * chans + n]
             put(r, t, 2 * chans * SUB, jnp.concatenate(rest))
         if done is not None:
             done(last, t)
@@ -243,13 +254,11 @@
 def far_own_kernel(got_ref, first_ref, out_ref, second_ref, *, rows, chans, windows):
     for t in range(TILES):
         for r in range(rows - 2):
-            spread_first(
-                first_ref.at[r * chans // SUB, t],
-                r % (SUB // chans),
-                got_ref[r * TILES + t],
-                windows,
-                chans,
-            )
+            places = [(0, r)] if r < 4 else [(1, r - 4), (1, r - 2)]
+            places += [(2, r), (2, r + 2)] if r < 2 else []
+            for block, slot in places:
+                first = first_ref.at[block, t]
+                spread_first(first, slot, got_ref[r * TILES + t], windows, chans)
 
     def put(r, t, at, vals):
         out_ref[r * TILES + t, at : at + 2 * SUB, :] = vals.astype(jnp.bfloat16)
@@ -285,7 +294,7 @@
         for r in which:
             send(r * TILES + t, 1)
 
-    far_sums(first_ref, other_ref, second_ref, put, rows, chans, windows, done)
+    far_sums(first_ref, other_ref, second_ref, put, rows, chans, windows, done, skip=2)
     for copy in copies:
         copy.wait()
 
@@ -302,7 +311,7 @@
     first, own = pl.pallas_call(
         functools.partial(far_own_kernel, **sizes),
         out_shape=[
-            jax.ShapeDtypeStruct((2, TILES, 3, windows * SUB, LANES), jnp.float32),
+            jax.ShapeDtypeStruct((3, TILES, 3, windows * SUB, LANES), jnp.float32),
             jax.ShapeDtypeStruct((rows * TILES, size, LANES), jnp.bfloat16),
         ],
         in_specs=[vmem],
@@ -323,7 +332,7 @@
         ],
         name="far_other",
         **params,
-    )(swap(got), first, own)
+    )(swap(got[2 * TILES :]), first, own)
 
 
 def halves_kernel(own_ref, keep_ref, give_ref):

time: 44.6 us -> 44.4 us (level)
  no operation moved by 1% of the time
where the time goes in v7:
time: 44.4 us; the launch traced here: 44.1 us
  waiting for transfers between devices  18.3 us (41%)
  starting transfers between devices  15.6 us (35%)
  Pallas kernels  9.09 us (20%)
  local copies, waits for them, and re-layouts  1.1 us (2%)
    ppermute x2, waiting for transfers between devices, level_swap(): return lax.ppermute(value, 'row', [(r, r ^ 1) for r in range(rows)])  13.4 us
    all_to_all x1, starting transfers between devices, on_device_packed(): got = lax.all_to_all(own, 'row', 0, 0, tiled=True)  7.29 us
    ppermute x2, starting transfers between devices, level_swap(): return lax.ppermute(value, 'row', [(r, r ^ 1) for r in range(rows)])  4.17 us
    all_to_all x1, starting transfers between devices, on_device_packed(): far = lax.all_to_all(far, 'row', 0, 0, tiled=True)  4.01 us
    pallas_call x1, Pallas kernels, whiten_packed(): pl.pallas_call(functools.partial(whiten_kernel, chans=chans), out_shape=j...  2.75 us
    pallas_call x1, Pallas kernels, near_packed(): pl.pallas_call(functools.partial(near_kernel, windows=windows), out_shape...  2.26 us
    all_to_all x1, waiting for transfers between devices, on_device_packed(): far = lax.all_to_all(far, 'row', 0, 0, tiled=True)  2.22 us
    ppermute x3, waiting for transfers between devices, swap(): return lax.ppermute(value, 'col', [(0, 1), (1, 0)])  1.97 us
  transfers between devices with their start and end apart: 7, of which 6 were waited for; matrix products, arithmetic and copies ran while one was open for 0% of the time, Pallas kernels for 10%

profile of v7, /device:TPU:0, one launch (start us, length us, event | category | flops | bytes accessed | tf_op | source)
XLA Modules:
  0.0 44.1 jit_solution(3084077977342822100)
XLA Ops:
  0.0 2.8 %whiten.1.own_ref = bf16[16,128,128]{2,1,0:T(8,128)(2,1)} custom-call(s32[2,32]{1,0:T(2,128)} %bitcast.12, bf16[2,32,2,16,128]{4,3,2,1,0:T(8,128)(2,1)} %bitcast.11), custom_call_target="tpu_custom_call" | custom-call | flops 1000000000 | bytes 1048576 | tf_op jit(solution)/shard_map/whiten/pallas_call | solution.py:150
  2.8 7.3 %all-to-all-start = ((bf16[16,128,128]{2,1,0:T(8,128)(2,1)}), bf16[16,128,128]{2,1,0:T(8,128)(2,1)S(1)}, u32[]{:S(2)}, u32[]{:S(2)}) async-start(bf16[16,128,128]{2,1,0:T(8,128)(2,1)} %whiten.1.own_ref), calls=%async_computation | async-start | bytes 1048576 | tf_op jit(solution)/shard_map/all_to_all | solution.py:560
  10.1 0.0 copy-start
  10.1 1.1 %copy-done = bf16[16,128,128]{2,1,0:T(8,128)(2,1)S(1)} copy-done((bf16[16,128,128]{2,1,0:T(8,128)(2,1)S(1)}, bf16[16,128,128]{2,1,0:T(8,128)(2,1)}, u32[]{:S(2)}) %copy-start) | copy-done | bytes 524312
  11.2 2.1 %collective-permute-start = (bf16[8,128,128]{2,1,0:T(8,128)(2,1)S(1)}, bf16[8,128,128]{2,1,0:T(8,128)(2,1)S(1)}, u32[]{:S(2)}, u32[]{:S(2)}) collective-permute-start(bf16[8,128,128]{2,1,0:T(8,128)(2,1)S(1)} %get-tuple-element.14), channel_id=1, source_target_pairs={{0,2},{2,0},{4,6},{6,4},{8,10},{10,8},{12,14},{14,12},{1,3},{3,1},... | collective-permute-start | bytes 786440 | tf_op jit(solution)/shard_map/ppermute | solution.py:563
  13.3 0.0 collective-permute-start.1
  13.3 10.7 %collective-permute-done.refs_2_ = bf16[8,128,128]{2,1,0:T(8,128)(2,1)S(1)} collective-permute-done((bf16[8,128,128]{2,1,0:T(8,128)(2,1)S(1)}, bf16[8,128,128]{2,1,0:T(8,128)(2,1)S(1)}, u32[]{:S(2)}, u32[]{:S(2)}) %collective-permute-start) | collective-permute-done | bytes 262176 | tf_op jit(solution)/shard_map/ppermute | solution.py:563
  23.9 0.0 collective-permute-done.1.refs_1_
  23.9 0.6 %all-to-all-done.got_ref = bf16[16,128,128]{2,1,0:T(8,128)(2,1)S(1)} async-done(((bf16[16,128,128]{2,1,0:T(8,128)(2,1)}), bf16[16,128,128]{2,1,0:T(8,128)(2,1)S(1)}, u32[]{:S(2)}, u32[]{:S(2)}) %all-to-all-start) | async-done | bytes 524320 | tf_op jit(solution)/shard_map/all_to_all | solution.py:560
  24.6 0.1 collective-permute-start.2
  24.6 1.3 %far_own.1 = (f32[3,2,3,256,128]{4,3,2,1,0:T(8,128)S(1)}, bf16[16,48,128]{2,1,0:T(8,128)(2,1)S(1)}) custom-call(bf16[16,128,128]{2,1,0:T(8,128)(2,1)S(1)} %all-to-all-done.got_ref), custom_call_target="tpu_custom_call" | custom-call | flops 1000000000 | bytes 1048576 | tf_op jit(solution)/shard_map/far_own/pallas_call | solution.py:311
  25.9 0.4 %collective-permute-done.2.other_ref = bf16[12,128,128]{2,1,0:T(8,128)(2,1)S(1)} collective-permute-done((bf16[12,128,128]{2,1,0:T(8,128)(2,1)S(1)}, bf16[12,128,128]{2,1,0:T(8,128)(2,1)S(1)}, u32[]{:S(2)}, u32[]{:S(2)}) %collective-permute-start.2) | collective-permute-done | bytes 393248 | tf_op jit(solution)/shard_map/ppermute | solution.py:557
  26.4 1.6 %far_other.1 = bf16[16,96,128]{2,1,0:T(8,128)(2,1)} custom-call(bf16[12,128,128]{2,1,0:T(8,128)(2,1)S(1)} %collective-permute-done.2.other_ref, f32[3,2,3,256,128]{4,3,2,1,0:T(8,128)S(1)} %get-tuple-element.17.first_ref, bf16[16,48,128]{2,1,0:T(8,128)(2,1)S(1)} %get-tuple-element.18.own_ref), custom_call_target="tpu_custom_call" | custom-call | flops 1000000000 | bytes 1048576 | tf_op jit(solution)/shard_map/far_other/pallas_call | solution.py:323
  28.0 4.0 %all-to-all-start.1 = ((bf16[16,96,128]{2,1,0:T(8,128)(2,1)}), bf16[16,96,128]{2,1,0:T(8,128)(2,1)S(1)}, u32[]{:S(2)}, u32[]{:S(2)}) async-start(bf16[16,96,128]{2,1,0:T(8,128)(2,1)} %far_other.1), calls=%async_computation.1 | async-start | bytes 786432 | tf_op jit(solution)/shard_map/all_to_all | solution.py:570
  32.0 0.0 collective-permute-start.3
  32.0 1.5 %collective-permute-done.3.refs_3_ = bf16[8,128,128]{2,1,0:T(8,128)(2,1)S(1)} collective-permute-done((bf16[8,128,128]{2,1,0:T(8,128)(2,1)S(1)}, bf16[8,128,128]{2,1,0:T(8,128)(2,1)S(1)}, u32[]{:S(2)}, u32[]{:S(2)}) %collective-permute-start.3) | collective-permute-done | bytes 262176 | tf_op jit(solution)/shard_map/ppermute | solution.py:557
  33.5 2.3 %near.1 = (bf16[8,32,128]{2,1,0:T(8,128)(2,1)S(1)}, bf16[8,32,128]{2,1,0:T(8,128)(2,1)S(1)}) custom-call(bf16[8,128,128]{2,1,0:T(8,128)(2,1)S(1)} %get-tuple-element.15.refs_0_, bf16[8,128,128]{2,1,0:T(8,128)(2,1)S(1)} %collective-permute-done.1.refs_1_, bf16[8,128,128]{2,1,0:T(8,128)(2,1)S(1)} %collective-permute-done.refs_2_, ...), custom_call_target="tpu_custom_call" | custom-call | flops 1000000000 | bytes 1048576 | tf_op jit(solution)/shard_map/near/pallas_call | solution.py:394
  35.8 2.1 %collective-permute-start.4 = (bf16[8,32,128]{2,1,0:T(8,128)(2,1)S(1)}, bf16[8,32,128]{2,1,0:T(8,128)(2,1)S(1)}, u32[]{:S(2)}, u32[]{:S(2)}) collective-permute-start(bf16[8,32,128]{2,1,0:T(8,128)(2,1)S(1)} %get-tuple-element.22), channel_id=1, source_target_pairs={{0,2},{2,0},{4,6},{6,4},{8,10},{10,8},{12,14},{14,12},{1,3},{3,1},... | collective-permute-start | bytes 196616 | tf_op jit(solution)/shard_map/ppermute | solution.py:563
  37.9 2.8 %collective-permute-done.4.taken_ref = bf16[8,32,128]{2,1,0:T(8,128)(2,1)S(1)} collective-permute-done((bf16[8,32,128]{2,1,0:T(8,128)(2,1)S(1)}, bf16[8,32,128]{2,1,0:T(8,128)(2,1)S(1)}, u32[]{:S(2)}, u32[]{:S(2)}) %collective-permute-start.4) | collective-permute-done | bytes 65568 | tf_op jit(solution)/shard_map/ppermute | solution.py:563
  40.7 1.1 %near_out.1._ = f32[2,2,16,4,8,128]{5,4,3,2,1,0:T(8,128)} custom-call(bf16[8,32,128]{2,1,0:T(8,128)(2,1)S(1)} %get-tuple-element.21.kept_ref, bf16[8,32,128]{2,1,0:T(8,128)(2,1)S(1)} %collective-permute-done.4.taken_ref), custom_call_target="tpu_custom_call" | custom-call | flops 1000000000 | bytes 1048576 | tf_op jit(solution)/shard_map/near_out/pallas_call | solution.py:448
  41.7 2.2 %all-to-all-done.1.far_ref = bf16[16,96,128]{2,1,0:T(8,128)(2,1)S(1)} async-done(((bf16[16,96,128]{2,1,0:T(8,128)(2,1)}), bf16[16,96,128]{2,1,0:T(8,128)(2,1)S(1)}, u32[]{:S(2)}, u32[]{:S(2)}) %all-to-all-start.1) | async-done | bytes 393248 | tf_op jit(solution)/shard_map/all_to_all | solution.py:570
  44.0 0.1 finish.1
  (2 shorter events, 0.1 us)
Async XLA Ops:
  2.8 21.8 %all-to-all-start = ((bf16[16,128,128]{2,1,0:T(8,128)(2,1)}), bf16[16,128,128]{2,1,0:T(8,128)(2,1)S(1)}, u32[]{:S(2)}, u32[]{:S(2)}) async-start(bf16[16,128,128]{2,1,0:T(8,128)(2,1)} %whiten.1.own_ref), calls=%async_computation | async-start | bytes 1048576 | tf_op jit(solution)/shard_map/all_to_all | solution.py:560
  10.1 1.1 %copy-start = (bf16[16,128,128]{2,1,0:T(8,128)(2,1)S(1)}, bf16[16,128,128]{2,1,0:T(8,128)(2,1)}, u32[]{:S(2)}) copy-start(bf16[16,128,128]{2,1,0:T(8,128)(2,1)} %whiten.1.own_ref) | copy-start | bytes 1572868
  11.2 12.7 %collective-permute-start = (bf16[8,128,128]{2,1,0:T(8,128)(2,1)S(1)}, bf16[8,128,128]{2,1,0:T(8,128)(2,1)S(1)}, u32[]{:S(2)}, u32[]{:S(2)}) collective-permute-start(bf16[8,128,128]{2,1,0:T(8,128)(2,1)S(1)} %get-tuple-element.14), channel_id=1, source_target_pairs={{0,2},{2,0},{4,6},{6,4},{8,10},{10,8},{12,14},{14,12},{1,3},{3,1},... | collective-permute-start | bytes 786440 | tf_op jit(solution)/shard_map/ppermute | solution.py:563
  13.3 10.7 %collective-permute-start.1 = (bf16[8,128,128]{2,1,0:T(8,128)(2,1)S(1)}, bf16[8,128,128]{2,1,0:T(8,128)(2,1)S(1)}, u32[]{:S(2)}, u32[]{:S(2)}) collective-permute-start(bf16[8,128,128]{2,1,0:T(8,128)(2,1)S(1)} %get-tuple-element.15.refs_0_), channel_id=1, source_target_pairs={{0,1},{1,0},{2,3},{3,2},{4,5},{5,4},{6,7},{7,6},{8,9},{9,8},{10,11... | collective-permute-start | bytes 786440 | tf_op jit(solution)/shard_map/ppermute | solution.py:557
  24.6 1.8 %collective-permute-start.2 = (bf16[12,128,128]{2,1,0:T(8,128)(2,1)S(1)}, bf16[12,128,128]{2,1,0:T(8,128)(2,1)S(1)}, u32[]{:S(2)}, u32[]{:S(2)}) collective-permute-start(bf16[12,128,128]{2,1,0:T(8,128)(2,1)S(1)} %slice.3), channel_id=1, source_target_pairs={{0,1},{1,0},{2,3},{3,2},{4,5},{5,4},{6,7},{7,6},{8,9},{9,8},{10,11... | collective-permute-start | bytes 1179656 | tf_op jit(solution)/shard_map/ppermute | solution.py:557
  28.0 16.0 %all-to-all-start.1 = ((bf16[16,96,128]{2,1,0:T(8,128)(2,1)}), bf16[16,96,128]{2,1,0:T(8,128)(2,1)S(1)}, u32[]{:S(2)}, u32[]{:S(2)}) async-start(bf16[16,96,128]{2,1,0:T(8,128)(2,1)} %far_other.1), calls=%async_computation.1 | async-start | bytes 786432 | tf_op jit(solution)/shard_map/all_to_all | solution.py:570
  32.0 1.5 %collective-permute-start.3 = (bf16[8,128,128]{2,1,0:T(8,128)(2,1)S(1)}, bf16[8,128,128]{2,1,0:T(8,128)(2,1)S(1)}, u32[]{:S(2)}, u32[]{:S(2)}) collective-permute-start(bf16[8,128,128]{2,1,0:T(8,128)(2,1)S(1)} %collective-permute-done.refs_2_), channel_id=1, source_target_pairs={{0,1},{1,0},{2,3},{3,2},{4,5},{5,4},{6,7},{7,6},{8,9},{9,8},{10,11... | collective-permute-start | bytes 786440 | tf_op jit(solution)/shard_map/ppermute | solution.py:557
  35.8 4.9 %collective-permute-start.4 = (bf16[8,32,128]{2,1,0:T(8,128)(2,1)S(1)}, bf16[8,32,128]{2,1,0:T(8,128)(2,1)S(1)}, u32[]{:S(2)}, u32[]{:S(2)}) collective-permute-start(bf16[8,32,128]{2,1,0:T(8,128)(2,1)S(1)} %get-tuple-element.22), channel_id=1, source_target_pairs={{0,2},{2,0},{4,6},{6,4},{8,10},{10,8},{12,14},{14,12},{1,3},{3,1},... | collective-permute-start | bytes 196616 | tf_op jit(solution)/shard_map/ppermute | solution.py:563

commit v8 on v7

--- a/solution.py
+++ b/solution.py
@@ -216,12 +216,15 @@
 
 
 def far_sums(first_ref, values_ref, second_ref, put, rows, chans, windows, done=None, skip=0):
+    tiles = []
     for t in range(TILES):
         firsts, last_firsts, level_firsts = (first_ref.at[block, t] for block in range(3))
         seconds = {}
         for r in range(2, rows):
             spread_second(second_ref.at[t, r], values_ref[(r - skip) * TILES + t], windows, chans)
             seconds[r] = tuple(second_ref.at[t, r, k] for k in range(chans))
+        tiles.append((firsts, last_firsts, level_firsts, seconds))
+    for t, (firsts, last_firsts, level_firsts, seconds) in enumerate(tiles):
         mid = range(4, rows - 2)
         work = [(level_firsts, seconds[r]) for r in (2, 3)]
         work += [(firsts, g) for r in mid for g in seconds[r]]
@@ -235,8 +238,9 @@
             for q in range(2):
                 vals = jnp.concatenate([sums[2 + n * chans + k][q] for k in range(chans)])
                 put(r, t, q * chans * SUB, vals)
-        if done is not None:
-            done(range(2, rows - 2), t)
+    if done is not None:
+        done(range(2, rows - 2))
+    for t, (firsts, last_firsts, level_firsts, seconds) in enumerate(tiles):
         last = range(rows - 2, rows)
         work = [(firsts, g) for r in last for g in seconds[r]]
         work += [(last_firsts, seconds[r]) for r in last]
@@ -247,8 +251,8 @@
                 put(r, t, q * chans * SUB, vals)
             rest = sums[len(last) * chans + n]
             put(r, t, 2 * chans * SUB, jnp.concatenate(rest))
-        if done is not None:
-            done(last, t)
+    if done is not None:
+        done(range(rows - 2, rows))
 
 
 def far_own_kernel(got_ref, first_ref, out_ref, second_ref, *, rows, chans, windows):
@@ -290,9 +294,9 @@
         at += size
         out_ref[r * TILES + t, at : at + 2 * SUB, :] = vals.astype(jnp.bfloat16)
 
-    def done(which, t):
+    def done(which):
         for r in which:
-            send(r * TILES + t, 1)
+            send(r * TILES, TILES)
 
     far_sums(first_ref, other_ref, second_ref, put, rows, chans, windows, done, skip=2)
     for copy in copies:
@@ -328,7 +332,7 @@
         scratch_shapes=scratch
         + [
             pltpu.VMEM((rows * TILES, 2 * size, LANES), jnp.bfloat16),
-            pltpu.SemaphoreType.DMA((1 + (rows - 2) * TILES,)),
+            pltpu.SemaphoreType.DMA((rows - 1,)),
         ],
         name="far_other",
         **params,

time: 44.4 us -> 44.4 us (level)
  transfers between devices with their start and end apart: 7 -> 7, of which waited for: 6 -> 6; matrix products, arithmetic and copies ran while one was open for 0% -> 0% of each run, Pallas kernels for 10% -> 11%
where the time goes in v8:
time: 44.4 us; the launch traced here: 44 us
  waiting for transfers between devices  18.3 us (41%)
  starting transfers between devices  15.6 us (35%)
  Pallas kernels  9.05 us (20%)
  local copies, waits for them, and re-layouts  1.1 us (2%)
    ppermute x2, waiting for transfers between devices, level_swap(): return lax.ppermute(value, 'row', [(r, r ^ 1) for r in range(rows)])  13.4 us
    all_to_all x1, starting transfers between devices, on_device_packed(): got = lax.all_to_all(own, 'row', 0, 0, tiled=True)  7.29 us
    ppermute x2, starting transfers between devices, level_swap(): return lax.ppermute(value, 'row', [(r, r ^ 1) for r in range(rows)])  4.17 us
    all_to_all x1, starting transfers between devices, on_device_packed(): far = lax.all_to_all(far, 'row', 0, 0, tiled=True)  4.01 us
    pallas_call x1, Pallas kernels, whiten_packed(): pl.pallas_call(functools.partial(whiten_kernel, chans=chans), out_shape=j...  2.75 us
    pallas_call x1, Pallas kernels, near_packed(): pl.pallas_call(functools.partial(near_kernel, windows=windows), out_shape...  2.26 us
    all_to_all x1, waiting for transfers between devices, on_device_packed(): far = lax.all_to_all(far, 'row', 0, 0, tiled=True)  2.22 us
    ppermute x3, waiting for transfers between devices, swap(): return lax.ppermute(value, 'col', [(0, 1), (1, 0)])  1.97 us
  transfers between devices with their start and end apart: 7, of which 6 were waited for; matrix products, arithmetic and copies ran while one was open for 0% of the time, Pallas kernels for 11%

profile of v8, /device:TPU:0, one launch (start us, length us, event | category | flops | bytes accessed | tf_op | source)
XLA Modules:
  0.0 44.0 jit_solution(10267150622842211040)
XLA Ops:
  0.0 2.8 %whiten.1.own_ref = bf16[16,128,128]{2,1,0:T(8,128)(2,1)} custom-call(s32[2,32]{1,0:T(2,128)} %bitcast.12, bf16[2,32,2,16,128]{4,3,2,1,0:T(8,128)(2,1)} %bitcast.11), custom_call_target="tpu_custom_call" | custom-call | flops 1000000000 | bytes 1048576 | tf_op jit(solution)/shard_map/whiten/pallas_call | solution.py:150
  2.8 7.3 %all-to-all-start = ((bf16[16,128,128]{2,1,0:T(8,128)(2,1)}), bf16[16,128,128]{2,1,0:T(8,128)(2,1)S(1)}, u32[]{:S(2)}, u32[]{:S(2)}) async-start(bf16[16,128,128]{2,1,0:T(8,128)(2,1)} %whiten.1.own_ref), calls=%async_computation | async-start | bytes 1048576 | tf_op jit(solution)/shard_map/all_to_all | solution.py:564
  10.1 0.0 copy-start
  10.1 1.1 %copy-done = bf16[16,128,128]{2,1,0:T(8,128)(2,1)S(1)} copy-done((bf16[16,128,128]{2,1,0:T(8,128)(2,1)S(1)}, bf16[16,128,128]{2,1,0:T(8,128)(2,1)}, u32[]{:S(2)}) %copy-start) | copy-done | bytes 524312
  11.2 2.1 %collective-permute-start = (bf16[8,128,128]{2,1,0:T(8,128)(2,1)S(1)}, bf16[8,128,128]{2,1,0:T(8,128)(2,1)S(1)}, u32[]{:S(2)}, u32[]{:S(2)}) collective-permute-start(bf16[8,128,128]{2,1,0:T(8,128)(2,1)S(1)} %get-tuple-element.14), channel_id=1, source_target_pairs={{0,2},{2,0},{4,6},{6,4},{8,10},{10,8},{12,14},{14,12},{1,3},{3,1},... | collective-permute-start | bytes 786440 | tf_op jit(solution)/shard_map/ppermute | solution.py:567
  13.3 0.0 collective-permute-start.1
  13.3 10.7 %collective-permute-done.refs_2_ = bf16[8,128,128]{2,1,0:T(8,128)(2,1)S(1)} collective-permute-done((bf16[8,128,128]{2,1,0:T(8,128)(2,1)S(1)}, bf16[8,128,128]{2,1,0:T(8,128)(2,1)S(1)}, u32[]{:S(2)}, u32[]{:S(2)}) %collective-permute-start) | collective-permute-done | bytes 262176 | tf_op jit(solution)/shard_map/ppermute | solution.py:567
  23.9 0.0 collective-permute-done.1.refs_1_
  23.9 0.6 %all-to-all-done.got_ref = bf16[16,128,128]{2,1,0:T(8,128)(2,1)S(1)} async-done(((bf16[16,128,128]{2,1,0:T(8,128)(2,1)}), bf16[16,128,128]{2,1,0:T(8,128)(2,1)S(1)}, u32[]{:S(2)}, u32[]{:S(2)}) %all-to-all-start) | async-done | bytes 524320 | tf_op jit(solution)/shard_map/all_to_all | solution.py:564
  24.6 0.1 collective-permute-start.2
  24.6 1.3 %far_own.1 = (f32[3,2,3,256,128]{4,3,2,1,0:T(8,128)S(1)}, bf16[16,48,128]{2,1,0:T(8,128)(2,1)S(1)}) custom-call(bf16[16,128,128]{2,1,0:T(8,128)(2,1)S(1)} %all-to-all-done.got_ref), custom_call_target="tpu_custom_call" | custom-call | flops 1000000000 | bytes 1048576 | tf_op jit(solution)/shard_map/far_own/pallas_call | solution.py:315
  25.9 0.4 %collective-permute-done.2.other_ref = bf16[12,128,128]{2,1,0:T(8,128)(2,1)S(1)} collective-permute-done((bf16[12,128,128]{2,1,0:T(8,128)(2,1)S(1)}, bf16[12,128,128]{2,1,0:T(8,128)(2,1)S(1)}, u32[]{:S(2)}, u32[]{:S(2)}) %collective-permute-start.2) | collective-permute-done | bytes 393248 | tf_op jit(solution)/shard_map/ppermute | solution.py:561
  26.4 1.6 %far_other.1 = bf16[16,96,128]{2,1,0:T(8,128)(2,1)} custom-call(bf16[12,128,128]{2,1,0:T(8,128)(2,1)S(1)} %collective-permute-done.2.other_ref, f32[3,2,3,256,128]{4,3,2,1,0:T(8,128)S(1)} %get-tuple-element.17.first_ref, bf16[16,48,128]{2,1,0:T(8,128)(2,1)S(1)} %get-tuple-element.18.own_ref), custom_call_target="tpu_custom_call" | custom-call | flops 1000000000 | bytes 1048576 | tf_op jit(solution)/shard_map/far_other/pallas_call | solution.py:327
  27.9 4.0 %all-to-all-start.1 = ((bf16[16,96,128]{2,1,0:T(8,128)(2,1)}), bf16[16,96,128]{2,1,0:T(8,128)(2,1)S(1)}, u32[]{:S(2)}, u32[]{:S(2)}) async-start(bf16[16,96,128]{2,1,0:T(8,128)(2,1)} %far_other.1), calls=%async_computation.1 | async-start | bytes 786432 | tf_op jit(solution)/shard_map/all_to_all | solution.py:574
  31.9 0.0 collective-permute-start.3
  32.0 1.5 %collective-permute-done.3.refs_3_ = bf16[8,128,128]{2,1,0:T(8,128)(2,1)S(1)} collective-permute-done((bf16[8,128,128]{2,1,0:T(8,128)(2,1)S(1)}, bf16[8,128,128]{2,1,0:T(8,128)(2,1)S(1)}, u32[]{:S(2)}, u32[]{:S(2)}) %collective-permute-start.3) | collective-permute-done | bytes 262176 | tf_op jit(solution)/shard_map/ppermute | solution.py:561
  33.5 2.3 %near.1 = (bf16[8,32,128]{2,1,0:T(8,128)(2,1)S(1)}, bf16[8,32,128]{2,1,0:T(8,128)(2,1)S(1)}) custom-call(bf16[8,128,128]{2,1,0:T(8,128)(2,1)S(1)} %get-tuple-element.15.refs_0_, bf16[8,128,128]{2,1,0:T(8,128)(2,1)S(1)} %collective-permute-done.1.refs_1_, bf16[8,128,128]{2,1,0:T(8,128)(2,1)S(1)} %collective-permute-done.refs_2_, ...), custom_call_target="tpu_custom_call" | custom-call | flops 1000000000 | bytes 1048576 | tf_op jit(solution)/shard_map/near/pallas_call | solution.py:398
  35.7 2.1 %collective-permute-start.4 = (bf16[8,32,128]{2,1,0:T(8,128)(2,1)S(1)}, bf16[8,32,128]{2,1,0:T(8,128)(2,1)S(1)}, u32[]{:S(2)}, u32[]{:S(2)}) collective-permute-start(bf16[8,32,128]{2,1,0:T(8,128)(2,1)S(1)} %get-tuple-element.22), channel_id=1, source_target_pairs={{0,2},{2,0},{4,6},{6,4},{8,10},{10,8},{12,14},{14,12},{1,3},{3,1},... | collective-permute-start | bytes 196616 | tf_op jit(solution)/shard_map/ppermute | solution.py:567
  37.8 2.8 %collective-permute-done.4.taken_ref = bf16[8,32,128]{2,1,0:T(8,128)(2,1)S(1)} collective-permute-done((bf16[8,32,128]{2,1,0:T(8,128)(2,1)S(1)}, bf16[8,32,128]{2,1,0:T(8,128)(2,1)S(1)}, u32[]{:S(2)}, u32[]{:S(2)}) %collective-permute-start.4) | collective-permute-done | bytes 65568 | tf_op jit(solution)/shard_map/ppermute | solution.py:567
  40.6 1.1 %near_out.1._ = f32[2,2,16,4,8,128]{5,4,3,2,1,0:T(8,128)} custom-call(bf16[8,32,128]{2,1,0:T(8,128)(2,1)S(1)} %get-tuple-element.21.kept_ref, bf16[8,32,128]{2,1,0:T(8,128)(2,1)S(1)} %collective-permute-done.4.taken_ref), custom_call_target="tpu_custom_call" | custom-call | flops 1000000000 | bytes 1048576 | tf_op jit(solution)/shard_map/near_out/pallas_call | solution.py:452
  41.7 2.2 %all-to-all-done.1.far_ref = bf16[16,96,128]{2,1,0:T(8,128)(2,1)S(1)} async-done(((bf16[16,96,128]{2,1,0:T(8,128)(2,1)}), bf16[16,96,128]{2,1,0:T(8,128)(2,1)S(1)}, u32[]{:S(2)}, u32[]{:S(2)}) %all-to-all-start.1) | async-done | bytes 393248 | tf_op jit(solution)/shard_map/all_to_all | solution.py:574
  43.9 0.1 finish.1
  (2 shorter events, 0.1 us)
Async XLA Ops:
  2.8 21.8 %all-to-all-start = ((bf16[16,128,128]{2,1,0:T(8,128)(2,1)}), bf16[16,128,128]{2,1,0:T(8,128)(2,1)S(1)}, u32[]{:S(2)}, u32[]{:S(2)}) async-start(bf16[16,128,128]{2,1,0:T(8,128)(2,1)} %whiten.1.own_ref), calls=%async_computation | async-start | bytes 1048576 | tf_op jit(solution)/shard_map/all_to_all | solution.py:564
  10.1 1.1 %copy-start = (bf16[16,128,128]{2,1,0:T(8,128)(2,1)S(1)}, bf16[16,128,128]{2,1,0:T(8,128)(2,1)}, u32[]{:S(2)}) copy-start(bf16[16,128,128]{2,1,0:T(8,128)(2,1)} %whiten.1.own_ref) | copy-start | bytes 1572868
  11.2 12.7 %collective-permute-start = (bf16[8,128,128]{2,1,0:T(8,128)(2,1)S(1)}, bf16[8,128,128]{2,1,0:T(8,128)(2,1)S(1)}, u32[]{:S(2)}, u32[]{:S(2)}) collective-permute-start(bf16[8,128,128]{2,1,0:T(8,128)(2,1)S(1)} %get-tuple-element.14), channel_id=1, source_target_pairs={{0,2},{2,0},{4,6},{6,4},{8,10},{10,8},{12,14},{14,12},{1,3},{3,1},... | collective-permute-start | bytes 786440 | tf_op jit(solution)/shard_map/ppermute | solution.py:567
  13.3 10.7 %collective-permute-start.1 = (bf16[8,128,128]{2,1,0:T(8,128)(2,1)S(1)}, bf16[8,128,128]{2,1,0:T(8,128)(2,1)S(1)}, u32[]{:S(2)}, u32[]{:S(2)}) collective-permute-start(bf16[8,128,128]{2,1,0:T(8,128)(2,1)S(1)} %get-tuple-element.15.refs_0_), channel_id=1, source_target_pairs={{0,1},{1,0},{2,3},{3,2},{4,5},{5,4},{6,7},{7,6},{8,9},{9,8},{10,11... | collective-permute-start | bytes 786440 | tf_op jit(solution)/shard_map/ppermute | solution.py:561
  24.6 1.8 %collective-permute-start.2 = (bf16[12,128,128]{2,1,0:T(8,128)(2,1)S(1)}, bf16[12,128,128]{2,1,0:T(8,128)(2,1)S(1)}, u32[]{:S(2)}, u32[]{:S(2)}) collective-permute-start(bf16[12,128,128]{2,1,0:T(8,128)(2,1)S(1)} %slice.3), channel_id=1, source_target_pairs={{0,1},{1,0},{2,3},{3,2},{4,5},{5,4},{6,7},{7,6},{8,9},{9,8},{10,11... | collective-permute-start | bytes 1179656 | tf_op jit(solution)/shard_map/ppermute | solution.py:561
  27.9 16.0 %all-to-all-start.1 = ((bf16[16,96,128]{2,1,0:T(8,128)(2,1)}), bf16[16,96,128]{2,1,0:T(8,128)(2,1)S(1)}, u32[]{:S(2)}, u32[]{:S(2)}) async-start(bf16[16,96,128]{2,1,0:T(8,128)(2,1)} %far_other.1), calls=%async_computation.1 | async-start | bytes 786432 | tf_op jit(solution)/shard_map/all_to_all | solution.py:574
  31.9 1.5 %collective-permute-start.3 = (bf16[8,128,128]{2,1,0:T(8,128)(2,1)S(1)}, bf16[8,128,128]{2,1,0:T(8,128)(2,1)S(1)}, u32[]{:S(2)}, u32[]{:S(2)}) collective-permute-start(bf16[8,128,128]{2,1,0:T(8,128)(2,1)S(1)} %collective-permute-done.refs_2_), channel_id=1, source_target_pairs={{0,1},{1,0},{2,3},{3,2},{4,5},{5,4},{6,7},{7,6},{8,9},{9,8},{10,11... | collective-permute-start | bytes 786440 | tf_op jit(solution)/shard_map/ppermute | solution.py:561
  35.7 4.9 %collective-permute-start.4 = (bf16[8,32,128]{2,1,0:T(8,128)(2,1)S(1)}, bf16[8,32,128]{2,1,0:T(8,128)(2,1)S(1)}, u32[]{:S(2)}, u32[]{:S(2)}) collective-permute-start(bf16[8,32,128]{2,1,0:T(8,128)(2,1)S(1)} %get-tuple-element.22), channel_id=1, source_target_pairs={{0,2},{2,0},{4,6},{6,4},{8,10},{10,8},{12,14},{14,12},{1,3},{3,1},... | collective-permute-start | bytes 196616 | tf_op jit(solution)/shard_map/ppermute | solution.py:567
